TPU v7x, 128 devices: a whole 4x4x4 slice. The times are simulated.
128 devices in a mesh: section: 2 (over core), shard: 8 (over z_lo, x), replica: 8 (over y, z_hi).
Axes of the slice: x: 4, y: 4, z: 4 (z_hi: 2, z_lo: 2; z = z_hi * 2 + z_lo), core: 2. Of those that a mesh axis runs over, the one named last changes fastest.
Arguments:
- inputs: bfloat16 [2, 8, 1024, 1088], P(None, 'replica', 'shard'), may hold values from -6 to 6
- cotangent: bfloat16 [2, 8, 1024, 1088], P(None, 'replica', 'shard'), may hold values from -6 to 6
- w_qkv: bfloat16 [2, 1088, 3264], P('section', 'shard'), may hold values from -0.1875 to 0.1875
- qv_bias: bfloat16 [2, 2176], P('section', 'shard'), may hold values from -3 to 3
- w_out: bfloat16 [2, 1088, 1088], P('section', 'shard'), may hold values from -2 to 2
- out_bias: bfloat16 [2, 1088], P('section', 'shard'), may hold values from -3 to 3
- gain_one: bfloat16 [2, 1088], P('section', 'shard'), may hold values from 0.5 to 1.5
- bias_one: bfloat16 [2, 1088], P('section', 'shard'), may hold values from -3 to 3
- gain_two: bfloat16 [2, 1088], P('section', 'shard'), may hold values from 0.5 to 1.5
- bias_two: bfloat16 [2, 1088], P('section', 'shard'), may hold values from -3 to 3
- w_up: bfloat16 [2, 1088, 4352], P('section', 'shard'), may hold values from -0.1875 to 0.1875
- up_bias: bfloat16 [2, 4352], P('section', 'shard'), may hold values from -3 to 3
- w_down: bfloat16 [2, 4352, 1088], P('section', 'shard'), may hold values from -0.09375 to 0.09375
- down_bias: bfloat16 [2, 1088], P('section', 'shard'), may hold values from -3 to 3
Outputs:
- section_out: float32 [2, 2, 8, 1024, 1088], P('section', None, 'replica', 'shard')
- input_grad: float32 [2, 2, 8, 1024, 1088], P('section', None, 'replica', 'shard')
- grad_w_qkv: float32 [2, 1088, 3264], P('section', 'shard')
- grad_qv_bias: float32 [2, 2176], P('section', 'shard')
- grad_w_out: float32 [2, 1088, 1088], P('section', 'shard')
- grad_out_bias: float32 [2, 1088], P('section', 'shard')
- grad_gain_one: float32 [2, 1088], P('section', 'shard')
- grad_bias_one: float32 [2, 1088], P('section', 'shard')
- grad_gain_two: float32 [2, 1088], P('section', 'shard')
- grad_bias_two: float32 [2, 1088], P('section', 'shard')
- grad_w_up: float32 [2, 1088, 4352], P('section', 'shard')
- grad_up_bias: float32 [2, 4352], P('section', 'shard')
- grad_w_down: float32 [2, 4352, 1088], P('section', 'shard')
- grad_down_bias: float32 [2, 1088], P('section', 'shard')
All inputs are finite; a program needn't handle non-finite values.
Results may differ from a plain program's by a relative error of at most 0.02.
Values may be sent and summed in bfloat16 or wider, within the bound.
A program may use at most 256 MiB of HBM per device.

v0:
```python
import jax
import jax.numpy as jnp
from jax import lax
from jax.sharding import PartitionSpec as P

HEADS = 17
HEAD_DIM = 64


EPSILON = 1e-05
GELU_C = 0.7978845608028654
NEG_FILL = -1e30


def from_behind(block, axis, distance):
    devices = range(lax.axis_size(axis))
    route = [(i - distance, i) for i in devices if i - distance in devices]
    return lax.ppermute(block, axis, route)


def matmul(left_side, right_side):
    return jnp.dot(left_side, right_side, preferred_element_type=jnp.float32)


def times_transposed(left_side, right_side):
    return lax.dot_general(
        left_side, right_side, (((1,), (1,)), ((), ())), preferred_element_type=jnp.float32
    )


def transposed_times(left_side, right_side):
    return lax.dot_general(
        left_side, right_side, (((0,), (0,)), ((), ())), preferred_element_type=jnp.float32
    )


def norm_forward(hidden, gain_vec, offset):
    center = hidden - jnp.mean(hidden, axis=-1, keepdims=True)
    inverse = lax.rsqrt(jnp.mean(center * center, axis=-1, keepdims=True) + EPSILON)
    unit_rows = center * inverse
    return (unit_rows * gain_vec + offset, unit_rows, inverse)


def norm_backward(grad_rows, unit_rows, inverse, gain_vec):
    grad_unit = grad_rows * gain_vec
    grad_in = inverse * (
        grad_unit
        - jnp.mean(grad_unit, axis=-1, keepdims=True)
        - unit_rows * jnp.mean(grad_unit * unit_rows, axis=-1, keepdims=True)
    )
    return (grad_in, jnp.sum(grad_rows * unit_rows, axis=0), jnp.sum(grad_rows, axis=0))


def gelu_pair(values):
    tangent = jnp.tanh(GELU_C * (values + 0.044715 * values * values * values))
    output_rows = 0.5 * values * (1.0 + tangent)
    slope = 0.5 * (1.0 + tangent) + 0.5 * values * (1.0 - tangent * tangent) * GELU_C * (
        1.0 + 3.0 * 0.044715 * values * values
    )
    return (output_rows, slope)


def when_active(active, function, operand):

    def skipped(operand_again):
        return jax.tree.map(jnp.zeros_like, function(operand_again))

    return lax.cond(active, function, skipped, operand)


def pick(is_first, early, late):
    return jax.tree.map(
        lambda early_item, late_item: jnp.where(is_first, early_item, late_item), early, late
    )


def head_view(row_array, seq_count):
    return row_array.reshape(seq_count, -1, HEADS, HEAD_DIM)


def split_projection(projected, seq_count):
    model_width = projected.shape[1] // 3
    shaped_rows = projected.reshape(seq_count, -1, 3 * model_width)
    return (
        shaped_rows[:, :, :model_width],
        shaped_rows[:, :, model_width : 2 * model_width],
        shaped_rows[:, :, 2 * model_width :],
    )


def attention_scores(query_heads, key_heads, query_pos, key_pos):
    raw_scores = jnp.einsum(
        "sqhe,skhe->shqk", query_heads, key_heads, preferred_element_type=jnp.float32
    ) * HEAD_DIM ** (-0.5)
    allowed = key_pos <= query_pos
    return (jnp.where(allowed, raw_scores, NEG_FILL), allowed)


def front_part(hidden, weights):
    model_width = hidden.shape[1]
    normed, unit_one, inverse_one = norm_forward(hidden, weights[4], weights[5])
    normed_low = normed.astype(jnp.bfloat16)
    bias_full = jnp.concatenate(
        [
            weights[1][:model_width],
            jnp.zeros((model_width,), jnp.bfloat16),
            weights[1][model_width:],
        ]
    )
    projected = (matmul(normed_low, weights[0]) + bias_full).astype(jnp.bfloat16)
    return (normed_low, unit_one, inverse_one, projected)


def rear_part(operand, weights, query_pos, key_pos):
    hidden, queries, key_rows, value_rows = operand
    seq_count = queries.shape[0]
    masked, allowed = attention_scores(
        head_view(queries, seq_count), head_view(key_rows, seq_count), query_pos, key_pos
    )
    row_max = jnp.max(masked, axis=-1, keepdims=True)
    shifted = jnp.exp(masked - row_max)
    row_total = jnp.sum(shifted, axis=-1, keepdims=True)
    soft_low = (shifted / row_total).astype(jnp.bfloat16)
    log_total = row_max + jnp.log(row_total)
    mixed_heads = jnp.einsum(
        "shqk,skhe->sqhe",
        soft_low,
        head_view(value_rows, seq_count),
        preferred_element_type=jnp.float32,
    )
    attended_low = mixed_heads.reshape(hidden.shape).astype(jnp.bfloat16)
    middle = hidden + matmul(attended_low, weights[2]) + weights[3]
    second, unit_two, inverse_two = norm_forward(middle, weights[6], weights[7])
    second_low = second.astype(jnp.bfloat16)
    upper_pre = matmul(second_low, weights[8]) + weights[9]
    activated, slope_unused = gelu_pair(upper_pre)
    activated_low = activated.astype(jnp.bfloat16)
    output_rows = middle + matmul(activated_low, weights[10]) + weights[11]
    return (
        output_rows,
        log_total,
        attended_low,
        unit_two,
        inverse_two,
        second_low,
        upper_pre,
        activated_low,
    )


def back_rear(operand, weights):
    grad_out, upper_pre, unit_two, inverse_two = operand
    grad_low = grad_out.astype(jnp.bfloat16)
    grad_act = times_transposed(grad_low, weights[10])
    activated_unused, slope = gelu_pair(upper_pre)
    up_low = (grad_act * slope).astype(jnp.bfloat16)
    grad_second = times_transposed(up_low, weights[8])
    grad_norm_in, gain_two_grad, bias_two_grad = norm_backward(
        grad_second, unit_two, inverse_two, weights[6]
    )
    grad_middle = grad_out + grad_norm_in
    middle_low = grad_middle.astype(jnp.bfloat16)
    attended_grad = times_transposed(middle_low, weights[2]).astype(jnp.bfloat16)
    return (grad_low, up_low, grad_middle, middle_low, attended_grad, gain_two_grad, bias_two_grad)


def back_attention(operand, query_pos, key_pos):
    queries, key_rows, value_rows, log_total, attended_grad = operand
    seq_count = queries.shape[0]
    query_heads = head_view(queries, seq_count)
    key_heads = head_view(key_rows, seq_count)
    value_heads = head_view(value_rows, seq_count)
    masked, allowed = attention_scores(query_heads, key_heads, query_pos, key_pos)
    soft_rows = jnp.where(allowed, jnp.exp(masked - log_total), 0.0)
    grad_heads = head_view(attended_grad, seq_count)
    grad_soft = jnp.einsum(
        "sqhe,skhe->shqk", grad_heads, value_heads, preferred_element_type=jnp.float32
    )
    inner_sum = jnp.sum(soft_rows * grad_soft, axis=-1, keepdims=True)
    grad_scores = (soft_rows * (grad_soft - inner_sum)).astype(jnp.bfloat16)
    scale_factor = HEAD_DIM ** (-0.5)
    grad_queries = (
        jnp.einsum("shqk,skhe->sqhe", grad_scores, key_heads, preferred_element_type=jnp.float32)
        * scale_factor
    )
    grad_keys = (
        jnp.einsum("shqk,sqhe->skhe", grad_scores, query_heads, preferred_element_type=jnp.float32)
        * scale_factor
    )
    grad_values = jnp.einsum(
        "shqk,sqhe->skhe",
        soft_rows.astype(jnp.bfloat16),
        grad_heads,
        preferred_element_type=jnp.float32,
    )
    return (
        grad_queries.reshape(queries.shape),
        grad_keys.reshape(key_rows.shape),
        grad_values.reshape(value_rows.shape),
        inner_sum,
    )


def back_front(operand, weights):
    grad_queries, grad_keys, grad_values, unit_one, inverse_one, grad_middle = operand
    merged = (
        jnp.concatenate([grad_queries, grad_keys, grad_values], axis=-1)
        .astype(jnp.bfloat16)
        .reshape(grad_middle.shape[0], -1)
    )
    grad_normed = times_transposed(merged, weights[0])
    grad_norm_in, gain_one_grad, bias_one_grad = norm_backward(
        grad_normed, unit_one, inverse_one, weights[4]
    )
    return (merged, grad_middle + grad_norm_in, gain_one_grad, bias_one_grad)


def joined(collection, slot_index):
    return jnp.concatenate([member[slot_index] for member in collection], axis=0)


def local(
    inputs,
    cotangent,
    w_qkv,
    qv_bias,
    w_out,
    out_bias,
    gain_one,
    bias_one,
    gain_two,
    bias_two,
    w_up,
    up_bias,
    w_down,
    down_bias,
):
    micro_count, seq_count, part_len, model_width = inputs.shape
    row_count = seq_count * part_len
    is_first = lax.axis_index("section") == 0
    shard_start = lax.axis_index("shard") * part_len
    query_pos = shard_start + lax.broadcasted_iota(jnp.int32, (1, 1, part_len, 1), 2)
    full_len = part_len * lax.axis_size("shard")
    key_pos_all = lax.broadcasted_iota(jnp.int32, (1, 1, 1, full_len), 3)
    weights = (
        lax.all_gather(w_qkv[0], "shard", axis=0, tiled=True),
        lax.all_gather(qv_bias[0], "shard", axis=0, tiled=True),
        lax.all_gather(w_out[0], "shard", axis=0, tiled=True),
        lax.all_gather(out_bias[0], "shard", axis=0, tiled=True),
        lax.all_gather(gain_one[0], "shard", axis=0, tiled=True),
        lax.all_gather(bias_one[0], "shard", axis=0, tiled=True),
        lax.all_gather(gain_two[0], "shard", axis=0, tiled=True),
        lax.all_gather(bias_two[0], "shard", axis=0, tiled=True),
        lax.all_gather(w_up[0], "shard", axis=0, tiled=True),
        lax.all_gather(up_bias[0], "shard", axis=0, tiled=True),
        lax.all_gather(w_down[0], "shard", axis=0, tiled=True),
        lax.all_gather(down_bias[0], "shard", axis=0, tiled=True),
    )
    incoming = jnp.zeros((seq_count, part_len, model_width), jnp.bfloat16)
    forward_saved = []
    for tick_index in range(micro_count + 1):
        active = jnp.where(is_first, tick_index < micro_count, tick_index >= 1)
        own_rows = inputs[min(tick_index, micro_count - 1)].astype(jnp.float32)
        hidden = jnp.where(is_first, own_rows, incoming.astype(jnp.float32)).reshape(
            row_count, model_width
        )
        normed_low, unit_one, inverse_one, projected = when_active(
            active, lambda operand: front_part(operand, weights), hidden
        )
        queries, keys_own, values_own = split_projection(projected, seq_count)
        key_rows, value_rows = (
            lax.all_gather(keys_own, "shard", axis=1, tiled=True),
            lax.all_gather(values_own, "shard", axis=1, tiled=True),
        )
        rear_out = when_active(
            active,
            lambda operand: rear_part(operand, weights, query_pos, key_pos_all),
            (hidden, queries, key_rows, value_rows),
        )
        if tick_index < micro_count:
            incoming = from_behind(
                rear_out[0].astype(jnp.bfloat16).reshape(seq_count, part_len, model_width),
                "section",
                1,
            )
        forward_saved.append(
            (normed_low, unit_one, inverse_one, projected, key_rows, value_rows) + rear_out
        )
    back_weights = (
        lax.all_gather(w_qkv[0], "shard", axis=0, tiled=True),
        lax.all_gather(qv_bias[0], "shard", axis=0, tiled=True),
        lax.all_gather(w_out[0], "shard", axis=0, tiled=True),
        lax.all_gather(out_bias[0], "shard", axis=0, tiled=True),
        lax.all_gather(gain_one[0], "shard", axis=0, tiled=True),
        lax.all_gather(bias_one[0], "shard", axis=0, tiled=True),
        lax.all_gather(gain_two[0], "shard", axis=0, tiled=True),
        lax.all_gather(bias_two[0], "shard", axis=0, tiled=True),
        lax.all_gather(w_up[0], "shard", axis=0, tiled=True),
        lax.all_gather(up_bias[0], "shard", axis=0, tiled=True),
        lax.all_gather(w_down[0], "shard", axis=0, tiled=True),
        lax.all_gather(down_bias[0], "shard", axis=0, tiled=True),
    )
    incoming_grad = jnp.zeros((seq_count, part_len, model_width), jnp.bfloat16)
    backward_saved = []
    for tick_index in range(micro_count + 1):
        active = jnp.where(is_first, tick_index >= 1, tick_index < micro_count)
        tick_state = pick(
            is_first,
            forward_saved[max(tick_index - 1, 0)],
            forward_saved[min(tick_index + 1, micro_count)],
        )
        own_grad = cotangent[min(tick_index, micro_count - 1)].astype(jnp.float32)
        grad_out = jnp.where(is_first, incoming_grad.astype(jnp.float32), own_grad).reshape(
            row_count, model_width
        )
        rear_grads = when_active(
            active,
            lambda operand: back_rear(operand, back_weights),
            (grad_out, tick_state[12], tick_state[9], tick_state[10]),
        )
        queries, keys_own, values_own = split_projection(tick_state[3], seq_count)
        key_rows, value_rows = (
            lax.all_gather(keys_own, "shard", axis=1, tiled=True),
            lax.all_gather(values_own, "shard", axis=1, tiled=True),
        )
        grad_queries, grad_keys, grad_values, inner_sum = when_active(
            active,
            lambda operand: back_attention(operand, query_pos, key_pos_all),
            (queries, key_rows, value_rows, tick_state[7], rear_grads[4]),
        )
        grad_keys_own, grad_values_own = (
            lax.psum_scatter(
                grad_keys.astype(jnp.bfloat16), "shard", scatter_dimension=1, tiled=True
            ).astype(jnp.float32),
            lax.psum_scatter(
                grad_values.astype(jnp.bfloat16), "shard", scatter_dimension=1, tiled=True
            ).astype(jnp.float32),
        )
        merged, grad_input, gain_one_grad, bias_one_grad = when_active(
            active,
            lambda operand: back_front(operand, back_weights),
            (
                grad_queries,
                grad_keys_own,
                grad_values_own,
                tick_state[1],
                tick_state[2],
                rear_grads[2],
            ),
        )
        if tick_index < micro_count:
            incoming_grad = from_behind(
                grad_input.astype(jnp.bfloat16).reshape(seq_count, part_len, model_width),
                "section",
                -1,
            )
        backward_saved.append(rear_grads + (merged, grad_input, gain_one_grad, bias_one_grad))
    forward_rows = [
        pick(is_first, forward_saved[batch_index], forward_saved[batch_index + 1])
        for batch_index in range(micro_count)
    ]
    backward_rows = [
        pick(is_first, backward_saved[batch_index + 1], backward_saved[batch_index])
        for batch_index in range(micro_count)
    ]
    merged_all = joined(backward_rows, 7)
    merged_sums = jnp.sum(merged_all, axis=0, dtype=jnp.float32)
    grad_qv = jnp.concatenate([merged_sums[:model_width], merged_sums[2 * model_width :]])
    grad_qkv_w = transposed_times(joined(forward_rows, 0), merged_all)
    middle_all = joined(backward_rows, 3)
    grad_out_w = transposed_times(joined(forward_rows, 8), middle_all)
    grad_out_b = jnp.sum(middle_all, axis=0, dtype=jnp.float32)
    up_all = joined(backward_rows, 1)
    grad_up_w = transposed_times(joined(forward_rows, 11), up_all)
    grad_up_b = jnp.sum(up_all, axis=0, dtype=jnp.float32)
    low_all = joined(backward_rows, 0)
    grad_down_w = transposed_times(joined(forward_rows, 13), low_all)
    grad_down_b = jnp.sum(low_all, axis=0, dtype=jnp.float32)
    gain_one_total = sum((member[9] for member in backward_rows))
    bias_one_total = sum((member[10] for member in backward_rows))
    gain_two_total = sum((member[5] for member in backward_rows))
    bias_two_total = sum((member[6] for member in backward_rows))
    (
        shard_qkv,
        shard_qv,
        shard_out_w,
        shard_out_b,
        shard_gain_one,
        shard_bias_one,
        shard_gain_two,
        shard_bias_two,
        shard_up_w,
        shard_up_b,
        shard_down_w,
        shard_down_b,
    ) = (
        lax.psum_scatter(
            grad_qkv_w.astype(jnp.bfloat16), "shard", scatter_dimension=0, tiled=True
        ).astype(jnp.float32),
        lax.psum_scatter(
            grad_qv.astype(jnp.bfloat16), "shard", scatter_dimension=0, tiled=True
        ).astype(jnp.float32),
        lax.psum_scatter(
            grad_out_w.astype(jnp.bfloat16), "shard", scatter_dimension=0, tiled=True
        ).astype(jnp.float32),
        lax.psum_scatter(
            grad_out_b.astype(jnp.bfloat16), "shard", scatter_dimension=0, tiled=True
        ).astype(jnp.float32),
        lax.psum_scatter(
            gain_one_total.astype(jnp.bfloat16), "shard", scatter_dimension=0, tiled=True
        ).astype(jnp.float32),
        lax.psum_scatter(
            bias_one_total.astype(jnp.bfloat16), "shard", scatter_dimension=0, tiled=True
        ).astype(jnp.float32),
        lax.psum_scatter(
            gain_two_total.astype(jnp.bfloat16), "shard", scatter_dimension=0, tiled=True
        ).astype(jnp.float32),
        lax.psum_scatter(
            bias_two_total.astype(jnp.bfloat16), "shard", scatter_dimension=0, tiled=True
        ).astype(jnp.float32),
        lax.psum_scatter(
            grad_up_w.astype(jnp.bfloat16), "shard", scatter_dimension=0, tiled=True
        ).astype(jnp.float32),
        lax.psum_scatter(
            grad_up_b.astype(jnp.bfloat16), "shard", scatter_dimension=0, tiled=True
        ).astype(jnp.float32),
        lax.psum_scatter(
            grad_down_w.astype(jnp.bfloat16), "shard", scatter_dimension=0, tiled=True
        ).astype(jnp.float32),
        lax.psum_scatter(
            grad_down_b.astype(jnp.bfloat16), "shard", scatter_dimension=0, tiled=True
        ).astype(jnp.float32),
    )
    summed_grads = (
        lax.psum(shard_qkv.astype(jnp.bfloat16), "replica").astype(jnp.float32),
        lax.psum(shard_qv.astype(jnp.bfloat16), "replica").astype(jnp.float32),
        lax.psum(shard_out_w.astype(jnp.bfloat16), "replica").astype(jnp.float32),
        lax.psum(shard_out_b.astype(jnp.bfloat16), "replica").astype(jnp.float32),
        lax.psum(shard_gain_one.astype(jnp.bfloat16), "replica").astype(jnp.float32),
        lax.psum(shard_bias_one.astype(jnp.bfloat16), "replica").astype(jnp.float32),
        lax.psum(shard_gain_two.astype(jnp.bfloat16), "replica").astype(jnp.float32),
        lax.psum(shard_bias_two.astype(jnp.bfloat16), "replica").astype(jnp.float32),
        lax.psum(shard_up_w.astype(jnp.bfloat16), "replica").astype(jnp.float32),
        lax.psum(shard_up_b.astype(jnp.bfloat16), "replica").astype(jnp.float32),
        lax.psum(shard_down_w.astype(jnp.bfloat16), "replica").astype(jnp.float32),
        lax.psum(shard_down_b.astype(jnp.bfloat16), "replica").astype(jnp.float32),
    )
    section_out = jnp.stack(
        [member[6].reshape(seq_count, part_len, model_width) for member in forward_rows]
    )[None]
    input_grad = jnp.stack(
        [member[8].reshape(seq_count, part_len, model_width) for member in backward_rows]
    )[None]
    return (section_out, input_grad) + tuple((summed_grad[None] for summed_grad in summed_grads))


def solution(mesh):
    return jax.shard_map(
        local,
        mesh=mesh,
        in_specs=(
            P(None, "replica", "shard", None),
            P(None, "replica", "shard", None),
            P("section", "shard", None),
            P("section", "shard"),
            P("section", "shard", None),
            P("section", "shard"),
            P("section", "shard"),
            P("section", "shard"),
            P("section", "shard"),
            P("section", "shard"),
            P("section", "shard", None),
            P("section", "shard"),
            P("section", "shard", None),
            P("section", "shard"),
        ),
        out_specs=(
            P("section", None, "replica", "shard", None),
            P("section", None, "replica", "shard", None),
            P("section", "shard", None),
            P("section", "shard"),
            P("section", "shard", None),
            P("section", "shard"),
            P("section", "shard"),
            P("section", "shard"),
            P("section", "shard"),
            P("section", "shard"),
            P("section", "shard", None),
            P("section", "shard"),
            P("section", "shard", None),
            P("section", "shard"),
        ),
        check_vma=False,
    )
```

profile of v0, /device:TPU:16, one launch (start us, length us, event | category | flops | bytes accessed | tf_op | source)
XLA Modules:
  0.0 1870.9 jit_solution(8483489916552934349)
XLA Ops:
  19.4 36.7 %all-reduce.20 = (bf16[1088]{0:T(1024)(128)(2,1)S(1)}, bf16[1088]{0:T(1024)(128)(2,1)}, bf16[2176]{0:T(1024)(128)(2,1)}, bf16[1088]{0:T(1024)(128)(2,1)S(1)}, bf...) all-reduce(bf16[1088]{0:T(1024)(128)(2,1)S(1)} %dynamic-update-slic, ...), channel_id=2, replica_groups=mesh['section'=2,'shard'=8,'replica'=8] {'shard'}, use_global_device_ids=true, to_apply=%add | all-reduce | flops 13056 | bytes 52224 | tf_op jit(solution)/shard_map/all_gather | solution.py:250
  57.1 37.3 %all-gather.53.cloned.1.call-done = bf16[1,1088,3264]{2,1,0:T(8,128)(2,1)} async-done(((bf16[1,136,3264]{2,1,0:T(8,128)(2,1)}), bf16[1,1088,3264]{2,1,0:T(8,128)(2,1)}) %all-gather.53.cloned.1.call-update) | async-done | bytes 7102480 | tf_op jit(solution)/shard_map/all_gather | solution.py:246
  94.4 8.7 conditional.10
  105.9 30.7 %all-gather.55.cloned.1.call-done = bf16[1,1088,1088]{2,1,0:T(8,128)(2,1)} async-done(((bf16[1,136,1088]{2,1,0:T(8,128)(2,1)}), bf16[1,1088,1088]{2,1,0:T(8,128)(2,1)}) %all-gather.55.cloned.1.call-update) | async-done | bytes 2367504 | tf_op jit(solution)/shard_map/all_gather | solution.py:248
  136.6 47.4 %all-gather.29.cloned.1.call-done = bf16[1,1024,1088]{1,2,0:T(8,128)(2,1)} async-done(((bf16[1,128,1088]{1,2,0:T(8,128)(2,1)}), bf16[1,1024,1088]{1,2,0:T(8,128)(2,1)}) %all-gather.29.cloned.1.call-update) | async-done | bytes 2228240 | tf_op jit(solution)/shard_map/all_gather | solution.py:272
  184.0 49.6 %all-gather.31.cloned.1.call-done = bf16[1,1024,1088]{1,2,0:T(8,128)(2,1)} async-done(((bf16[1,128,1088]{1,2,0:T(8,128)(2,1)}), bf16[1,1024,1088]{1,2,0:T(8,128)(2,1)}) %all-gather.31.cloned.1.call-update) | async-done | bytes 2228240 | tf_op jit(solution)/shard_map/all_gather | solution.py:273
  233.6 105.7 %all-gather.57.cloned.1.call-done = bf16[1,1088,4352]{2,1,0:T(8,128)(2,1)} async-done(((bf16[1,136,4352]{2,1,0:T(8,128)(2,1)}), bf16[1,1088,4352]{2,1,0:T(8,128)(2,1)}) %all-gather.57.cloned.1.call-update) | async-done | bytes 9469968 | tf_op jit(solution)/shard_map/all_gather | solution.py:254
  339.3 107.6 %all-gather.59.cloned.1.call-done = bf16[1,4352,1088]{2,1,0:T(8,128)(2,1)} async-done(((bf16[1,544,1088]{2,1,0:T(8,128)(2,1)}), bf16[1,4352,1088]{2,1,0:T(8,128)(2,1)}) %all-gather.59.cloned.1.call-update) | async-done | bytes 9469968 | tf_op jit(solution)/shard_map/all_gather | solution.py:256
  446.9 27.1 %conditional.11 = (f32[128,1088]{0,1:T(8,128)}, f32[1,17,128,1]{2,1,3,0:T(8,128)S(1)}, bf16[128,1088]{0,1:T(8,128)(2,1)}, f32[128,1088]{0,1:T(8,128)}, f32[128,1...) conditional(s32[]{:T(128)} %convert_element_type.508, () %tuple.103, ...), branch_computations={%region_4.5_spmd, %region_5.10_spmd} | conditional | flops 3332168192 | bytes 136038336 | solution.py:68
  493.0 41.4 %all-gather.35.cloned.1.call-done = bf16[1,1024,1088]{1,2,0:T(8,128)(2,1)} async-done(((bf16[1,128,1088]{1,2,0:T(8,128)(2,1)}), bf16[1,1024,1088]{1,2,0:T(8,128)(2,1)}) %all-gather.35.cloned.1.call-update) | async-done | bytes 2228240 | tf_op jit(solution)/shard_map/all_gather | solution.py:272
  543.4 40.7 %all-gather.33.cloned.1.call-done = bf16[1,1024,1088]{1,2,0:T(8,128)(2,1)} async-done(((bf16[1,128,1088]{1,2,0:T(8,128)(2,1)}), bf16[1,1024,1088]{1,2,0:T(8,128)(2,1)}) %all-gather.33.cloned.1.call-update) | async-done | bytes 2228240 | tf_op jit(solution)/shard_map/all_gather | solution.py:273
  584.1 6.9 fusion.90
  631.2 46.0 %all-gather.41.cloned.1.call-done = bf16[1,1024,1088]{1,2,0:T(8,128)(2,1)} async-done(((bf16[1,128,1088]{1,2,0:T(8,128)(2,1)}), bf16[1,1024,1088]{1,2,0:T(8,128)(2,1)}) %all-gather.41.cloned.1.call-update) | async-done | bytes 2228240 | tf_op jit(solution)/shard_map/all_gather | solution.py:323
  677.1 49.6 %all-gather.43.cloned.1.call-done = bf16[1,1024,1088]{1,2,0:T(8,128)(2,1)} async-done(((bf16[1,128,1088]{1,2,0:T(8,128)(2,1)}), bf16[1,1024,1088]{1,2,0:T(8,128)(2,1)}) %all-gather.43.cloned.1.call-update) | async-done | bytes 2228240 | tf_op jit(solution)/shard_map/all_gather | solution.py:324
  731.0 11.3 copy.100
  746.5 11.3 copy.102
  762.5 13.4 all-gather.37.cloned.1.call-done
  776.0 48.9 %all-gather.39.cloned.1.call-done = bf16[1,1024,1088]{1,2,0:T(8,128)(2,1)} async-done(((bf16[1,128,1088]{1,2,0:T(8,128)(2,1)}), bf16[1,1024,1088]{1,2,0:T(8,128)(2,1)}) %all-gather.39.cloned.1.call-update) | async-done | bytes 2228240 | tf_op jit(solution)/shard_map/all_gather | solution.py:273
  824.9 10.7 conditional.13
  835.6 38.3 %all-gather.45.cloned.1.call-done = bf16[1,1024,1088]{1,2,0:T(8,128)(2,1)} async-done(((bf16[1,128,1088]{1,2,0:T(8,128)(2,1)}), bf16[1,1024,1088]{1,2,0:T(8,128)(2,1)}) %all-gather.45.cloned.1.call-update) | async-done | bytes 2228240 | tf_op jit(solution)/shard_map/all_gather | solution.py:323
  873.9 6.6 fusion.162
  880.5 42.1 %reduce-scatter.32.cloned.1.call-done = bf16[128,1088]{1,0:T(8,128)(2,1)} async-done(((bf16[1024,1088]{1,0:T(8,128)(2,1)}), bf16[128,1088]{1,0:T(8,128)(2,1)}) %reduce-scatter.32.cloned.1.call-update) | async-done | bytes 278544
  926.7 41.6 %reduce-scatter.34.cloned.1.call-done = bf16[128,1088]{1,0:T(8,128)(2,1)} async-done(((bf16[1024,1088]{1,0:T(8,128)(2,1)}), bf16[128,1088]{1,0:T(8,128)(2,1)}) %reduce-scatter.34.cloned.1.call-update) | async-done | bytes 278544
  977.7 10.9 collective-permute-done.2
  988.7 7.7 fusion.60
  1003.9 7.7 fusion.83
  1011.6 11.3 copy.106
  1027.5 8.2 multiply_reduce_fusion.18
  1042.6 11.3 copy.104
  1075.3 41.8 %reduce-scatter.36.cloned.1.call-done = bf16[128,1088]{1,0:T(8,128)(2,1)} async-done(((bf16[1024,1088]{1,0:T(8,128)(2,1)}), bf16[128,1088]{1,0:T(8,128)(2,1)}) %reduce-scatter.36.cloned.1.call-update) | async-done | bytes 278544
  1132.4 18.1 conditional.17
  1133.4 9.3 fusion.46
  1150.6 12.7 all-gather.49.cloned.1.call-done
  1163.3 49.0 %all-gather.51.cloned.1.call-done = bf16[1,1024,1088]{1,2,0:T(8,128)(2,1)} async-done(((bf16[1,128,1088]{1,2,0:T(8,128)(2,1)}), bf16[1,1024,1088]{1,2,0:T(8,128)(2,1)}) %all-gather.51.cloned.1.call-update) | async-done | bytes 2228240 | tf_op jit(solution)/shard_map/all_gather | solution.py:324
  1212.3 19.1 %conditional.18 = (bf16[1,128,1088]{1,2,0:T(8,128)(2,1)S(1)}, bf16[1,1024,1088]{1,2,0:T(8,128)(2,1)}, bf16[1,1024,1088]{1,2,0:T(8,128)(2,1)}) conditional(s32[]{:T(128)} %convert_element_type.508, () %tuple.118, (s32[1,1,1,1024]{3,2,1,0:T(1,128)S(1)}, s32[1,1,128,1]{2,3,1,0:T(1,128)S(1)}, bf16[1,128,3264]{1,2,0:T(8,128)(2,1)}, ...), branch_computations={%region_56.57_spmd, %region_57.59_spmd} | conditional | flops 1468809216 | bytes 100590224 | solution.py:68
  1231.4 11.3 copy.108
  1246.9 11.3 copy.110
  1269.0 23.7 %reduce-scatter.40.cloned.1.call-done = bf16[128,1088]{1,0:T(8,128)(2,1)} async-done(((bf16[1024,1088]{1,0:T(8,128)(2,1)}), bf16[128,1088]{1,0:T(8,128)(2,1)}) %reduce-scatter.40.cloned.1.call-update) | async-done | bytes 278544
  1295.1 42.5 %reduce-scatter.42.cloned.1.call-done = bf16[128,1088]{1,0:T(8,128)(2,1)} async-done(((bf16[1024,1088]{1,0:T(8,128)(2,1)}), bf16[128,1088]{1,0:T(8,128)(2,1)}) %reduce-scatter.42.cloned.1.call-update) | async-done | bytes 278544
  1340.1 10.8 conditional.19
  1361.1 6.2 convolution_convert_fusion.3
  1376.0 8.8 reduce-scatter.44.cloned.1.call-done
  1384.8 83.6 %reduce-scatter.26.cloned.1.call-done = bf16[136,3264]{1,0:T(8,128)(2,1)} async-done(((bf16[1088,3264]{1,0:T(8,128)(2,1)}), bf16[136,3264]{1,0:T(8,128)(2,1)}) %reduce-scatter.26.cloned.1.call-update) | async-done | bytes 887824 | tf_op jit(solution)/shard_map/reduce_scatter | solution.py:397
  1468.4 104.4 %reduce-scatter.28.cloned.1.call-done = bf16[136,4352]{1,0:T(8,128)(2,1)} async-done(((bf16[1088,4352]{1,0:T(8,128)(2,1)}), bf16[136,4352]{1,0:T(8,128)(2,1)}) %reduce-scatter.28.cloned.1.call-update) | async-done | bytes 1183760 | tf_op jit(solution)/shard_map/reduce_scatter | solution.py:421
  1572.8 109.3 %reduce-scatter.30.cloned.1.call-done = bf16[544,1088]{1,0:T(8,128)(2,1)} async-done(((bf16[4352,1088]{1,0:T(8,128)(2,1)}), bf16[544,1088]{1,0:T(8,128)(2,1)}) %reduce-scatter.30.cloned.1.call-update) | async-done | bytes 1183760 | tf_op jit(solution)/shard_map/reduce_scatter | solution.py:427
  1686.6 32.4 %all-reduce.19 = (bf16[2176]{0:T(1024)(128)(2,1)S(1)}, bf16[1088]{0:T(1024)(128)(2,1)S(1)}, bf16[1088]{0:T(1024)(128)(2,1)S(1)}, bf16[1088]{0:T(1024)(128)(2,1)S...) all-reduce(bf16[2176]{0:T(1024)(128)(2,1)S(1)} %pad_maximum_fusion., ...), channel_id=21, replica_groups=mesh['section'=2,'shard'=8,'replica'=8] {'shard'}, use_global_device_ids=true, to_apply=%region_70.71.clone | all-reduce | flops 13056 | bytes 52224
  1719.8 40.2 %all-reduce.17 = (bf16[1,272]{1,0:T(2,128)(2,1)S(1)}, bf16[1,136]{1,0:T(2,128)(2,1)S(1)}, bf16[1,136]{1,0:T(2,128)(2,1)S(1)}, bf16[1,136]{1,0:T(2,128)(2,1)S(1)}...) all-reduce(bf16[1,272]{1,0:T(2,128)(2,1)S(1)} %broadcast_in_dim.214, ...), channel_id=1, replica_groups=mesh['section'=2,'shard'=8,'replica'=8] {'replica'}, use_global_device_ids=true, to_apply=%region_71.72 | all-reduce | flops 1632 | bytes 6528 | tf_op jit(solution)/shard_map/psum | solution.py:436
  1765.7 91.2 %all-reduce.23.cloned.1.call-done = (bf16[1,136,3264]{2,1,0:T(8,128)(2,1)}, bf16[1,136,1088]{2,1,0:T(8,128)(2,1)}, bf16[1,136,4352]{2,1,0:T(8,128)(2,1)}, bf16[1,544,1088]{2,1,0:T(8,128)(2,1)}) async-done(((bf16[1,136,3264]{2,1,0:T(8,128)(2,1)}, bf16[1,136,1088]{2,1,0:T(8,128)(2,1)}, bf16[1,136,4352]{2,1,0:T(8,128)(2,1)}, bf16[1,544,1088]{2,1,0:T(8,128)(2,1)}), (bf16[1,136,3264]{2,1,0:T(8,128)(2,1)}, ...) | async-done | bytes 3551248 | tf_op jit(solution)/shard_map/psum | solution.py:435
  (605 shorter events, 309.9 us)
Async XLA Ops:
  7.2 87.2 %all-gather.53.cloned.1.call-start = ((), (), s32[]{:S(2)}) async-start(), calls=%async_computation.25 | async-start | bytes 8146944 | tf_op jit(solution)/shard_map/all_gather | solution.py:246
  7.9 128.7 %all-gather.55.cloned.1.call-start = ((), (), s32[]{:S(2)}) async-start(), calls=%async_computation.26 | async-start | bytes 2820096 | tf_op jit(solution)/shard_map/all_gather | solution.py:248
  8.7 175.3 %all-gather.29.cloned.1.call-start = ((), (), s32[]{:S(2)}) async-start(), calls=%async_computation.10 | async-start | bytes 2506752 | tf_op jit(solution)/shard_map/all_gather | solution.py:272
  56.1 434.9 %copy-start.83 = (bf16[1088]{0:T(1024)(128)(2,1)}, bf16[1088]{0:T(1024)(128)(2,1)S(1)}, u32[]{:S(2)}) copy-start(bf16[1088]{0:T(1024)(128)(2,1)S(1)} %get-tuple-element.810) | copy-start | bytes 6532
  56.1 768.8 %copy-start.74 = (bf16[1088]{0:T(1024)(128)(2,1)}, bf16[1088]{0:T(1024)(128)(2,1)S(1)}, u32[]{:S(2)}) copy-start(bf16[1088]{0:T(1024)(128)(2,1)S(1)} %get-tuple-element.811) | copy-start | bytes 6532
  103.1 343.8 %copy-start.14 = (bf16[128,3264]{0,1:T(8,128)(2,1)}, bf16[128,3264]{0,1:T(8,128)(2,1)S(1)}, u32[]{:S(2)}) copy-start(bf16[128,3264]{0,1:T(8,128)(2,1)S(1)} %get-tuple-element.511) | copy-start | bytes 2506756
  103.1 343.8 %copy-start.16 = (f32[128,1088]{1,0:T(8,128)}, f32[128,1088]{1,0:T(8,128)S(1)}, u32[]{:S(2)}) copy-start(f32[128,1088]{1,0:T(8,128)S(1)} %get-tuple-element.524) | copy-start | bytes 1671172
  103.1 343.8 %copy-start.53 = (bf16[128,1088]{0,1:T(8,128)(2,1)}, bf16[128,1088]{0,1:T(8,128)(2,1)S(1)}, u32[]{:S(2)}) copy-start(bf16[128,1088]{0,1:T(8,128)(2,1)S(1)} %get-tuple-element.756) | copy-start | bytes 835588
  103.1 343.8 %copy-start.122 = (f32[128,1]{0,1:T(1,128)}, f32[128,1]{0,1:T(1,128)S(1)}, u32[]{:S(2)}) copy-start(f32[128,1]{0,1:T(1,128)S(1)} %get-tuple-element.523) | copy-start | bytes 1540
  104.1 129.5 %all-gather.31.cloned.1.call-start = ((), (), s32[]{:S(2)}) async-start(), calls=%async_computation.11 | async-start | bytes 2506752 | tf_op jit(solution)/shard_map/all_gather | solution.py:273
  104.7 234.6 %all-gather.57.cloned.1.call-start = ((), (), s32[]{:S(2)}) async-start(), calls=%async_computation.27 | async-start | bytes 10653696 | tf_op jit(solution)/shard_map/all_gather | solution.py:254
  105.3 341.6 %all-gather.59.cloned.1.call-start = ((), (), s32[]{:S(2)}) async-start(), calls=%async_computation.28 | async-start | bytes 11280384 | tf_op jit(solution)/shard_map/all_gather | solution.py:256
  105.8 428.5 %all-gather.35.cloned.1.call-start = ((), (), s32[]{:S(2)}) async-start(), calls=%async_computation.13 | async-start | bytes 2506752 | tf_op jit(solution)/shard_map/all_gather | solution.py:272
  105.9 341.0 %copy-start.110 = (s32[1,1,128,1]{2,3,1,0:T(1,128)}, s32[1,1,128,1]{2,3,1,0:T(1,128)S(1)}, u32[]{:S(2)}) copy-start(s32[1,1,128,1]{2,3,1,0:T(1,128)S(1)} %iota_add_fusion.1) | copy-start | bytes 1540
  475.2 2.9 collective-permute-start
  490.1 94.0 %all-gather.33.cloned.1.call-start = ((), (), s32[]{:S(2)}) async-start(), calls=%async_computation.12 | async-start | bytes 2506752 | tf_op jit(solution)/shard_map/all_gather | solution.py:273
  490.8 186.3 %all-gather.41.cloned.1.call-start = ((), (), s32[]{:S(2)}) async-start(), calls=%async_computation.16 | async-start | bytes 2506752 | tf_op jit(solution)/shard_map/all_gather | solution.py:323
  492.3 100.2 %copy-start.63 = (f32[1088]{0:T(1024)}, f32[1088]{0:T(1024)S(1)}, u32[]{:S(2)}) copy-start(f32[1088]{0:T(1024)S(1)} %convert_element_type.525) | copy-start | bytes 13060
  605.0 2.5 collective-permute-start.1
  616.8 109.9 %all-gather.43.cloned.1.call-start = ((), (), s32[]{:S(2)}) async-start(), calls=%async_computation.17 | async-start | bytes 2506752 | tf_op jit(solution)/shard_map/all_gather | solution.py:324
  617.4 158.6 %all-gather.37.cloned.1.call-start = ((), (), s32[]{:S(2)}) async-start(), calls=%async_computation.14 | async-start | bytes 2506752 | tf_op jit(solution)/shard_map/all_gather | solution.py:272
  619.3 205.6 %all-gather.39.cloned.1.call-start = ((), (), s32[]{:S(2)}) async-start(), calls=%async_computation.15 | async-start | bytes 2506752 | tf_op jit(solution)/shard_map/all_gather | solution.py:273
  619.9 254.1 %all-gather.45.cloned.1.call-start = ((), (), s32[]{:S(2)}) async-start(), calls=%async_computation.18 | async-start | bytes 2506752 | tf_op jit(solution)/shard_map/all_gather | solution.py:323
  622.1 300.6 %reduce-scatter.32.cloned.1.call-start = ((), (), s32[]{:S(2)}) async-start(), calls=%async_computation.29 | async-start | bytes 2654208
  627.6 99.1 %copy-start.70 = (f32[1,17,128,1]{2,1,3,0:T(8,128)S(1)}, f32[1,17,128,1]{2,1,3,0:T(8,128)}, u32[]{:S(2)}) copy-start(f32[1,17,128,1]{2,1,3,0:T(8,128)} %copy-done.69) | copy-start | bytes 26116
  627.6 99.1 %copy-start.111 = (s32[1,1,128,1]{2,3,1,0:T(1,128)S(1)}, s32[1,1,128,1]{2,3,1,0:T(1,128)}, u32[]{:S(2)}) copy-start(s32[1,1,128,1]{2,3,1,0:T(1,128)} %copy-done.110) | copy-start | bytes 1540
  631.1 95.6 %copy-start.96 = (f32[1088]{0:T(1024)}, f32[1088]{0:T(1024)S(1)}, u32[]{:S(2)}) copy-start(f32[1088]{0:T(1024)S(1)} %get-tuple-element.551) | copy-start | bytes 13060
  631.2 95.6 %copy-start.98 = (f32[1088]{0:T(1024)}, f32[1088]{0:T(1024)S(1)}, u32[]{:S(2)}) copy-start(f32[1088]{0:T(1024)S(1)} %get-tuple-element.553) | copy-start | bytes 13060
  631.2 95.6 %copy-start.67 = (f32[1,17,128,1]{2,1,3,0:T(8,128)}, f32[1,17,128,1]{2,1,3,0:T(8,128)S(1)}, u32[]{:S(2)}) copy-start(f32[1,17,128,1]{2,1,3,0:T(8,128)S(1)} %add_bitcast_fusion.2) | copy-start | bytes 26116
  746.4 221.8 %reduce-scatter.34.cloned.1.call-start = ((), (), s32[]{:S(2)}) async-start(), calls=%async_computation.30 | async-start | bytes 2654208
  761.9 265.5 %all-gather.47.cloned.1.call-start = ((), (), s32[]{:S(2)}) async-start(), calls=%async_computation.19 | async-start | bytes 2506752 | tf_op jit(solution)/shard_map/all_gather | solution.py:324
  762.5 309.0 %reduce-scatter.38.cloned.1.call-start = ((), (), s32[]{:S(2)}) async-start(), calls=%async_computation.32 | async-start | bytes 2654208
  880.5 91.8 %copy-start.17 = (f32[128,1088]{1,0:T(8,128)S(1)}, f32[128,1088]{1,0:T(8,128)}, u32[]{:S(2)}) copy-start(f32[128,1088]{1,0:T(8,128)} %copy-done.16) | copy-start | bytes 1671172
  880.5 91.8 %copy-start.113 = (f32[128,1]{0,1:T(1,128)S(1)}, f32[128,1]{0,1:T(1,128)}, u32[]{:S(2)}) copy-start(f32[128,1]{0,1:T(1,128)} %get-tuple-element.931) | copy-start | bytes 1540
  880.5 91.8 %copy-start.123 = (f32[128,1]{0,1:T(1,128)S(1)}, f32[128,1]{0,1:T(1,128)}, u32[]{:S(2)}) copy-start(f32[128,1]{0,1:T(1,128)} %copy-done.122) | copy-start | bytes 1540
  975.4 13.3 collective-permute-start.2
  1027.0 90.1 %reduce-scatter.36.cloned.1.call-start = ((), (), s32[]{:S(2)}) async-start(), calls=%async_computation.31 | async-start | bytes 2654208
  1058.1 105.2 %all-gather.49.cloned.1.call-start = ((), (), s32[]{:S(2)}) async-start(), calls=%async_computation.20 | async-start | bytes 2506752 | tf_op jit(solution)/shard_map/all_gather | solution.py:323
  1060.0 152.2 %all-gather.51.cloned.1.call-start = ((), (), s32[]{:S(2)}) async-start(), calls=%async_computation.21 | async-start | bytes 2506752 | tf_op jit(solution)/shard_map/all_gather | solution.py:324
  1062.2 230.5 %reduce-scatter.40.cloned.1.call-start = ((), (), s32[]{:S(2)}) async-start(), calls=%async_computation.33 | async-start | bytes 2654208
  1128.8 3.5 collective-permute-start.3
  1246.8 90.8 %reduce-scatter.42.cloned.1.call-start = ((), (), s32[]{:S(2)}) async-start(), calls=%async_computation.34 | async-start | bytes 2654208
  1262.4 122.4 %reduce-scatter.44.cloned.1.call-start = ((), (), s32[]{:S(2)}) async-start(), calls=%async_computation.35 | async-start | bytes 2820096
  1268.0 200.4 %reduce-scatter.26.cloned.1.call-start = ((), (), s32[]{:S(2)}) async-start(), calls=%async_computation.22 | async-start | bytes 8146944 | tf_op jit(solution)/shard_map/reduce_scatter | solution.py:397
  1357.8 214.9 %reduce-scatter.28.cloned.1.call-start = ((), (), s32[]{:S(2)}) async-start(), calls=%async_computation.23 | async-start | bytes 10653696 | tf_op jit(solution)/shard_map/reduce_scatter | solution.py:421
  1367.4 314.7 %reduce-scatter.30.cloned.1.call-start = ((), (), s32[]{:S(2)}) async-start(), calls=%async_computation.24 | async-start | bytes 11280384 | tf_op jit(solution)/shard_map/reduce_scatter | solution.py:427
  1375.9 308.1 %copy-start.24 = (f32[128,1088]{0,1:T(8,128)S(1)}, f32[128,1088]{0,1:T(8,128)}, u32[]{:S(2)}) copy-start(f32[128,1088]{0,1:T(8,128)} %copy-done.23) | copy-start | bytes 1671172
  1375.9 481.0 %all-reduce.23.cloned.1.call-start = ((), (), s32[]{:S(2)}) async-start(), calls=%async_computation.36 | async-start | bytes 7311360 | tf_op jit(solution)/shard_map/psum | solution.py:435
  (123 other events, 1611.1 us)
Sparse Core Ops, SparseCore 0:
  9.7 84.7 all-gather.52
  96.1 40.5 all-gather.54
  138.8 45.1 all-gather.28
  186.0 47.5 all-gather.30
  235.1 104.1 all-gather.56
  340.8 106.0 all-gather.58
  490.2 44.1 all-gather.34
  536.5 47.5 all-gather.32
  616.9 60.2 all-gather.40
  679.1 47.5 all-gather.42
  728.3 47.6 all-gather.36
  777.4 47.4 all-gather.38
  826.4 47.4 all-gather.44
  876.8 45.8 reduce-scatter.31
  925.5 42.7 reduce-scatter.33
  969.7 44.5 all-gather.46
  1027.1 44.3 reduce-scatter.37
  1074.3 42.7 reduce-scatter.35
  1118.7 44.5 all-gather.48
  1164.7 47.5 all-gather.50
  1247.0 45.6 reduce-scatter.39
  1295.1 42.4 reduce-scatter.41
  1340.6 44.1 reduce-scatter.43
  1387.2 81.1 reduce-scatter.25
  1470.8 101.9 reduce-scatter.27
  1575.0 106.9 reduce-scatter.29
  1684.7 172.2 all-reduce.22
where the time goes:
time: 1880 us; the launch traced here: 1870 us
  waiting for transfers between devices  1330 us (71%)
  local copies, waits for them, and re-layouts  169 us (9%)
  matrix products  158 us (8%)
  blocking collectives  109 us (6%)
  other arithmetic  70.2 us (4%)
  between operations  20.4 us (1%)
    all_gather x6, waiting for transfers between devices, local(): lax.all_gather(values_own, 'shard', axis=1, tiled=True)  238 us
    unnamed x34, waiting for transfers between devices  210 us
    all_gather x6, waiting for transfers between devices, local(): lax.all_gather(keys_own, 'shard', axis=1, tiled=True)  199 us
    unnamed x293, local copies, waits for them, and re-layouts  130 us
    reduce_scatter x1, waiting for transfers between devices, local(): lax.psum_scatter(grad_down_w.astype(jnp.bfloat16), 'shard', scatter_dimen...  109 us
    all_gather x1, waiting for transfers between devices, local(): lax.all_gather(w_down[0], 'shard', axis=0, tiled=True)  108 us
    all_gather x1, waiting for transfers between devices, local(): lax.all_gather(w_up[0], 'shard', axis=0, tiled=True)  106 us
    reduce_scatter x1, waiting for transfers between devices, local(): lax.psum_scatter(grad_up_w.astype(jnp.bfloat16), 'shard', scatter_dimensi...  104 us
  transfers between devices with their start and end apart: 31, of which 29 were waited for; matrix products, arithmetic and copies ran while one was open for 15% of the time, Pallas kernels for 0%

commit v1 on v0

v1 whole, which is shorter than its diff:
```python
import functools

import jax
import jax.numpy as jnp
from jax import lax
from jax.experimental import pallas as pl
from jax.experimental.pallas import tpu as pltpu
from jax.sharding import PartitionSpec as P

D = 1088
FF = 4352
HEAD_DIM = 64
EPSILON = 1e-05
GELU_C = 0.7978845608028654
NEG_FILL = -1e30
BF = jnp.bfloat16
F32 = jnp.float32
MESH = pl.DeviceIdType.MESH
VMEM = pl.BlockSpec(memory_space=pltpu.VMEM)
LIMIT = 56 * 1024 * 1024


def place():
    c = lax.axis_index("section")
    j = lax.axis_index("shard")
    return c, j // 4, j % 4


def at(c, z, x):
    return {"section": c, "shard": z * 4 + x}


def greet(devices):
    barrier = pltpu.get_barrier_semaphore()
    for device in devices:
        pl.semaphore_signal(barrier, inc=1, device_id=device, device_id_type=MESH)
    pl.semaphore_wait(barrier, len(devices))


def sender(send_sems, recv_sems):
    def make(src, dst, index, device):
        copy = pltpu.make_async_remote_copy(
            src_ref=src,
            dst_ref=dst,
            send_sem=send_sems.at[index],
            recv_sem=recv_sems.at[index],
            device_id=device,
            device_id_type=MESH,
        )
        copy.start()
        return copy

    return make


def gather_kernel(half, own, out, send_sems, recv_sems, local_sem):
    c, z, x = place()
    ahead, behind, far = (x + 1) % 4, (x + 3) % 4, (x + 2) % 4
    partner, up, down = at(1 - c, z, x), at(c, z, ahead), at(c, z, behind)
    rows = own.shape[0]
    first, second = pl.ds(0, half), pl.ds(half, rows - half)
    me = c * 4 + x
    local = pltpu.make_async_copy(own, out.at[me], local_sem)
    local.start()
    greet((partner, up, down))
    send = sender(send_sems, recv_sems)
    to_up = send(own, out.at[me], 0, up)
    to_down = send(own, out.at[me], 1, down)
    to_partner = send(own, out.at[me], 2, partner)
    from_down, from_up, from_far = c * 4 + behind, c * 4 + ahead, c * 4 + far
    to_up.wait_recv()
    pass_up = send(out.at[from_down, first], out.at[from_down, first], 3, up)
    share_down = send(out.at[from_down], out.at[from_down], 4, partner)
    to_down.wait_recv()
    pass_down = send(out.at[from_up, second], out.at[from_up, second], 5, down)
    share_up = send(out.at[from_up], out.at[from_up], 6, partner)
    pass_up.wait_recv()
    share_first = send(out.at[from_far, first], out.at[from_far, first], 7, partner)
    pass_down.wait_recv()
    share_second = send(out.at[from_far, second], out.at[from_far, second], 8, partner)
    for copy in (to_partner, share_down, share_up, share_first, share_second):
        copy.wait_recv()
    for copy in (
        to_up,
        to_down,
        to_partner,
        pass_up,
        share_down,
        pass_down,
        share_up,
        share_first,
        share_second,
    ):
        copy.wait_send()
    local.wait()


def team_gather(own):
    rows, columns = own.shape
    return pl.pallas_call(
        functools.partial(gather_kernel, rows // 2),
        out_shape=jax.ShapeDtypeStruct((8, rows, columns), BF),
        in_specs=[VMEM],
        out_specs=VMEM,
        scratch_shapes=[
            pltpu.SemaphoreType.DMA((9,)),
            pltpu.SemaphoreType.DMA((9,)),
            pltpu.SemaphoreType.DMA,
        ],
        compiler_params=pltpu.CompilerParams(
            collective_id=0, has_side_effects=True, vmem_limit_bytes=LIMIT
        ),
    )(own)


def scatter_kernel(
    half,
    parts,
    out,
    from_partner,
    far_sum,
    up_sum,
    down_sum,
    far_first,
    far_second,
    got_down,
    got_up,
    send_sems,
    recv_sems,
):
    c, z, x = place()
    ahead, behind, far = (x + 1) % 4, (x + 3) % 4, (x + 2) % 4
    partner, up, down = at(1 - c, z, x), at(c, z, ahead), at(c, z, behind)
    rows = parts.shape[1]
    first, second = pl.ds(0, half), pl.ds(half, rows - half)
    greet((partner, up, down))
    send = sender(send_sems, recv_sems)
    other = (1 - c) * 4
    mine = c * 4
    swap_far = send(parts.at[other + far], from_partner.at[far], 0, partner)
    swap_up = send(parts.at[other + ahead], from_partner.at[ahead], 1, partner)
    swap_down = send(parts.at[other + behind], from_partner.at[behind], 2, partner)
    swap_own = send(parts.at[other + x], from_partner.at[x], 3, partner)

    def both(place_x, part):
        return parts[mine + place_x, part, :].astype(F32) + from_partner[
            place_x, part, :
        ].astype(F32)

    swap_far.wait_recv()
    far_sum[first, :] = both(far, first).astype(BF)
    far_up = send(far_sum.at[first], far_first, 4, up)
    far_sum[second, :] = both(far, second).astype(BF)
    far_down = send(far_sum.at[second], far_second, 5, down)
    swap_up.wait_recv()
    up_sum[second, :] = both(ahead, second).astype(BF)
    up_second = send(up_sum.at[second], got_down.at[second], 6, up)
    swap_down.wait_recv()
    down_sum[first, :] = both(behind, first).astype(BF)
    down_first = send(down_sum.at[first], got_up.at[first], 7, down)
    far_up.wait_recv()
    up_sum[first, :] = (both(ahead, first) + far_first[...].astype(F32)).astype(BF)
    up_first = send(up_sum.at[first], got_down.at[first], 8, up)
    far_down.wait_recv()
    down_sum[second, :] = (both(behind, second) + far_second[...].astype(F32)).astype(BF)
    down_second = send(down_sum.at[second], got_up.at[second], 9, down)
    swap_own.wait_recv()
    out[...] = parts[mine + x].astype(F32) + from_partner[x].astype(F32)
    up_second.wait_recv()
    up_first.wait_recv()
    down_first.wait_recv()
    down_second.wait_recv()
    out[...] = out[...] + got_down[...].astype(F32) + got_up[...].astype(F32)
    for copy in (
        swap_far,
        swap_up,
        swap_down,
        swap_own,
        far_up,
        far_down,
        up_second,
        down_first,
        up_first,
        down_second,
    ):
        copy.wait_send()


def team_scatter(parts, collective_id):
    count, rows, columns = parts.shape
    half = rows // 32 * 16
    block = pltpu.VMEM((rows, columns), BF)
    return pl.pallas_call(
        functools.partial(scatter_kernel, half),
        out_shape=jax.ShapeDtypeStruct((rows, columns), F32),
        in_specs=[VMEM],
        out_specs=VMEM,
        scratch_shapes=[
            pltpu.VMEM((4, rows, columns), BF),
            block,
            block,
            block,
            pltpu.VMEM((half, columns), BF),
            pltpu.VMEM((rows - half, columns), BF),
            block,
            block,
            pltpu.SemaphoreType.DMA((10,)),
            pltpu.SemaphoreType.DMA((10,)),
        ],
        compiler_params=pltpu.CompilerParams(
            collective_id=collective_id, has_side_effects=True, vmem_limit_bytes=LIMIT
        ),
    )(parts)


TEAM_STEPS = tuple((dc, dx) for dc in range(2) for dx in range(4) if dc or dx)


def heads_to_rows_kernel(heads, extra, out, send_sems, recv_sems, local_sems):
    c, z, x = place()
    me = c * 4 + x
    spots = [((c + dc) % 2, (x + dx) % 4) for dc, dx in TEAM_STEPS]
    own_columns = pl.ds(pl.multiple_of(me * 128, 128), 128)
    local = pltpu.make_async_copy(heads.at[me], out.at[:, own_columns], local_sems.at[0])
    local.start()
    last = pltpu.make_async_copy(extra, out.at[:, pl.ds(1024, 128)], local_sems.at[1])
    last.start()
    greet([at(tc, z, tx) for tc, tx in spots])
    send = sender(send_sems, recv_sems)
    copies = [
        send(heads.at[tc * 4 + tx], out.at[:, own_columns], index, at(tc, z, tx))
        for index, (tc, tx) in enumerate(spots)
    ]
    for copy in copies:
        copy.wait_recv()
    for copy in copies:
        copy.wait_send()
    local.wait()
    last.wait()


def heads_to_rows(heads, extra):
    return pl.pallas_call(
        heads_to_rows_kernel,
        out_shape=jax.ShapeDtypeStruct((128, 1152), BF),
        in_specs=[VMEM, VMEM],
        out_specs=VMEM,
        scratch_shapes=[
            pltpu.SemaphoreType.DMA((7,)),
            pltpu.SemaphoreType.DMA((7,)),
            pltpu.SemaphoreType.DMA((2,)),
        ],
        compiler_params=pltpu.CompilerParams(
            collective_id=1, has_side_effects=True, vmem_limit_bytes=LIMIT
        ),
    )(heads, extra)


def rows_to_heads_kernel(rows, out, send_sems, recv_sems, local_sem):
    c, z, x = place()
    me = c * 4 + x
    spots = [((c + dc) % 2, (x + dx) % 4) for dc, dx in TEAM_STEPS]

    def columns(q):
        return rows.at[:, pl.ds(pl.multiple_of(q * 128, 128), 128)]

    local = pltpu.make_async_copy(columns(me), out.at[me], local_sem)
    local.start()
    greet([at(tc, z, tx) for tc, tx in spots])
    send = sender(send_sems, recv_sems)
    copies = [
        send(columns(tc * 4 + tx), out.at[me], index, at(tc, z, tx))
        for index, (tc, tx) in enumerate(spots)
    ]
    for copy in copies:
        copy.wait_recv()
    for copy in copies:
        copy.wait_send()
    local.wait()


def rows_to_heads(rows):
    return pl.pallas_call(
        rows_to_heads_kernel,
        out_shape=jax.ShapeDtypeStruct((8, 128, 128), BF),
        in_specs=[VMEM],
        out_specs=VMEM,
        scratch_shapes=[
            pltpu.SemaphoreType.DMA((7,)),
            pltpu.SemaphoreType.DMA((7,)),
            pltpu.SemaphoreType.DMA,
        ],
        compiler_params=pltpu.CompilerParams(
            collective_id=2, has_side_effects=True, vmem_limit_bytes=LIMIT
        ),
    )(rows)


GROUP_STEPS = tuple(
    (dc, dz, dx) for dx in (2, 1, 3, 0) for dz in range(2) for dc in range(2) if dc or dz or dx
)


def weights_kernel(blocks, common, out, out_common, send_sems, recv_sems, local_sems):
    c, z, x = place()
    slot = (c, z * 4 + x)
    spots = [((c + dc) % 2, (z + dz) % 2, (x + dx) % 4) for dc, dz, dx in GROUP_STEPS]
    locals_ = [
        pltpu.make_async_copy(blocks.at[c * 4 + x], out.at[slot], local_sems.at[0]),
        pltpu.make_async_copy(common, out_common.at[slot], local_sems.at[1]),
    ]
    for copy in locals_:
        copy.start()
    greet([at(*spot) for spot in spots])
    send = sender(send_sems, recv_sems)
    copies = []
    for index, (tc, tz, tx) in enumerate(spots):
        device = at(tc, tz, tx)
        copies.append(send(blocks.at[tc * 4 + tx], out.at[slot], 2 * index, device))
        copies.append(send(common, out_common.at[slot], 2 * index + 1, device))
    for copy in copies:
        copy.wait_recv()
    for copy in copies:
        copy.wait_send()
    for copy in locals_:
        copy.wait()


def spread_weights(blocks, common):
    return pl.pallas_call(
        weights_kernel,
        out_shape=(
            jax.ShapeDtypeStruct((2,) + blocks.shape, BF),
            jax.ShapeDtypeStruct((2, 8) + common.shape, BF),
        ),
        in_specs=[VMEM, VMEM],
        out_specs=(VMEM, VMEM),
        scratch_shapes=[
            pltpu.SemaphoreType.DMA((30,)),
            pltpu.SemaphoreType.DMA((30,)),
            pltpu.SemaphoreType.DMA((2,)),
        ],
        compiler_params=pltpu.CompilerParams(
            collective_id=3, has_side_effects=True, vmem_limit_bytes=LIMIT
        ),
    )(blocks, common)


def grads_kernel(blocks, out, got, send_sems, recv_sems, local_sem):
    c, z, x = place()
    spots = [((c + dc) % 2, (z + dz) % 2, (x + dx) % 4) for dc, dz, dx in GROUP_STEPS]
    slot = (z, c * 4 + x)
    local = pltpu.make_async_copy(blocks.at[c, z * 4 + x], got.at[slot], local_sem)
    local.start()
    greet([at(*spot) for spot in spots])
    send = sender(send_sems, recv_sems)
    copies = [
        send(blocks.at[tc, tz * 4 + tx], got.at[slot], index, at(tc, tz, tx))
        for index, (tc, tz, tx) in enumerate(spots)
    ]
    for copy in copies:
        copy.wait_recv()
    local.wait()
    for q in range(8):
        out[q] = (got[0, q].astype(F32) + got[1, q].astype(F32)).astype(BF)
    for copy in copies:
        copy.wait_send()


def collect_grads(blocks):
    shape = blocks.shape[1:]
    return pl.pallas_call(
        grads_kernel,
        out_shape=jax.ShapeDtypeStruct(shape, BF),
        in_specs=[VMEM],
        out_specs=VMEM,
        scratch_shapes=[
            pltpu.VMEM((2,) + shape, BF),
            pltpu.SemaphoreType.DMA((15,)),
            pltpu.SemaphoreType.DMA((15,)),
            pltpu.SemaphoreType.DMA,
        ],
        compiler_params=pltpu.CompilerParams(
            collective_id=4, has_side_effects=True, vmem_limit_bytes=LIMIT
        ),
    )(blocks)


def dot_nt(left, right):
    return lax.dot_general(left, right, (((1,), (1,)), ((), ())), preferred_element_type=F32)


def dot_tn(left, right):
    return lax.dot_general(left, right, (((0,), (0,)), ((), ())), preferred_element_type=F32)


def dot(left, right):
    return jnp.dot(left, right, preferred_element_type=F32)


def lane_half(block, which):
    lane = lax.broadcasted_iota(jnp.int32, block.shape, 1)
    keep = lane < 64 if which == 0 else lane >= 64
    return jnp.where(keep, block, jnp.zeros_like(block))


def softmax_rows(scores, start):
    row = lax.broadcasted_iota(jnp.int32, scores.shape, 0) + start
    key = lax.broadcasted_iota(jnp.int32, scores.shape, 1)
    masked = jnp.where(key <= row, scores, NEG_FILL)
    shifted = jnp.exp(masked - jnp.max(masked, axis=1, keepdims=True))
    return shifted * (1.0 / jnp.sum(shifted, axis=1, keepdims=True))


STEP = 256


def attend_kernel(projected, last_query, attended, attended_last):
    c, z, x = place()
    for start in range(0, 1024, STEP):
        size = start + STEP
        query = projected[start:size, 0:128] * 0.125
        total = jnp.zeros((STEP, 128), F32)
        for head in range(2):
            keys = lane_half(projected[0:size, 128:256], head)
            values = lane_half(projected[0:size, 256:384], head)
            soft = softmax_rows(dot_nt(query, keys), start).astype(BF)
            total = total + dot(soft, values)
        attended[start:size, :] = total.astype(BF)
    both = projected[:, 384:512]
    soft = softmax_rows(dot_nt(last_query[...] * 0.125, both), (c * 4 + x) * 128).astype(BF)
    attended_last[...] = dot(soft, lane_half(both, 1)).astype(BF)


def attend(projected, last_query):
    return pl.pallas_call(
        attend_kernel,
        out_shape=(
            jax.ShapeDtypeStruct((1024, 128), BF),
            jax.ShapeDtypeStruct((128, 128), BF),
        ),
        in_specs=[VMEM, VMEM],
        out_specs=(VMEM, VMEM),
        compiler_params=pltpu.CompilerParams(vmem_limit_bytes=LIMIT),
    )(projected, last_query)


def attend_back_kernel(
    projected, last_query, grad, last_grad, out, out_last, key_total, value_total
):
    c, z, x = place()
    key_total[...] = jnp.zeros_like(key_total)
    value_total[...] = jnp.zeros_like(value_total)
    for start in range(0, 1024, STEP):
        size = start + STEP
        query = projected[start:size, 0:128] * 0.125
        grad_rows = grad[start:size, :]
        total = jnp.zeros((STEP, 128), F32)
        for head in range(2):
            keys = lane_half(projected[0:size, 128:256], head)
            values = lane_half(projected[0:size, 256:384], head)
            soft = softmax_rows(dot_nt(query, keys), start)
            grad_soft = dot_nt(grad_rows, values)
            inner = jnp.sum(soft * grad_soft, axis=1, keepdims=True)
            grad_scores = (soft * (grad_soft - inner)).astype(BF)
            total = total + dot(grad_scores, keys)
            key_total[0:size, :] += dot_tn(grad_scores, lane_half(query, head))
            value_total[0:size, :] += dot_tn(soft.astype(BF), lane_half(grad_rows, head))
        out[start:size, 0:128] = (total * 0.125).astype(BF)
    out[:, 128:256] = key_total[...].astype(BF)
    out[:, 256:384] = value_total[...].astype(BF)
    both = projected[:, 384:512]
    query = last_query[...] * 0.125
    soft = softmax_rows(dot_nt(query, both), (c * 4 + x) * 128)
    grad_soft = dot_nt(last_grad[...], both)
    inner = jnp.sum(soft * grad_soft, axis=1, keepdims=True)
    grad_scores = (soft * (grad_soft - inner)).astype(BF)
    out_last[...] = (dot(grad_scores, lane_half(both, 0)) * 0.125).astype(BF)
    out[:, 384:512] = (dot_tn(grad_scores, query) + dot_tn(soft.astype(BF), last_grad[...])).astype(
        BF
    )


def attend_back(projected, last_query, grad, last_grad):
    return pl.pallas_call(
        attend_back_kernel,
        out_shape=(
            jax.ShapeDtypeStruct((1024, 512), BF),
            jax.ShapeDtypeStruct((128, 128), BF),
        ),
        in_specs=[VMEM] * 4,
        out_specs=(VMEM, VMEM),
        scratch_shapes=[pltpu.VMEM((1024, 128), F32), pltpu.VMEM((1024, 128), F32)],
        compiler_params=pltpu.CompilerParams(vmem_limit_bytes=LIMIT),
    )(projected, last_query, grad, last_grad)


def norm_forward(hidden, gain, offset):
    center = hidden - jnp.mean(hidden, axis=-1, keepdims=True)
    inverse = lax.rsqrt(jnp.mean(center * center, axis=-1, keepdims=True) + EPSILON)
    unit = center * inverse
    return unit * gain + offset, unit, inverse


def norm_backward(grad_rows, unit, inverse, gain):
    grad_unit = grad_rows * gain
    grad_in = inverse * (
        grad_unit
        - jnp.mean(grad_unit, axis=-1, keepdims=True)
        - unit * jnp.mean(grad_unit * unit, axis=-1, keepdims=True)
    )
    return grad_in, jnp.sum(grad_rows * unit, axis=0), jnp.sum(grad_rows, axis=0)


def gelu_pair(values):
    tangent = jnp.tanh(GELU_C * (values + 0.044715 * values * values * values))
    output = 0.5 * values * (1.0 + tangent)
    slope = 0.5 * (1.0 + tangent) + 0.5 * values * (1.0 - tangent * tangent) * GELU_C * (
        1.0 + 3.0 * 0.044715 * values * values
    )
    return output, slope


def layer_forward(hidden, w):
    normed, unit_one, inverse_one = norm_forward(hidden, w["gain_one"], w["bias_one"])
    normed = normed.astype(BF)
    normed_all = team_gather(normed).reshape(1024, D)
    projected = (dot(normed_all, w["qkv"]) + w["qkv_bias"]).astype(BF)
    last_query = (dot(normed, w["last_query"]) + w["last_bias"]).astype(BF)
    heads, last = attend(projected, last_query)
    attended = heads_to_rows(heads.reshape(8, 128, 128), last)
    middle = hidden + dot(attended, w["out"]) + w["out_bias"]
    second, unit_two, inverse_two = norm_forward(middle, w["gain_two"], w["bias_two"])
    second_all = team_gather(second.astype(BF)).reshape(1024, D)
    upper = dot(second_all, w["up"]) + w["up_bias"]
    activated = gelu_pair(upper)[0].astype(BF)
    parts = dot(activated, w["down"]).astype(BF).reshape(8, 128, D)
    output = middle + team_scatter(parts, 5) + w["down_bias"]
    saved = dict(
        normed=normed,
        normed_all=normed_all,
        unit_one=unit_one,
        inverse_one=inverse_one,
        projected=projected,
        last_query=last_query,
        attended=attended,
        unit_two=unit_two,
        inverse_two=inverse_two,
        second_all=second_all,
        upper=upper,
        activated=activated,
    )
    return output, saved


def layer_backward(grad_out, w, kept, q):
    grad_low = grad_out.astype(BF)
    grad_low_all = team_gather(grad_low).reshape(1024, D)
    slope = gelu_pair(kept["upper"])[1]
    up_grad = (dot_nt(grad_low_all, w["down"]) * slope).astype(BF)
    parts = dot_nt(up_grad, w["up"]).astype(BF).reshape(8, 128, D)
    grad_second = team_scatter(parts, 5)
    grad_in, gain_two, bias_two = norm_backward(
        grad_second, kept["unit_two"], kept["inverse_two"], w["gain_two"]
    )
    grad_middle = grad_out + grad_in
    middle_low = grad_middle.astype(BF)
    attended_grad = dot_nt(middle_low, w["out"]).astype(BF)
    heads_grad = rows_to_heads(attended_grad).reshape(1024, 128)
    qkv_grad, last_grad = attend_back(
        kept["projected"], kept["last_query"], heads_grad, attended_grad[:, 1024:]
    )
    parts = dot_nt(qkv_grad, w["qkv"]).astype(BF).reshape(8, 128, D)
    grad_normed = team_scatter(parts, 5) + dot_nt(last_grad, w["last_query"])
    grad_in, gain_one, bias_one = norm_backward(
        grad_normed, kept["unit_one"], kept["inverse_one"], w["gain_one"]
    )
    grad_input = grad_middle + grad_in

    grad_qkv = dot_tn(kept["normed_all"], qkv_grad)
    grad_last_query = dot_tn(kept["normed"], last_grad)
    grad_up = dot_tn(kept["second_all"], up_grad)
    grad_down = dot_tn(kept["activated"], grad_low_all)
    grad_out_w = dot_tn(kept["attended"], middle_low)
    split = jnp.concatenate([grad_qkv[:, :384], grad_up], axis=1).astype(BF).reshape(8, 136, 928)
    out_rows = jnp.concatenate([grad_out_w[:1024], grad_out_w[1088:]], axis=0)
    shared = jnp.concatenate(
        [out_rows, grad_qkv[:, 384:512], grad_last_query[:, :64]], axis=1
    ).reshape(8, 136, 1280)

    qkv_sums = jnp.sum(qkv_grad, axis=0, dtype=F32)
    last_sums = jnp.sum(last_grad, axis=0, dtype=F32)
    zeros = jnp.zeros((1024,), F32)
    qv = jnp.concatenate(
        [
            lax.dynamic_update_slice(zeros, qkv_sums[:128], (q * 128,)),
            last_sums[:64],
            lax.dynamic_update_slice(zeros, qkv_sums[256:384], (q * 128,)),
            qkv_sums[448:512],
        ]
    )
    up_sums = lax.dynamic_update_slice(
        jnp.zeros((FF,), F32), jnp.sum(up_grad, axis=0, dtype=F32), (q * 544,)
    )
    vectors = jnp.concatenate(
        [
            qv.reshape(8, 272),
            jnp.sum(middle_low, axis=0, dtype=F32).reshape(8, 136),
            gain_one.reshape(8, 136),
            bias_one.reshape(8, 136),
            gain_two.reshape(8, 136),
            bias_two.reshape(8, 136),
            up_sums.reshape(8, 544),
            jnp.sum(grad_low, axis=0, dtype=F32).reshape(8, 136),
        ],
        axis=1,
    )
    vectors = jnp.pad(vectors, ((0, 0), (0, 8 * 1280 - 1632))).reshape(8, 8, 1280)
    shared = jnp.concatenate([shared, vectors], axis=1).astype(BF)
    shared = team_scatter(shared, 6).astype(BF)
    return grad_input, (split, grad_down.astype(BF), shared)


BOTH = ("section", "shard")


def pairs(route):
    out = []
    for c in range(2):
        for z in range(2):
            for x in range(4):
                tc, tz = route(c, z)
                out.append((c * 8 + z * 4 + x, tc * 8 + tz * 4 + x))
    return out


def local(
    inputs,
    cotangent,
    w_qkv,
    qv_bias,
    w_out,
    out_bias,
    gain_one,
    bias_one,
    gain_two,
    bias_two,
    w_up,
    up_bias,
    w_down,
    down_bias,
):
    c, z, x = place()
    q = c * 4 + x
    swap = pairs(lambda a, b: (b, a))
    cross = pairs(lambda a, b: (1 - b, a))
    cross_back = pairs(lambda a, b: (b, 1 - a))

    def mine(array):
        return lax.ppermute(jnp.where(c == z, array[z], array[1 - z])[0], BOTH, swap)

    def by_z(own, other):
        return jnp.where(z == 0, jnp.stack([own, other]), jnp.stack([other, own]))

    small = jnp.concatenate(
        [
            qv_bias[0],
            out_bias[0],
            gain_one[0],
            bias_one[0],
            gain_two[0],
            bias_two[0],
            up_bias[0],
            down_bias[0],
        ]
    )
    own_qkv = w_qkv[0]
    last_cols = [own_qkv[:, part * D + 1024 : (part + 1) * D] for part in range(3)]
    common = jnp.concatenate(
        [
            jnp.concatenate(
                [last_cols[1], last_cols[2], last_cols[0], jnp.zeros((136, 64), BF)], axis=1
            ),
            jnp.pad(small, (0, 2048 - 1632)).reshape(8, 256),
        ]
    )
    blocks = jnp.concatenate(
        [own_qkv[:, part * D : part * D + 1024].reshape(136, 8, 128) for part in range(3)]
        + [w_up[0].reshape(136, 8, 544)],
        axis=2,
    ).transpose(1, 0, 2)
    all_blocks, all_common = spread_weights(blocks, common)
    all_out = lax.all_gather(w_out[0], BOTH, axis=0, tiled=True).reshape(2, D, D)
    down_own = lax.ppermute(w_down[0], BOTH, swap)
    down_other = lax.ppermute(w_down[0], BOTH, cross_back)
    all_down = by_z(down_own, down_other)

    def layer_weights(layer):
        cut = all_blocks[layer].reshape(D, 928)
        shared = all_common[layer, :, :136].reshape(D, 256)
        vec = all_common[layer, :, 136:].reshape(8, 2048)[:, :1632].astype(F32)

        def piece(start, size):
            return vec[:, start : start + size].reshape(-1)

        qv = piece(0, 272)
        none = jnp.zeros((128,), F32)
        qkv_bias = jnp.concatenate(
            [
                lax.dynamic_slice(qv, (q * 128,), (128,)),
                none,
                lax.dynamic_slice(qv, (D + q * 128,), (128,)),
                none[:64],
                qv[2 * D - 64 :],
            ]
        )
        out = all_out[layer]
        return dict(
            qkv=jnp.concatenate([cut[:, :384], shared[:, :128]], axis=1),
            last_query=shared[:, 128:],
            qkv_bias=qkv_bias,
            last_bias=jnp.concatenate([qv[1024:D], none[:64]]),
            out=jnp.concatenate([out[:1024], jnp.zeros((64, D), BF), out[1024:]]),
            out_bias=piece(272, 136),
            gain_one=piece(408, 136),
            bias_one=piece(544, 136),
            gain_two=piece(680, 136),
            bias_two=piece(816, 136),
            up=cut[:, 384:],
            up_bias=lax.dynamic_slice(piece(952, 544), (q * 544,), (544,)),
            down=all_down[layer],
            down_bias=piece(1496, 136),
        )

    weights = [layer_weights(0), layer_weights(1)]
    hidden = mine(inputs).astype(F32)
    top_grad = mine(cotangent).astype(F32)
    out_first, kept_first = layer_forward(hidden, weights[0])
    out_second, kept_second = layer_forward(out_first.astype(BF).astype(F32), weights[1])
    grad_second, parts_second = layer_backward(top_grad, weights[1], kept_second, q)
    grad_first, parts_first = layer_backward(
        grad_second.astype(BF).astype(F32), weights[0], kept_first, q
    )

    def home(first, second):
        own = lax.ppermute(jnp.where(z == 0, first, second), BOTH, swap)
        other = lax.ppermute(jnp.where(z == 0, second, first), BOTH, cross)
        return own, other

    def rows_home(first, second):
        own, other = home(first.astype(BF), second.astype(BF))
        stacked = jnp.where(c == 0, jnp.stack([own, other]), jnp.stack([other, own]))
        return stacked.astype(F32)[None, :, None]

    section_out = rows_home(out_first, out_second)
    input_grad = rows_home(grad_first, grad_second)

    def sum_home(first, second):
        own, other = home(first, second)
        return (own.astype(F32) + other.astype(F32)).astype(BF)

    down_grad = sum_home(parts_first[1], parts_second[1])
    shared_grad = sum_home(parts_first[2], parts_second[2])
    split_grad = collect_grads(jnp.stack([parts_first[0], parts_second[0]]))
    split_grad, down_grad, shared_grad = lax.psum((split_grad, down_grad, shared_grad), "replica")
    split_grad, down_grad, shared_grad = (
        array.astype(F32) for array in (split_grad, down_grad, shared_grad)
    )
    split_rows = split_grad.transpose(1, 0, 2)
    head_rows = split_rows[:, :, :384].reshape(136, 8, 3, 128)
    last = shared_grad[:136, D:]
    grad_qkv = jnp.concatenate(
        [
            head_rows[:, :, 0].reshape(136, 1024),
            last[:, 128:],
            head_rows[:, :, 1].reshape(136, 1024),
            last[:, :64],
            head_rows[:, :, 2].reshape(136, 1024),
            last[:, 64:128],
        ],
        axis=1,
    )
    grad_up = split_rows[:, :, 384:].reshape(136, FF)
    vec = shared_grad[136:].reshape(-1)
    grads = (
        grad_qkv,
        vec[:272],
        shared_grad[:136, :D],
        vec[272:408],
        vec[408:544],
        vec[544:680],
        vec[680:816],
        vec[816:952],
        grad_up,
        vec[952:1496],
        down_grad,
        vec[1496:1632],
    )
    return (section_out, input_grad) + tuple(grad[None] for grad in grads)


def solution(mesh):
    return jax.shard_map(
        local,
        mesh=mesh,
        in_specs=(
            P(None, "replica", "shard", None),
            P(None, "replica", "shard", None),
            P("section", "shard", None),
            P("section", "shard"),
            P("section", "shard", None),
            P("section", "shard"),
            P("section", "shard"),
            P("section", "shard"),
            P("section", "shard"),
            P("section", "shard"),
            P("section", "shard", None),
            P("section", "shard"),
            P("section", "shard", None),
            P("section", "shard"),
        ),
        out_specs=(
            P("section", None, "replica", "shard", None),
            P("section", None, "replica", "shard", None),
            P("section", "shard", None),
            P("section", "shard"),
            P("section", "shard", None),
            P("section", "shard"),
            P("section", "shard"),
            P("section", "shard"),
            P("section", "shard"),
            P("section", "shard"),
            P("section", "shard", None),
            P("section", "shard"),
            P("section", "shard", None),
            P("section", "shard"),
        ),
        check_vma=False,
    )
```

time: 1880 us -> 971 us (0.52)
  waiting for transfers between devices: 1330 us -> 174 us
  Pallas kernels: 0 us -> 489 us
  blocking collectives: 109 us -> 0 us
  matrix products: 158 us -> 80 us
  local copies, waits for them, and re-layouts: 169 us -> 108 us
  starting transfers between devices: 7.63 us -> 37.5 us
    all_gather x16 -> x1, waiting for transfers between devices: 718 us -> 0.01 us  [local(): lax.all_gather(w_out[0], BOTH, axis=0, tiled=True).reshape(2, D, D)]
    pallas_call x0 -> x24, Pallas kernels: none -> 489 us  [the longest x8 149 us: team_scatter(): pl.pallas_call(functools.partial(scatter_kernel, half), out_shape=jax.Sha...]
    reduce_scatter x3 -> x0, waiting for transfers between devices: 297 us -> none  [the longest x1 109 us: local(): lax.psum_scatter(grad_down_w.astype(jnp.bfloat16), 'shard', scatter_dimen...]
    unnamed x34 -> x2, waiting for transfers between devices: 210 us -> 0.7 us
    unnamed x293 -> x241, local copies, waits for them, and re-layouts: 130 us -> 16.8 us
    dot_general x34 -> x30, matrix products: 158 us -> 80 us  [the longest x10 27.5 us: dot_nt(): lax.dot_general(left, right, (((1,), (1,)), ((), ())), preferred_element_...]
    psum x1, waiting for transfers between devices: 91.2 us -> 158 us  [local(): lax.psum((split_grad, down_grad, shared_grad), 'replica')]
    psum x1 -> x0, blocking collectives: 40.2 us -> none  [local(): lax.psum(shard_qv.astype(jnp.bfloat16), 'replica').astype(jnp.float32)]
  transfers between devices with their start and end apart: 31 -> 14, of which waited for: 29 -> 3; matrix products, arithmetic and copies ran while one was open for 15% -> 6% of each run, Pallas kernels for 0% -> 24%
where the time goes in v1:
time: 971 us; the launch traced here: 963 us
  Pallas kernels  489 us (50%)
  waiting for transfers between devices  174 us (18%)
  local copies, waits for them, and re-layouts  108 us (11%)
  matrix products  80 us (8%)
  other arithmetic  57.4 us (6%)
  starting transfers between devices  37.5 us (4%)
  between operations  16.1 us (2%)
    psum x1, waiting for transfers between devices, local(): lax.psum((split_grad, down_grad, shared_grad), 'replica')  158 us
    pallas_call x8, Pallas kernels, team_scatter(): pl.pallas_call(functools.partial(scatter_kernel, half), out_shape=jax.Sha...  149 us
    pallas_call x6, Pallas kernels, team_gather(): pl.pallas_call(functools.partial(gather_kernel, rows // 2), out_shape=jax...  111 us
    pallas_call x1, Pallas kernels, spread_weights(): pl.pallas_call(weights_kernel, out_shape=(jax.ShapeDtypeStruct((2,) + blo...  93.1 us
    pallas_call x1, Pallas kernels, collect_grads(): pl.pallas_call(grads_kernel, out_shape=jax.ShapeDtypeStruct(shape, BF), i...  68.7 us
    dot_general x10, matrix products, dot_nt(): lax.dot_general(left, right, (((1,), (1,)), ((), ())), preferred_element_...  27.5 us
    dot_general x10, matrix products, dot_tn(): lax.dot_general(left, right, (((0,), (0,)), ((), ())), preferred_element_...  26.5 us
    dot_general x10, matrix products, dot(): return jnp.dot(left, right, preferred_element_type=F32)  26 us
  transfers between devices with their start and end apart: 14, of which 3 were waited for; matrix products, arithmetic and copies ran while one was open for 6% of the time, Pallas kernels for 24%

profile of v1, /device:TPU:16, one launch (start us, length us, event | category | flops | bytes accessed | tf_op | source)
XLA Modules:
  0.0 962.6 jit_solution(14876436170058721389)
XLA Ops:
  10.0 11.1 %collective-permute-start.1 = (bf16[544,1088]{1,0:T(8,128)(2,1)}, bf16[544,1088]{1,0:T(8,128)(2,1)}, u32[]{:S(2)}, u32[]{:S(2)}) collective-permute-start(bf16[544,1088]{1,0:T(8,128)(2,1)} %bitcast.239), channel_id=1, source_target_pairs={{0,0},{8,8},{16,16},{24,24},{32,64},{40,72},{48,80},{56,88},{64,32... | collective-permute-start | bytes 3551240 | tf_op jit(solution)/shard_map/ppermute | solution.py:694
  26.2 3.7 collective-permute-start.5
  38.3 93.1 %shard_map.245 = (bf16[2,8,136,928]{3,2,1,0:T(8,128)(2,1)}, bf16[2,8,144,256]{3,2,1,0:T(8,128)(2,1)}) custom-call(bf16[8,136,928]{2,1,0:T(8,128)(2,1)} %maximum_bitcast_fusion.blocks, bf16[144,256]{1,0:T(8,128)(2,1)} %pad_maximum_fusion.16.common), custom_call_target="tpu_custom_call" | custom-call | tf_op jit(solution)/shard_map/pallas_call | solution.py:330
  134.8 4.5 fusion.84
  150.6 19.8 %shard_map.246 = bf16[8,128,1088]{2,1,0:T(8,128)(2,1)} custom-call(bf16[128,1088]{1,0:T(8,128)(2,1)} %fusion.55.own), custom_call_target="tpu_custom_call" | custom-call | tf_op jit(solution)/shard_map/pallas_call | solution.py:100
  170.5 4.2 add_convert_fusion.2.projected
  175.5 5.4 shard_map.247
  180.9 8.7 shard_map.248
  189.6 18.0 %shard_map.256 = bf16[8,128,1088]{2,1,0:T(8,128)(2,1)} custom-call(bf16[128,1088]{1,0:T(8,128)(2,1)} %collective-permute-done.5.own), custom_call_target="tpu_custom_call" | custom-call | tf_op jit(solution)/shard_map/pallas_call | solution.py:100
  207.7 4.2 maximum_select_fusion
  213.5 4.2 slice_bitcast_fusion
  220.3 19.8 %shard_map.249 = bf16[8,128,1088]{2,1,0:T(8,128)(2,1)} custom-call(bf16[128,1088]{1,0:T(8,128)(2,1)} %add_convert_fusion.7.own), custom_call_target="tpu_custom_call" | custom-call | tf_op jit(solution)/shard_map/pallas_call | solution.py:100
  240.2 3.5 fusion.27
  250.0 18.0 %shard_map.250 = f32[128,1088]{1,0:T(8,128)} custom-call(bf16[8,128,1088]{2,1,0:T(8,128)(2,1)} %bitcast.174), custom_call_target="tpu_custom_call" | custom-call | tf_op jit(solution)/shard_map/pallas_call | solution.py:193
  270.5 17.0 %shard_map.251 = bf16[8,128,1088]{2,1,0:T(8,128)(2,1)} custom-call(bf16[128,1088]{1,0:T(8,128)(2,1)} %fusion.46.own), custom_call_target="tpu_custom_call" | custom-call | tf_op jit(solution)/shard_map/pallas_call | solution.py:100
  288.5 4.3 add_convert_fusion.1.projected
  292.8 5.4 shard_map.252
  298.1 10.2 %shard_map.253 = bf16[128,1152]{1,0:T(8,128)(2,1)} custom-call(bf16[8,128,128]{2,1,0:T(8,128)(2,1)} %bitcast.227, bf16[128,128]{1,0:T(8,128)(2,1)} %get-tuple-element.29.extra), custom_call_target="tpu_custom_call" | custom-call | tf_op jit(solution)/shard_map/pallas_call | solution.py:243
  311.3 18.9 %shard_map.254 = bf16[8,128,1088]{2,1,0:T(8,128)(2,1)} custom-call(bf16[128,1088]{1,0:T(8,128)(2,1)} %add_convert_fusion.5.own), custom_call_target="tpu_custom_call" | custom-call | tf_op jit(solution)/shard_map/pallas_call | solution.py:100
  330.3 3.5 fusion.24
  333.8 3.8 convolution_convert_fusion.6
  345.3 4.2 copy.68
  349.5 18.0 %shard_map.257 = f32[128,1088]{1,0:T(8,128)} custom-call(bf16[8,128,1088]{2,1,0:T(8,128)(2,1)} %bitcast.175), custom_call_target="tpu_custom_call" | custom-call | tf_op jit(solution)/shard_map/pallas_call | solution.py:193
  369.4 4.4 copy.65
  373.8 18.1 %shard_map.255 = f32[128,1088]{1,0:T(8,128)} custom-call(bf16[8,128,1088]{2,1,0:T(8,128)(2,1)} %bitcast.176), custom_call_target="tpu_custom_call" | custom-call | tf_op jit(solution)/shard_map/pallas_call | solution.py:193
  396.9 8.8 shard_map.258
  405.7 9.9 %shard_map.259 = (bf16[1024,512]{1,0:T(8,128)(2,1)}, bf16[128,128]{1,0:T(8,128)(2,1)}) custom-call(bf16[1024,512]{1,0:T(8,128)(2,1)} %add_convert_fusion.1.projected, bf16[128,128]{1,0:T(8,128)(2,1)} %fusion.30.last_query, bf16[1024,128]{1,0:T(8,128)(2,1)} %bitcast.214, bf16[128,128]{1,0:T(8,128)(2,1)} %slice.418.last_grad), custom_call_target="tpu_custom_call" | custom-call | tf_op jit(solution)/shard_map/pallas_call | solution.py:485
  430.3 4.1 copy.69
  434.5 18.1 %shard_map.260 = f32[128,1088]{1,0:T(8,128)} custom-call(bf16[8,128,1088]{2,1,0:T(8,128)(2,1)} %bitcast.177), custom_call_target="tpu_custom_call" | custom-call | tf_op jit(solution)/shard_map/pallas_call | solution.py:193
  456.4 17.2 %shard_map.261 = bf16[8,128,1088]{2,1,0:T(8,128)(2,1)} custom-call(bf16[128,1088]{1,0:T(8,128)(2,1)} %get-tuple-element.82.own), custom_call_target="tpu_custom_call" | custom-call | tf_op jit(solution)/shard_map/pallas_call | solution.py:100
  473.7 5.2 convert_reduce_fusion.1
  485.4 4.5 copy.71
  490.0 18.1 %shard_map.262 = f32[128,1088]{1,0:T(8,128)} custom-call(bf16[8,128,1088]{2,1,0:T(8,128)(2,1)} %bitcast.178), custom_call_target="tpu_custom_call" | custom-call | tf_op jit(solution)/shard_map/pallas_call | solution.py:193
  513.9 9.4 shard_map.263
  523.4 9.9 %shard_map.264 = (bf16[1024,512]{1,0:T(8,128)(2,1)}, bf16[128,128]{1,0:T(8,128)(2,1)}) custom-call(bf16[1024,512]{1,0:T(8,128)(2,1)} %add_convert_fusion.2.projected, bf16[128,128]{1,0:T(8,128)(2,1)} %fusion.29.last_query, bf16[1024,128]{1,0:T(8,128)(2,1)} %bitcast.215, bf16[128,128]{1,0:T(8,128)(2,1)} %slice.419.last_grad), custom_call_target="tpu_custom_call" | custom-call | tf_op jit(solution)/shard_map/pallas_call | solution.py:485
  561.8 4.3 pad_maximum_fusion.2
  569.5 3.6 pad_maximum_fusion.3.parts
  573.2 20.4 %shard_map.268 = f32[144,1280]{1,0:T(8,128)} custom-call(bf16[8,144,1280]{2,1,0:T(8,128)(2,1)} %pad_maximum_fusion.3.parts), custom_call_target="tpu_custom_call" | custom-call | tf_op jit(solution)/shard_map/pallas_call | solution.py:193
  596.0 5.1 fusion.17
  601.2 3.7 broadcast_select_fusion.1
  609.3 18.0 %shard_map.265 = f32[128,1088]{1,0:T(8,128)} custom-call(bf16[8,128,1088]{2,1,0:T(8,128)(2,1)} %bitcast.179), custom_call_target="tpu_custom_call" | custom-call | tf_op jit(solution)/shard_map/pallas_call | solution.py:193
  632.0 11.1 %collective-permute-start.10 = (bf16[544,1088]{1,0:T(8,128)(2,1)}, bf16[544,1088]{1,0:T(8,128)(2,1)}, u32[]{:S(2)}, u32[]{:S(2)}) collective-permute-start(bf16[544,1088]{1,0:T(8,128)(2,1)} %get-tuple-element.99), channel_id=1, source_target_pairs={{0,0},{8,8},{16,16},{24,24},{32,64},{40,72},{48,80},{56,88},{64,32... | collective-permute-start | bytes 3551240 | tf_op jit(solution)/shard_map/ppermute | solution.py:746
  643.1 4.5 pad_maximum_fusion
  651.0 3.6 pad_maximum_fusion.1.parts
  654.7 20.4 %shard_map.267 = f32[144,1280]{1,0:T(8,128)} custom-call(bf16[8,144,1280]{2,1,0:T(8,128)(2,1)} %pad_maximum_fusion.1.parts), custom_call_target="tpu_custom_call" | custom-call | tf_op jit(solution)/shard_map/pallas_call | solution.py:193
  683.9 68.7 %shard_map.266 = bf16[8,136,928]{2,1,0:T(8,128)(2,1)} custom-call(bf16[2,8,136,928]{3,2,1,0:T(8,128)(2,1)} %maximum_maximum_fusion.blocks), custom_call_target="tpu_custom_call" | custom-call | tf_op jit(solution)/shard_map/pallas_call | solution.py:372
  765.6 13.9 %collective-permute-done.7 = bf16[128,1088]{1,0:T(8,128)(2,1)S(1)} collective-permute-done((bf16[128,1088]{1,0:T(8,128)(2,1)S(1)}, bf16[128,1088]{1,0:T(8,128)(2,1)S(1)}, u32[]{:S(2)}, u32[]{:S(2)}) %collective-permute-start.7) | collective-permute-done | bytes 278560 | tf_op jit(solution)/shard_map/ppermute | solution.py:747
  781.0 158.2 %all-reduce.8.cloned.1.call-done = (bf16[136,8,928]{2,0,1:T(8,128)(2,1)}, bf16[144,1280]{1,0:T(8,128)(2,1)}, bf16[1,544,1088]{2,1,0:T(8,128)(2,1)}) async-done(((bf16[136,8,928]{2,0,1:T(8,128)(2,1)}, bf16[144,1280]{1,0:T(8,128)(2,1)}, bf16[1,544,1088]{2,1,0:T(8,128)(2,1)}), (bf16[136,8,928]{2,0,1:T(8,128)(2,1)}, bf16[144,1280]{1,0:T(8,128)(2,1)}, ...) | async-done | bytes 3571728 | tf_op jit(solution)/shard_map/psum | solution.py:765
  (482 shorter events, 179.7 us)
Async XLA Ops:
  7.2 204.7 %all-gather.3.cloned.1.call-start = ((), (), s32[]{:S(2)}) async-start(), calls=%async_computation | async-start | bytes 5326848 | tf_op jit(solution)/shard_map/all_gather | solution.py:693
  7.9 931.3 %all-reduce.8.cloned.1.call-start = ((), (), s32[]{:S(2)}) async-start(), calls=%async_computation.1 | async-start | bytes 7700480 | tf_op jit(solution)/shard_map/psum | solution.py:765
  8.0 199.7 %collective-permute-start.2 = (bf16[544,1088]{1,0:T(8,128)(2,1)}, bf16[544,1088]{1,0:T(8,128)(2,1)}, u32[]{:S(2)}, u32[]{:S(2)}) collective-permute-start(bf16[544,1088]{1,0:T(8,128)(2,1)} %bitcast.238), channel_id=1, source_target_pairs={{0,32},{8,40},{16,48},{24,56},{32,96},{40,104},{48,112},{56,120},{... | collective-permute-start | bytes 3551240 | tf_op jit(solution)/shard_map/ppermute | solution.py:695
  10.0 197.7 %collective-permute-start.1 = (bf16[544,1088]{1,0:T(8,128)(2,1)}, bf16[544,1088]{1,0:T(8,128)(2,1)}, u32[]{:S(2)}, u32[]{:S(2)}) collective-permute-start(bf16[544,1088]{1,0:T(8,128)(2,1)} %bitcast.239), channel_id=1, source_target_pairs={{0,0},{8,8},{16,16},{24,24},{32,64},{40,72},{48,80},{56,88},{64,32... | collective-permute-start | bytes 3551240 | tf_op jit(solution)/shard_map/ppermute | solution.py:694
  23.4 125.9 %collective-permute-start = (bf16[128,1088]{1,0:T(8,128)(2,1)}, bf16[128,1088]{1,0:T(8,128)(2,1)S(1)}, u32[]{:S(2)}, u32[]{:S(2)}) collective-permute-start(bf16[128,1088]{1,0:T(8,128)(2,1)} %select_bitcast_fusion.1), channel_id=1, source_target_pairs={{0,0},{8,8},{16,16},{24,24},{32,64},{40,72},{48,80},{56,88},{64,32... | collective-permute-start | bytes 835592 | tf_op jit(solution)/shard_map/ppermute | solution.py:660
  26.2 163.4 %collective-permute-start.5 = (bf16[128,1088]{1,0:T(8,128)(2,1)}, bf16[128,1088]{1,0:T(8,128)(2,1)}, u32[]{:S(2)}, u32[]{:S(2)}) collective-permute-start(bf16[128,1088]{1,0:T(8,128)(2,1)} %select_bitcast_fusion), channel_id=1, source_target_pairs={{0,0},{8,8},{16,16},{24,24},{32,64},{40,72},{48,80},{56,88},{64,32... | collective-permute-start | bytes 835592 | tf_op jit(solution)/shard_map/ppermute | solution.py:660
  134.8 39.8 %copy-start.30 = (bf16[1,8,136,256]{3,2,1,0:T(8,128)(2,1)}, bf16[1,8,136,256]{3,2,1,0:T(8,128)(2,1)S(1)}, u32[]{:S(2)}) copy-start(bf16[1,8,136,256]{3,2,1,0:T(8,128)(2,1)S(1)} %get-tuple-element.107) | copy-start | bytes 1671172
  139.4 100.8 %copy-start.7 = (bf16[1,8,136,928]{3,2,1,0:T(8,128)(2,1)}, bf16[1,8,136,928]{3,2,1,0:T(8,128)(2,1)S(1)}, u32[]{:S(2)}) copy-start(bf16[1,8,136,928]{3,2,1,0:T(8,128)(2,1)S(1)} %get-tuple-element.98) | copy-start | bytes 6057988
  141.7 101.9 %copy-start.84 = (f32[544]{0:T(1024)}, f32[544]{0:T(1024)S(1)}, u32[]{:S(2)}) copy-start(f32[544]{0:T(1024)S(1)} %dynamic_slice.34) | copy-start | bytes 6532
  147.8 69.9 %copy-start.79 = (bf16[1152]{0:T(1024)(128)(2,1)}, bf16[1152]{0:T(1024)(128)(2,1)S(1)}, u32[]{:S(2)}) copy-start(bf16[1152]{0:T(1024)(128)(2,1)S(1)} %pad.52.clone) | copy-start | bytes 6916
  149.2 21.2 %copy-start.42 = (bf16[1088,384]{1,0:T(8,128)(2,1)S(1)}, bf16[1088,384]{1,0:T(8,128)(2,1)}, u32[]{:S(2)}) copy-start(bf16[1088,384]{1,0:T(8,128)(2,1)} %slice.385) | copy-start | bytes 2506756
  149.4 25.3 %copy-start.74 = (f32[128]{0:T(128)}, f32[128]{0:T(128)S(1)}, u32[]{:S(2)}) copy-start(f32[128]{0:T(128)S(1)} %broadcast_multiply_fusion.11) | copy-start | bytes 1540
  149.6 25.0 %copy-start.87 = (f32[128]{0:T(128)}, f32[128]{0:T(128)S(1)}, u32[]{:S(2)}) copy-start(f32[128]{0:T(128)S(1)} %add_rsqrt_fusion.3) | copy-start | bytes 1540
  219.2 24.5 %copy-start.70 = (f32[128]{0:T(128)}, f32[128]{0:T(128)S(1)}, u32[]{:S(2)}) copy-start(f32[128]{0:T(128)S(1)} %broadcast_multiply_fusion.10) | copy-start | bytes 1540
  219.4 24.2 %copy-start.77 = (f32[128]{0:T(128)}, f32[128]{0:T(128)S(1)}, u32[]{:S(2)}) copy-start(f32[128]{0:T(128)S(1)} %add_rsqrt_fusion.2) | copy-start | bytes 1540
  268.0 19.6 %copy-start.32 = (bf16[1,8,136,256]{3,2,1,0:T(8,128)(2,1)S(1)}, bf16[1,8,136,256]{3,2,1,0:T(8,128)(2,1)}, u32[]{:S(2)}) copy-start(bf16[1,8,136,256]{3,2,1,0:T(8,128)(2,1)} %get-tuple-element.106) | copy-start | bytes 1671172
  268.0 19.6 %copy-start.102 = (f32[128]{0:T(128)S(1)}, f32[128]{0:T(128)}, u32[]{:S(2)}) copy-start(f32[128]{0:T(128)} %concatenate.147) | copy-start | bytes 1540
  269.3 19.1 %copy-start.44 = (bf16[1088,384]{1,0:T(8,128)(2,1)S(1)}, bf16[1088,384]{1,0:T(8,128)(2,1)}, u32[]{:S(2)}) copy-start(bf16[1088,384]{1,0:T(8,128)(2,1)} %slice.403) | copy-start | bytes 2506756
  269.3 19.1 %copy-start.55 = (bf16[1088,128]{1,0:T(8,128)(2,1)S(1)}, bf16[1088,128]{1,0:T(8,128)(2,1)}, u32[]{:S(2)}) copy-start(bf16[1088,128]{1,0:T(8,128)(2,1)} %slice.404) | copy-start | bytes 835588
  269.3 19.1 %copy-start.94 = (f32[512]{0:T(512)S(1)}, f32[512]{0:T(512)}, u32[]{:S(2)}) copy-start(f32[512]{0:T(512)} %concatenate.146) | copy-start | bytes 6148
  269.6 18.9 %copy-start.90 = (f32[128]{0:T(128)}, f32[128]{0:T(128)S(1)}, u32[]{:S(2)}) copy-start(f32[128]{0:T(128)S(1)} %add_rsqrt_fusion.1) | copy-start | bytes 1540
  288.4 19.9 %copy-start.24 = (bf16[1024,1088]{1,0:T(8,128)(2,1)S(1)}, bf16[1024,1088]{1,0:T(8,128)(2,1)}, u32[]{:S(2)}) copy-start(bf16[1024,1088]{1,0:T(8,128)(2,1)} %get-tuple-element.93) | copy-start | bytes 6684676
  288.4 19.9 %copy-start.59 = (bf16[64,1088]{1,0:T(8,128)(2,1)S(1)}, bf16[64,1088]{1,0:T(8,128)(2,1)}, u32[]{:S(2)}) copy-start(bf16[64,1088]{1,0:T(8,128)(2,1)} %get-tuple-element.95) | copy-start | bytes 417796
  288.4 19.9 %copy-start.73 = (f32[1088]{0:T(1024)S(1)}, f32[1088]{0:T(1024)}, u32[]{:S(2)}) copy-start(f32[1088]{0:T(1024)} %add.324) | copy-start | bytes 13060
  288.5 19.9 %copy-start.80 = (bf16[1152]{0:T(1024)(128)(2,1)S(1)}, bf16[1152]{0:T(1024)(128)(2,1)}, u32[]{:S(2)}) copy-start(bf16[1152]{0:T(1024)(128)(2,1)} %copy-done.79) | copy-start | bytes 6916
  310.2 20.1 %copy-start.9 = (bf16[1,8,136,928]{3,2,1,0:T(8,128)(2,1)S(1)}, bf16[1,8,136,928]{3,2,1,0:T(8,128)(2,1)}, u32[]{:S(2)}) copy-start(bf16[1,8,136,928]{3,2,1,0:T(8,128)(2,1)} %get-tuple-element.97) | copy-start | bytes 6057988
  373.8 18.1 %copy-start.6 = (f32[128,1088]{1,0:T(8,128)S(1)}, f32[128,1088]{1,0:T(8,128)}, u32[]{:S(2)}) copy-start(f32[128,1088]{1,0:T(8,128)} %shard_map.257) | copy-start | bytes 1671172
  434.4 20.3 %copy-start.35 = (bf16[128,1088]{1,0:T(8,128)(2,1)S(1)}, bf16[128,1088]{1,0:T(8,128)(2,1)}, u32[]{:S(2)}) copy-start(bf16[128,1088]{1,0:T(8,128)(2,1)} %get-tuple-element.117) | copy-start | bytes 835588
  454.7 19.0 %copy-start.18 = (bf16[2,544,1088]{2,1,0:T(8,128)(2,1)S(1)}, bf16[2,544,1088]{2,1,0:T(8,128)(2,1)}, u32[]{:S(2)}) copy-start(bf16[2,544,1088]{2,1,0:T(8,128)(2,1)} %maximum_select_fusion) | copy-start | bytes 7102468
  454.7 19.0 %copy-start.85 = (f32[544]{0:T(1024)S(1)}, f32[544]{0:T(1024)}, u32[]{:S(2)}) copy-start(f32[544]{0:T(1024)} %copy-done.84) | copy-start | bytes 6532
  454.7 19.0 %copy-start.108 = (f32[1024,544]{0,1:T(8,128)S(1)}, f32[1024,544]{0,1:T(8,128)}, u32[]{:S(2)}) copy-start(f32[1024,544]{0,1:T(8,128)} %copy-done.107) | copy-start | bytes 6684676
  489.9 20.2 %copy-start.3 = (bf16[128,1088]{1,0:T(8,128)(2,1)S(1)}, bf16[128,1088]{1,0:T(8,128)(2,1)}, u32[]{:S(2)}) copy-start(bf16[128,1088]{1,0:T(8,128)(2,1)} %get-tuple-element.82.own) | copy-start | bytes 835588
  512.1 31.3 %copy-start.4 = (f32[128,1088]{1,0:T(8,128)}, f32[128,1088]{1,0:T(8,128)S(1)}, u32[]{:S(2)}) copy-start(f32[128,1088]{1,0:T(8,128)S(1)} %get-tuple-element.84) | copy-start | bytes 1671172
  512.1 21.1 %copy-start.14 = (bf16[128,1088]{1,0:T(8,128)(2,1)S(1)}, bf16[128,1088]{1,0:T(8,128)(2,1)}, u32[]{:S(2)}) copy-start(bf16[128,1088]{1,0:T(8,128)(2,1)} %fusion.55.own) | copy-start | bytes 835588
  573.2 20.4 %copy-start = (bf16[8,128,1088]{2,1,0:T(8,128)(2,1)S(1)}, bf16[8,128,1088]{2,1,0:T(8,128)(2,1)}, u32[]{:S(2)}) copy-start(bf16[8,128,1088]{2,1,0:T(8,128)(2,1)} %shard_map.254) | copy-start | bytes 6684676
  609.3 21.0 %copy-start.69 = (bf16[8,136]{1,0:T(8,128)(2,1)S(1)}, bf16[8,136]{1,0:T(8,128)(2,1)}, u32[]{:S(2)}) copy-start(bf16[8,136]{1,0:T(8,128)(2,1)} %reshape.542) | copy-start | bytes 6532
  609.3 21.8 %slice-start.2 = ((bf16[1088,512]{1,0:T(8,128)(2,1)}), bf16[1088,128]{1,0:T(8,128)(2,1)S(1)}, s32[]{:S(2)}) async-start(bf16[1088,512]{1,0:T(8,128)(2,1)} %copy-done.11), calls=%async_computation.4 | async-start | bytes 557056 | tf_op jit(solution)/shard_map/slice | solution.py:588
  632.0 121.5 %collective-permute-start.10 = (bf16[544,1088]{1,0:T(8,128)(2,1)}, bf16[544,1088]{1,0:T(8,128)(2,1)}, u32[]{:S(2)}, u32[]{:S(2)}) collective-permute-start(bf16[544,1088]{1,0:T(8,128)(2,1)} %get-tuple-element.99), channel_id=1, source_target_pairs={{0,0},{8,8},{16,16},{24,24},{32,64},{40,72},{48,80},{56,88},{64,32... | collective-permute-start | bytes 3551240 | tf_op jit(solution)/shard_map/ppermute | solution.py:746
  643.0 110.4 %collective-permute-start.11 = (bf16[544,1088]{1,0:T(8,128)(2,1)}, bf16[544,1088]{1,0:T(8,128)(2,1)}, u32[]{:S(2)}, u32[]{:S(2)}) collective-permute-start(bf16[544,1088]{1,0:T(8,128)(2,1)} %get-tuple-element.100), channel_id=1, source_target_pairs={{0,64},{8,72},{16,80},{24,88},{32,0},{40,8},{48,16},{56,24},{64,96... | collective-permute-start | bytes 3551240 | tf_op jit(solution)/shard_map/ppermute | solution.py:747
  654.6 20.4 %copy-start.12 = (f32[144,1280]{1,0:T(8,128)S(1)}, f32[144,1280]{1,0:T(8,128)}, u32[]{:S(2)}) copy-start(f32[144,1280]{1,0:T(8,128)} %shard_map.268) | copy-start | bytes 2211844
  654.6 24.8 %copy-start.26 = (bf16[1088,1024]{1,0:T(8,128)(2,1)S(1)}, bf16[1088,1024]{1,0:T(8,128)(2,1)}, u32[]{:S(2)}) copy-start(bf16[1088,1024]{1,0:T(8,128)(2,1)} %copy.74) | copy-start | bytes 6684676
  654.6 24.8 %copy-start.110 = (bf16[1024,544]{0,1:T(8,128)(2,1)S(1)}, bf16[1024,544]{0,1:T(8,128)(2,1)}, u32[]{:S(2)}) copy-start(bf16[1024,544]{0,1:T(8,128)(2,1)} %copy-done.109) | copy-start | bytes 3342340
  676.2 76.4 %collective-permute-start.8 = (bf16[144,1280]{1,0:T(8,128)(2,1)S(1)}, bf16[144,1280]{1,0:T(8,128)(2,1)S(1)}, u32[]{:S(2)}, u32[]{:S(2)}) collective-permute-start(bf16[144,1280]{1,0:T(8,128)(2,1)S(1)} %get-tuple-element.104), channel_id=1, source_target_pairs={{0,0},{8,8},{16,16},{24,24},{32,64},{40,72},{48,80},{56,88},{64,32... | collective-permute-start | bytes 1105928 | tf_op jit(solution)/shard_map/ppermute | solution.py:746
  676.9 75.7 %collective-permute-start.9 = (bf16[144,1280]{1,0:T(8,128)(2,1)S(1)}, bf16[144,1280]{1,0:T(8,128)(2,1)S(1)}, u32[]{:S(2)}, u32[]{:S(2)}) collective-permute-start(bf16[144,1280]{1,0:T(8,128)(2,1)S(1)} %get-tuple-element.105), channel_id=1, source_target_pairs={{0,64},{8,72},{16,80},{24,88},{32,0},{40,8},{48,16},{56,24},{64,96... | collective-permute-start | bytes 1105928 | tf_op jit(solution)/shard_map/ppermute | solution.py:747
  757.4 6.7 collective-permute-start.4
  757.7 6.4 collective-permute-start.3
  758.9 20.6 %collective-permute-start.7 = (bf16[128,1088]{1,0:T(8,128)(2,1)S(1)}, bf16[128,1088]{1,0:T(8,128)(2,1)S(1)}, u32[]{:S(2)}, u32[]{:S(2)}) collective-permute-start(bf16[128,1088]{1,0:T(8,128)(2,1)S(1)} %broadcast_select_fusion.4), channel_id=1, source_target_pairs={{0,64},{8,72},{16,80},{24,88},{32,0},{40,8},{48,16},{56,24},{64,96... | collective-permute-start | bytes 835592 | tf_op jit(solution)/shard_map/ppermute | solution.py:747
  762.1 17.5 %collective-permute-start.6 = (bf16[128,1088]{1,0:T(8,128)(2,1)S(1)}, bf16[128,1088]{1,0:T(8,128)(2,1)S(1)}, u32[]{:S(2)}, u32[]{:S(2)}) collective-permute-start(bf16[128,1088]{1,0:T(8,128)(2,1)S(1)} %get-tuple-element.87), channel_id=1, source_target_pairs={{0,0},{8,8},{16,16},{24,24},{32,64},{40,72},{48,80},{56,88},{64,32... | collective-permute-start | bytes 835592 | tf_op jit(solution)/shard_map/ppermute | solution.py:746
  (83 other events, 482.2 us)
Sparse Core Ops, SparseCore 0:
  9.7 85.0 all-gather.2
  756.7 182.5 all-reduce.7

commit v2 on v1

--- a/solution.py
+++ b/solution.py
@@ -53,69 +53,117 @@
     return make
 
 
-def gather_kernel(half, own, out, send_sems, recv_sems, local_sem):
+def gather_core(own, out, send_sems, recv_sems, local_sem, use):
     c, z, x = place()
     ahead, behind, far = (x + 1) % 4, (x + 3) % 4, (x + 2) % 4
     partner, up, down = at(1 - c, z, x), at(c, z, ahead), at(c, z, behind)
     rows = own.shape[0]
-    first, second = pl.ds(0, half), pl.ds(half, rows - half)
-    me = c * 4 + x
+    first, second = pl.ds(0, rows // 2), pl.ds(rows // 2, rows // 2)
+    me, other = c * 4 + x, (1 - c) * 4
     local = pltpu.make_async_copy(own, out.at[me], local_sem)
     local.start()
     greet((partner, up, down))
     send = sender(send_sems, recv_sems)
-    to_up = send(own, out.at[me], 0, up)
-    to_down = send(own, out.at[me], 1, down)
+    to_up = send(own.at[first], out.at[me, first], 0, up)
+    to_down = send(own.at[second], out.at[me, second], 1, down)
     to_partner = send(own, out.at[me], 2, partner)
+    up_rest = send(own.at[second], out.at[me, second], 3, up)
+    down_rest = send(own.at[first], out.at[me, first], 4, down)
     from_down, from_up, from_far = c * 4 + behind, c * 4 + ahead, c * 4 + far
+    local.wait()
+    use(me)
     to_up.wait_recv()
-    pass_up = send(out.at[from_down, first], out.at[from_down, first], 3, up)
-    share_down = send(out.at[from_down], out.at[from_down], 4, partner)
+    pass_up = send(out.at[from_down, first], out.at[from_down, first], 5, up)
     to_down.wait_recv()
-    pass_down = send(out.at[from_up, second], out.at[from_up, second], 5, down)
-    share_up = send(out.at[from_up], out.at[from_up], 6, partner)
+    pass_down = send(out.at[from_up, second], out.at[from_up, second], 6, down)
+    to_partner.wait_recv()
+    use(other + x)
+    up_rest.wait_recv()
+    share_down = send(out.at[from_down], out.at[from_down], 7, partner)
+    down_rest.wait_recv()
+    share_up = send(out.at[from_up], out.at[from_up], 8, partner)
+    use(from_down)
+    use(from_up)
     pass_up.wait_recv()
-    share_first = send(out.at[from_far, first], out.at[from_far, first], 7, partner)
+    share_first = send(out.at[from_far, first], out.at[from_far, first], 9, partner)
     pass_down.wait_recv()
-    share_second = send(out.at[from_far, second], out.at[from_far, second], 8, partner)
-    for copy in (to_partner, share_down, share_up, share_first, share_second):
-        copy.wait_recv()
+    share_second = send(out.at[from_far, second], out.at[from_far, second], 10, partner)
+    use(from_far)
+    share_down.wait_recv()
+    use(other + behind)
+    share_up.wait_recv()
+    use(other + ahead)
+    share_first.wait_recv()
+    share_second.wait_recv()
+    use(other + far)
     for copy in (
         to_up,
         to_down,
         to_partner,
+        up_rest,
+        down_rest,
         pass_up,
+        pass_down,
         share_down,
-        pass_down,
         share_up,
         share_first,
         share_second,
     ):
         copy.wait_send()
-    local.wait()
-
-
-def team_gather(own):
+
+
+def row_block(q):
+    return pl.ds(pl.multiple_of(q * 128, 128), 128)
+
+
+def gather_qkv_kernel(own, weight, bias, out, projected, send_sems, recv_sems, local_sem):
+    def use(q):
+        projected[row_block(q), :] = (dot(out[q], weight[...]) + bias[...]).astype(BF)
+
+    gather_core(own, out, send_sems, recv_sems, local_sem, use)
+
+
+def gather_up_kernel(own, weight, bias, out, upper, activated, send_sems, recv_sems, local_sem):
+    def use(q):
+        values = dot(out[q], weight[...]) + bias[...]
+        upper[row_block(q), :] = values
+        activated[row_block(q), :] = gelu_pair(values)[0].astype(BF)
+
+    gather_core(own, out, send_sems, recv_sems, local_sem, use)
+
+
+def gather_back_kernel(own, weight, upper, out, up_grad, send_sems, recv_sems, local_sem):
+    def use(q):
+        slope = gelu_pair(upper[row_block(q), :])[1]
+        up_grad[row_block(q), :] = (dot_nt(out[q], weight[...]) * slope).astype(BF)
+
+    gather_core(own, out, send_sems, recv_sems, local_sem, use)
+
+
+def team_gather(kernel, collective_id, own, weight, third, results):
     rows, columns = own.shape
     return pl.pallas_call(
-        functools.partial(gather_kernel, rows // 2),
-        out_shape=jax.ShapeDtypeStruct((8, rows, columns), BF),
-        in_specs=[VMEM],
-        out_specs=VMEM,
+        kernel,
+        out_shape=(jax.ShapeDtypeStruct((8, rows, columns), BF),) + results,
+        in_specs=[VMEM] * 3,
+        out_specs=(VMEM,) * (1 + len(results)),
         scratch_shapes=[
-            pltpu.SemaphoreType.DMA((9,)),
-            pltpu.SemaphoreType.DMA((9,)),
+            pltpu.SemaphoreType.DMA((11,)),
+            pltpu.SemaphoreType.DMA((11,)),
             pltpu.SemaphoreType.DMA,
         ],
         compiler_params=pltpu.CompilerParams(
-            collective_id=0, has_side_effects=True, vmem_limit_bytes=LIMIT
+            collective_id=collective_id, has_side_effects=True, vmem_limit_bytes=LIMIT
         ),
-    )(own)
-
-
-def scatter_kernel(
+    )(own, weight, third)
+
+
+def scatter_core(
     half,
-    parts,
+    other_part,
+    mine_part,
+    prepare,
+    beside,
     out,
     from_partner,
     far_sum,
@@ -131,21 +179,20 @@
     c, z, x = place()
     ahead, behind, far = (x + 1) % 4, (x + 3) % 4, (x + 2) % 4
     partner, up, down = at(1 - c, z, x), at(c, z, ahead), at(c, z, behind)
-    rows = parts.shape[1]
+    rows = out.shape[0]
     first, second = pl.ds(0, half), pl.ds(half, rows - half)
-    greet((partner, up, down))
     send = sender(send_sems, recv_sems)
-    other = (1 - c) * 4
-    mine = c * 4
-    swap_far = send(parts.at[other + far], from_partner.at[far], 0, partner)
-    swap_up = send(parts.at[other + ahead], from_partner.at[ahead], 1, partner)
-    swap_down = send(parts.at[other + behind], from_partner.at[behind], 2, partner)
-    swap_own = send(parts.at[other + x], from_partner.at[x], 3, partner)
-
-    def both(place_x, part):
-        return parts[mine + place_x, part, :].astype(F32) + from_partner[
-            place_x, part, :
-        ].astype(F32)
+    greet([partner, up, down] + beside[0])
+    swaps = []
+    for index, where in enumerate((far, ahead, behind, x)):
+        swaps.append(send(other_part(where), from_partner.at[where], index, partner))
+    beside[1]()
+    for where in (far, ahead, behind, x):
+        prepare(where)
+    swap_far, swap_up, swap_down, swap_own = swaps
+
+    def both(where, part):
+        return mine_part(where, part) + from_partner[where, part, :].astype(F32)
 
     swap_far.wait_recv()
     far_sum[first, :] = both(far, first).astype(BF)
@@ -165,7 +212,9 @@
     down_sum[second, :] = (both(behind, second) + far_second[...].astype(F32)).astype(BF)
     down_second = send(down_sum.at[second], got_up.at[second], 9, down)
     swap_own.wait_recv()
-    out[...] = parts[mine + x].astype(F32) + from_partner[x].astype(F32)
+    out[first, :] = both(x, first)
+    out[second, :] = both(x, second)
+    beside[2]()
     up_second.wait_recv()
     up_first.wait_recv()
     down_first.wait_recv()
@@ -184,33 +233,60 @@
         down_second,
     ):
         copy.wait_send()
-
-
-def team_scatter(parts, collective_id):
-    count, rows, columns = parts.shape
-    half = rows // 32 * 16
+    beside[3]()
+
+
+def nothing():
+    pass
+
+
+ALONE = ([], nothing, nothing, nothing)
+
+
+def product_scatter_kernel(product, left, right, out, other, mine, *rest):
+    c, z, x = place()
+
+    def other_part(where):
+        rows = left[row_block((1 - c) * 4 + where), :]
+        other[where] = product(rows, right[...]).astype(BF)
+        return other.at[where]
+
+    def prepare(where):
+        mine[where] = product(left[row_block(c * 4 + where), :], right[...])
+
+    scatter_core(
+        64, other_part, lambda where, part: mine[where, part, :], prepare, ALONE, out, *rest
+    )
+
+
+def scatter_scratch(rows, columns, half):
     block = pltpu.VMEM((rows, columns), BF)
+    return [
+        pltpu.VMEM((4, rows, columns), BF),
+        block,
+        block,
+        block,
+        pltpu.VMEM((half, columns), BF),
+        pltpu.VMEM((rows - half, columns), BF),
+        block,
+        block,
+        pltpu.SemaphoreType.DMA((10,)),
+        pltpu.SemaphoreType.DMA((10,)),
+    ]
+
+
+def product_scatter(product, collective_id, left, right):
     return pl.pallas_call(
-        functools.partial(scatter_kernel, half),
-        out_shape=jax.ShapeDtypeStruct((rows, columns), F32),
-        in_specs=[VMEM],
+        functools.partial(product_scatter_kernel, product),
+        out_shape=jax.ShapeDtypeStruct((128, D), F32),
+        in_specs=[VMEM, VMEM],
         out_specs=VMEM,
-        scratch_shapes=[
-            pltpu.VMEM((4, rows, columns), BF),
-            block,
-            block,
-            block,
-            pltpu.VMEM((half, columns), BF),
-            pltpu.VMEM((rows - half, columns), BF),
-            block,
-            block,
-            pltpu.SemaphoreType.DMA((10,)),
-            pltpu.SemaphoreType.DMA((10,)),
-        ],
+        scratch_shapes=[pltpu.VMEM((4, 128, D), BF), pltpu.VMEM((4, 128, D), F32)]
+        + scatter_scratch(128, D, 64),
         compiler_params=pltpu.CompilerParams(
             collective_id=collective_id, has_side_effects=True, vmem_limit_bytes=LIMIT
         ),
-    )(parts)
+    )(left, right)
 
 
 TEAM_STEPS = tuple((dc, dx) for dc in range(2) for dx in range(4) if dc or dx)
@@ -296,94 +372,890 @@
     )(rows)
 
 
-GROUP_STEPS = tuple(
-    (dc, dz, dx) for dx in (2, 1, 3, 0) for dz in range(2) for dc in range(2) if dc or dz or dx
-)
-
-
-def weights_kernel(blocks, common, out, out_common, send_sems, recv_sems, local_sems):
+def ring_spread(send, base, source, block, me, up, down, first, second):
+    before, after = (me + 3) % 4, (me + 1) % 4
+    copies = [
+        send(source(first), block(me, first), base, up),
+        send(source(second), block(me, second), base + 1, down),
+        send(source(second), block(me, second), base + 2, up),
+        send(source(first), block(me, first), base + 3, down),
+    ]
+
+    def middle():
+        copies[0].wait_recv()
+        copies.append(send(block(before, first), block(before, first), base + 4, up))
+        copies[1].wait_recv()
+        copies.append(send(block(after, second), block(after, second), base + 5, down))
+
+    def last():
+        for copy in copies[2:]:
+            copy.wait_recv()
+
+    return copies, middle, last
+
+
+def weights_kernel(
+    late,
+    common,
+    rows,
+    other_rows,
+    first,
+    second,
+    out_common,
+    out_rows,
+    out_other,
+    send_sems,
+    recv_sems,
+    common_send,
+    common_recv,
+    share_send,
+    share_recv,
+    ring_send,
+    ring_recv,
+    swap_send,
+    swap_recv,
+    local_sems,
+):
     c, z, x = place()
-    slot = (c, z * 4 + x)
-    spots = [((c + dc) % 2, (z + dz) % 2, (x + dx) % 4) for dc, dz, dx in GROUP_STEPS]
-    locals_ = [
-        pltpu.make_async_copy(blocks.at[c * 4 + x], out.at[slot], local_sems.at[0]),
-        pltpu.make_async_copy(common, out_common.at[slot], local_sems.at[1]),
-    ]
-    for copy in locals_:
+    r = lax.axis_index("replica")
+    y, zh = r // 2, r % 2
+    zf = zh * 2 + z
+    slot = z * 4 + x
+
+    def device(ty, tz):
+        return {"section": c, "shard": (tz % 2) * 4 + x, "replica": ty * 2 + tz // 2}
+
+    y_up, y_down = device((y + 1) % 4, zf), device((y + 3) % 4, zf)
+    z_up, z_down = device(y, (zf + 1) % 4), device(y, (zf + 3) % 4)
+    z_other = device(y, (zf + 3 + 2 * z) % 4)
+    partner, diagonal, z_pair = at(1 - c, z, x), at(1 - c, 1 - z, x), at(c, 1 - z, x)
+    team = [((c + dc) % 2, (x + dx) % 4) for dc, dx in TEAM_STEPS]
+    core_steps = [(dz, dx) for dx in (1, 3, 2, 0) for dz in range(2) if dz or dx]
+    core = [((z + dz) % 2, (x + dx) % 4) for dz, dx in core_steps]
+    source_of = [core_steps.index((dz, (4 - dx) % 4)) for dz, dx in core_steps]
+    greet(
+        [at(tc, z, tx) for tc, tx in team]
+        + [at(c, 1 - z, (x + dx) % 4) for dx in range(4)]
+        + [diagonal, y_up, y_down, z_other]
+    )
+
+    def remote(src, dst, sends, recvs, index, target):
+        return pltpu.make_async_remote_copy(
+            src_ref=src,
+            dst_ref=dst,
+            send_sem=sends.at[index],
+            recv_sem=recvs.at[index],
+            device_id=target,
+            device_id_type=MESH,
+        )
+
+    def to_team(index, layer):
+        tc, tx = team[index]
+        place_at = first.at[y, zf, x] if layer == 0 else second.at[slot]
+        return remote(late.at[tc * 4 + tx], place_at, send_sems, recv_sems, index, at(tc, z, tx))
+
+    def swapped(index):
+        src, dst = ((rows, out_rows), (other_rows, out_other))[index]
+        return remote(src.at[c], dst, swap_send, swap_recv, index, diagonal)
+
+    def kept(index):
+        src, dst = ((rows, out_rows), (other_rows, out_other))[index]
+        return pltpu.make_async_copy(src.at[c], dst, local_sems.at[2 + index])
+
+    def common_to(index):
+        tz, tx = core[index]
+        return remote(
+            common, out_common.at[c, slot], common_send, common_recv, index, at(c, tz, tx)
+        )
+
+    def shared(index):
+        if index == 7:
+            source = out_common.at[c, slot]
+        else:
+            tz, tx = core[index]
+            source = out_common.at[c, tz * 4 + tx]
+        return remote(source, source, share_send, share_recv, index, partner)
+
+    keep = pltpu.make_async_copy(common, out_common.at[c, slot], local_sems.at[0])
+    keep.start()
+
+    @pl.when(c == 0)
+    def _():
+        for index in range(7):
+            to_team(index, 0).start()
+        pltpu.make_async_copy(late.at[c * 4 + x], first.at[y, zf, x], local_sems.at[1]).start()
+
+    @pl.when(c == 1)
+    def _():
+        for index in range(7):
+            to_team(index, 1).start()
+        pltpu.make_async_copy(late.at[c * 4 + x], second.at[slot], local_sems.at[1]).start()
+
+    for index in range(7):
+        common_to(index).start()
+
+    @pl.when(c == z)
+    def _():
+        kept(0).start()
+        kept(1).start()
+
+    @pl.when(c != z)
+    def _():
+        swapped(0).start()
+        swapped(1).start()
+
+    for index, (dc, dx) in enumerate(TEAM_STEPS):
+
+        @pl.when((c + dc) % 2 == 0)
+        def _():
+            to_team(index, 0).wait_recv()
+
+        @pl.when((c + dc) % 2 == 1)
+        def _():
+            to_team(index, 1).wait_recv()
+
+    @pl.when(c == 0)
+    def _():
+        pltpu.make_async_copy(late.at[c * 4 + x], first.at[y, zf, x], local_sems.at[1]).wait()
+
+    @pl.when(c == 1)
+    def _():
+        pltpu.make_async_copy(late.at[c * 4 + x], second.at[slot], local_sems.at[1]).wait()
+
+    def send(src, dst, index, target):
+        copy = remote(src, dst, ring_send, ring_recv, index, target)
         copy.start()
-    greet([at(*spot) for spot in spots])
-    send = sender(send_sems, recv_sems)
-    copies = []
-    for index, (tc, tz, tx) in enumerate(spots):
-        device = at(tc, tz, tx)
-        copies.append(send(blocks.at[tc * 4 + tx], out.at[slot], 2 * index, device))
-        copies.append(send(common, out_common.at[slot], 2 * index + 1, device))
-    for copy in copies:
-        copy.wait_recv()
-    for copy in copies:
+        return copy
+
+    one, two = pl.ds(0, 1), pl.ds(1, 1)
+    three, four = pl.ds(2, 1), pl.ds(3, 1)
+    left, right = pl.ds(0, 2), pl.ds(2, 2)
+    y_copies, y_middle, y_last = ring_spread(
+        send,
+        0,
+        lambda part: first.at[y, zf, part],
+        lambda i, part: first.at[i, zf, part],
+        y,
+        y_up,
+        y_down,
+        one,
+        two,
+    )
+    z_copies, z_middle, z_last = ring_spread(
+        send,
+        6,
+        lambda part: first.at[y, zf, part],
+        lambda i, part: first.at[y, i, part],
+        zf,
+        z_up,
+        z_down,
+        three,
+        four,
+    )
+    pair_copy = send(second.at[pl.ds(z * 4, 4)], second.at[pl.ds(z * 4, 4)], 24, z_pair)
+    keep.wait()
+    shared(7).start()
+    for index in range(7):
+        common_to(source_of[index]).wait_recv()
+        shared(index).start()
+    y_middle()
+    z_middle()
+    y_last()
+    more_z, z_middle_too, z_last_too = ring_spread(
+        send,
+        12,
+        lambda part: first.at[part, zf, pl.ds(0, 2)],
+        lambda i, part: first.at[part, i, pl.ds(0, 2)],
+        zf,
+        z_up,
+        z_down,
+        left,
+        right,
+    )
+    z_last()
+    more_y, y_middle_too, y_last_too = ring_spread(
+        send,
+        18,
+        lambda part: first.at[y, part, pl.ds(2, 2)],
+        lambda i, part: first.at[i, part, pl.ds(2, 2)],
+        y,
+        y_up,
+        y_down,
+        left,
+        right,
+    )
+    z_middle_too()
+    y_middle_too()
+    pair_copy.wait_recv()
+    for index in range(8):
+        shared(index).wait_recv()
+    z_last_too()
+    y_last_too()
+
+    @pl.when(c == z)
+    def _():
+        kept(0).wait()
+        kept(1).wait()
+
+    @pl.when(c != z)
+    def _():
+        for index in range(2):
+            swapped(index).wait_recv()
+            swapped(index).wait_send()
+
+    @pl.when(c == 0)
+    def _():
+        for index in range(7):
+            to_team(index, 0).wait_send()
+
+    @pl.when(c == 1)
+    def _():
+        for index in range(7):
+            to_team(index, 1).wait_send()
+
+    for index in range(7):
+        common_to(index).wait_send()
+    for index in range(8):
+        shared(index).wait_send()
+    for copy in y_copies + z_copies + more_z + more_y + [pair_copy]:
         copy.wait_send()
-    for copy in locals_:
-        copy.wait()
-
-
-def spread_weights(blocks, common):
+
+
+def spread_weights(late, common, rows, other_rows):
+    dma = pltpu.SemaphoreType.DMA
     return pl.pallas_call(
         weights_kernel,
         out_shape=(
-            jax.ShapeDtypeStruct((2,) + blocks.shape, BF),
+            jax.ShapeDtypeStruct((4, 4, 4, 144, 128), BF),
+            jax.ShapeDtypeStruct(late.shape, BF),
             jax.ShapeDtypeStruct((2, 8) + common.shape, BF),
+            jax.ShapeDtypeStruct(rows.shape[1:], BF),
+            jax.ShapeDtypeStruct(rows.shape[1:], BF),
         ),
-        in_specs=[VMEM, VMEM],
-        out_specs=(VMEM, VMEM),
+        in_specs=[VMEM] * 4,
+        out_specs=(VMEM,) * 5,
         scratch_shapes=[
-            pltpu.SemaphoreType.DMA((30,)),
-            pltpu.SemaphoreType.DMA((30,)),
-            pltpu.SemaphoreType.DMA((2,)),
+            dma((7,)),
+            dma((7,)),
+            dma((7,)),
+            dma((7,)),
+            dma((8,)),
+            dma((8,)),
+            dma((25,)),
+            dma((25,)),
+            dma((2,)),
+            dma((2,)),
+            dma((4,)),
         ],
         compiler_params=pltpu.CompilerParams(
             collective_id=3, has_side_effects=True, vmem_limit_bytes=LIMIT
         ),
-    )(blocks, common)
-
-
-def grads_kernel(blocks, out, got, send_sems, recv_sems, local_sem):
+    )(late, common, rows, other_rows)
+
+
+SPLIT_ROWS = 4 * 144
+DOWN_ROWS = 320
+SHARED_ROWS = 96
+ROWS = SPLIT_ROWS + DOWN_ROWS + SHARED_ROWS
+OWN_ROWS = DOWN_ROWS + SHARED_ROWS
+GOT_ROWS = 8 * 144 + 2 * OWN_ROWS
+
+
+def widen(block):
+    return block.astype(F32)
+
+
+def ring_reduce(send, base, block, me, up, down, first, second, far, relay, got, result):
+    after, before, opposite = (me + 1) % 4, (me + 3) % 4, (me + 2) % 4
+    copies = [
+        send(block(opposite, first), far[0], base, up),
+        send(block(opposite, second), far[1], base + 1, down),
+        send(block(after, second), got[0].at[second], base + 2, up),
+        send(block(before, first), got[1].at[first], base + 3, down),
+    ]
+
+    def middle():
+        copies[0].wait_recv()
+        relay[0][...] = (widen(block(after, first)[...]) + widen(far[0][...])).astype(BF)
+        copies.append(send(relay[0], got[0].at[first], base + 4, up))
+        copies[1].wait_recv()
+        relay[1][...] = (widen(block(before, second)[...]) + widen(far[1][...])).astype(BF)
+        copies.append(send(relay[1], got[1].at[second], base + 5, down))
+
+    def last():
+        for copy in copies[2:]:
+            copy.wait_recv()
+        for part in (first, second):
+            value = (
+                widen(block(me, part)[...])
+                + widen(got[0].at[part][...])
+                + widen(got[1].at[part][...])
+            )
+            result.at[part][...] = value.astype(BF)
+        for copy in copies:
+            copy.wait_send()
+
+    return middle, last
+
+
+TOP = ROWS // 2
+CUT = TOP // 32 * 16
+
+
+def rings_scratch():
+    dma = pltpu.SemaphoreType.DMA
+    return [
+        pltpu.VMEM((2, 4, TOP, 128), BF),
+        pltpu.VMEM((2, 2, 2, TOP, 128), BF),
+        pltpu.VMEM((2, 2, 2, TOP, 128), BF),
+        pltpu.VMEM((2, 2, 4, TOP, 128), BF),
+        pltpu.VMEM((2, 2, TOP - CUT, 128), BF),
+        pltpu.VMEM((2, 2, TOP - CUT, 128), BF),
+        pltpu.VMEM((2, 2, TOP, 128), BF),
+        dma((24,)),
+        dma((24,)),
+    ]
+
+
+def grid_place():
     c, z, x = place()
-    spots = [((c + dc) % 2, (z + dz) % 2, (x + dx) % 4) for dc, dz, dx in GROUP_STEPS]
-    slot = (z, c * 4 + x)
-    local = pltpu.make_async_copy(blocks.at[c, z * 4 + x], got.at[slot], local_sem)
-    local.start()
-    greet([at(*spot) for spot in spots])
-    send = sender(send_sems, recv_sems)
-    copies = [
-        send(blocks.at[tc, tz * 4 + tx], got.at[slot], index, at(tc, tz, tx))
-        for index, (tc, tz, tx) in enumerate(spots)
-    ]
+    r = lax.axis_index("replica")
+    y, zh = r // 2, r % 2
+    zf = zh * 2 + z
+
+    def device(ty, tz):
+        return {"section": c, "shard": (tz % 2) * 4 + x, "replica": ty * 2 + tz // 2}
+
+    return (
+        y,
+        zf,
+        (
+            device((y + 1) % 4, zf),
+            device((y + 3) % 4, zf),
+            device(y, (zf + 1) % 4),
+            device(y, (zf + 3) % 4),
+        ),
+    )
+
+
+def layer_rings(pieces, out, wide_sum, far, relay, got, far_s, relay_s, got_s, sends, recvs):
+    y, zf, (y_up, y_down, z_up, z_down) = grid_place()
+
+    def send(src, dst, index, target):
+        copy = pltpu.make_async_remote_copy(
+            src_ref=src,
+            dst_ref=dst,
+            send_sem=sends.at[index],
+            recv_sem=recvs.at[index],
+            device_id=target,
+            device_id_type=MESH,
+        )
+        copy.start()
+        return copy
+
+    low, high = pl.ds(0, 2), pl.ds(2, 2)
+    top, bottom = pl.ds(0, TOP), pl.ds(TOP, TOP)
+    first, second = pl.ds(0, CUT), pl.ds(CUT, TOP - CUT)
+
+    def wide(k):
+        return (
+            [far.at[k, 0], far.at[k, 1]],
+            [relay.at[k, 0], relay.at[k, 1]],
+            [got.at[k, 0], got.at[k, 1]],
+            wide_sum.at[k],
+        )
+
+    def small(k, result):
+        parts = pl.ds(0, CUT), pl.ds(0, TOP - CUT)
+        return (
+            [far_s.at[k, 0, parts[0]], far_s.at[k, 1, parts[1]]],
+            [relay_s.at[k, 0, parts[0]], relay_s.at[k, 1, parts[1]]],
+            [got_s.at[k, 0], got_s.at[k, 1]],
+            result,
+        )
+
+    y_mid, y_last = ring_reduce(
+        send,
+        0,
+        lambda i, part: pieces.at[i, part, top],
+        y,
+        y_up,
+        y_down,
+        low,
+        high,
+        *wide(0),
+    )
+    z_mid, z_last = ring_reduce(
+        send,
+        6,
+        lambda i, part: pieces.at[part, i, bottom],
+        zf,
+        z_up,
+        z_down,
+        low,
+        high,
+        *wide(1),
+    )
+    later = []
+
+    def turn():
+        y_last()
+        later.append(
+            ring_reduce(
+                send,
+                12,
+                lambda i, part: wide_sum.at[0, i, part],
+                zf,
+                z_up,
+                z_down,
+                first,
+                second,
+                *small(0, out.at[top]),
+            )
+        )
+        z_last()
+        later.append(
+            ring_reduce(
+                send,
+                18,
+                lambda i, part: wide_sum.at[1, i, part],
+                y,
+                y_up,
+                y_down,
+                first,
+                second,
+                *small(1, out.at[bottom]),
+            )
+        )
+
+    def middle():
+        y_mid()
+        z_mid()
+
+    def finish():
+        for mid, _ in later:
+            mid()
+        for _, last in later:
+            last()
+
+    return middle, turn, finish
+
+
+def reduce_kernel(
+    pieces,
+    second_layer,
+    out,
+    summed,
+    own,
+    home_send,
+    home_recv,
+    local_sems,
+    spread_send,
+    spread_recv,
+    *scratch,
+):
+    c, z, x = place()
+    r = lax.axis_index("replica")
+    y, zh = r // 2, r % 2
+    zf, (y_up, y_down, z_up, z_down) = grid_place()[1:]
+    across = {"section": c, "shard": z * 4 + x, "replica": y * 2 + 1 - zh}
+    team = [at((c + dc) % 2, z, (x + dx) % 4) for dc, dx in TEAM_STEPS]
+    greet([y_up, y_down, z_up, z_down, across, at(1 - c, 1 - z, x)] + team)
+
+    def remote(src, dst, sends, recvs, index, target):
+        copy = pltpu.make_async_remote_copy(
+            src_ref=src,
+            dst_ref=dst,
+            send_sem=sends.at[index],
+            recv_sem=recvs.at[index],
+            device_id=target,
+            device_id_type=MESH,
+        )
+        copy.start()
+        return copy
+
+    middle, turn, finish = layer_rings(pieces, summed.at[0], *scratch)
+    summed[1] = second_layer[...]
+    middle()
+    turn()
+    finish()
+
+    me = c * 4 + x
+    mine = pl.ds(pl.multiple_of(me * 144, 16), 144)
+    own_part = pl.ds(SPLIT_ROWS, OWN_ROWS)
+
+    def home_part(t):
+        return own.at[pl.ds(pl.multiple_of(8 * 144 + t * OWN_ROWS, 16), OWN_ROWS)]
+
+    def split_part(tc, tx):
+        return summed.at[tc, pl.ds(pl.multiple_of(tx * 144, 16), 144)]
+
+    keep = pltpu.make_async_copy(split_part(c, x), own.at[mine], local_sems.at[0])
+    keep.start()
+    copies = []
+    for index, (dc, dx) in enumerate(TEAM_STEPS):
+        tc, tx = (c + dc) % 2, (x + dx) % 4
+        copies.append(
+            remote(split_part(tc, tx), own.at[mine], home_send, home_recv, index, at(tc, z, tx))
+        )
+
+    def same_layer():
+        return pltpu.make_async_remote_copy(
+            src_ref=summed.at[c, own_part],
+            dst_ref=home_part(z),
+            send_sem=home_send.at[7],
+            recv_sem=home_recv.at[7],
+            device_id=at(c, 1 - z, x),
+            device_id_type=MESH,
+        )
+
+    def same_here():
+        return pltpu.make_async_copy(summed.at[c, own_part], home_part(z), local_sems.at[1])
+
+    def other_layer(t):
+        return pltpu.make_async_remote_copy(
+            src_ref=summed.at[1 - c, own_part],
+            dst_ref=home_part(z),
+            send_sem=home_send.at[8],
+            recv_sem=home_recv.at[8 + t],
+            device_id=at(1 - c, c, x),
+            device_id_type=MESH,
+        )
+
+    @pl.when(z == c)
+    def _():
+        same_here().start()
+
+    @pl.when(z != c)
+    def _():
+        same_layer().start()
+
+    other_layer(z).start()
     for copy in copies:
         copy.wait_recv()
-    local.wait()
-    for q in range(8):
-        out[q] = (got[0, q].astype(F32) + got[1, q].astype(F32)).astype(BF)
+
+    @pl.when(z == c)
+    def _():
+        same_here().wait()
+        same_layer().wait_recv()
+
+    @pl.when(z != c)
+    def _():
+        other_layer(0).wait_recv()
+        other_layer(1).wait_recv()
+        same_layer().wait_send()
+
+    other_layer(z).wait_send()
     for copy in copies:
         copy.wait_send()
-
-
-def collect_grads(blocks):
-    shape = blocks.shape[1:]
+    keep.wait()
+
+    here = y * 2 + zh
+    front, back = pl.ds(0, GOT_ROWS // 2), pl.ds(GOT_ROWS // 2, GOT_ROWS // 2)
+    local = pltpu.make_async_copy(own, out.at[here], local_sems.at[2])
+    local.start()
+
+    def send(src, dst, index, target):
+        return remote(src, dst, spread_send, spread_recv, index, target)
+
+    over = send(own, out.at[here], 0, across)
+
+    def spread(base, source, block):
+        return [
+            send(source.at[front], out.at[block, front], base, y_up),
+            send(source.at[back], out.at[block, back], base + 1, y_down),
+            send(source.at[back], out.at[block, back], base + 2, y_up),
+            send(source.at[front], out.at[block, front], base + 3, y_down),
+        ]
+
+    def forward(base, which, sent):
+        below, above = ((y + 3) % 4) * 2 + which, ((y + 1) % 4) * 2 + which
+        sent[0].wait_recv()
+        sent.append(send(out.at[below, front], out.at[below, front], base + 4, y_up))
+        sent[1].wait_recv()
+        sent.append(send(out.at[above, back], out.at[above, back], base + 5, y_down))
+
+    sent = spread(1, own, here)
+    forward(1, zh, sent)
+    over.wait_recv()
+    there = y * 2 + 1 - zh
+    more = spread(7, out.at[there], there)
+    forward(7, 1 - zh, more)
+    for copy in sent[2:] + more[2:]:
+        copy.wait_recv()
+    for copy in [over] + sent + more:
+        copy.wait_send()
+    local.wait()
+
+
+def reduce_grads(pieces, second_layer):
+    dma = pltpu.SemaphoreType.DMA
     return pl.pallas_call(
-        grads_kernel,
-        out_shape=jax.ShapeDtypeStruct(shape, BF),
-        in_specs=[VMEM],
+        reduce_kernel,
+        out_shape=jax.ShapeDtypeStruct((8, GOT_ROWS, 128), BF),
+        in_specs=[VMEM, VMEM],
         out_specs=VMEM,
         scratch_shapes=[
-            pltpu.VMEM((2,) + shape, BF),
-            pltpu.SemaphoreType.DMA((15,)),
-            pltpu.SemaphoreType.DMA((15,)),
-            pltpu.SemaphoreType.DMA,
-        ],
+            pltpu.VMEM((2, ROWS, 128), BF),
+            pltpu.VMEM((GOT_ROWS, 128), BF),
+            dma((9,)),
+            dma((10,)),
+            dma((3,)),
+            dma((13,)),
+            dma((13,)),
+        ]
+        + rings_scratch(),
         compiler_params=pltpu.CompilerParams(
             collective_id=4, has_side_effects=True, vmem_limit_bytes=LIMIT
         ),
-    )(blocks)
+    )(pieces, second_layer)
+
+
+def shared_kernel(rings, *refs):
+    if rings:
+        pieces, *refs = refs
+    attended, middle_low, normed_all, qkv_grad, normed, last_grad, vectors, rows = refs[:8]
+    refs = refs[8:]
+    if rings:
+        out, out_rows, out_pieces, *refs = refs
+    else:
+        out, out_rows, *refs = refs
+    products, last_keys, last_queries, parts, home_send, home_recv, home_local, *refs = refs
+    scatter_refs, ring_refs = refs[:10], refs[10:]
+    c, z, x = place()
+    products[...] = dot_tn(attended[...], middle_low[...])
+    last_keys[...] = dot_tn(normed_all[...], qkv_grad[:, 384:512])
+    last_queries[...] = dot_tn(normed[...], last_grad[...])
+    for j in range(8):
+        block = pl.ds(136 * j, 136)
+
+        def stack(value, lanes):
+            tail = vectors[j, :, lanes]
+            return jnp.concatenate([value, tail], axis=0).astype(BF)
+
+        if j < 7:
+            product = products[block, :]
+        else:
+            product = jnp.concatenate(
+                [products[952:1024, :], products[1088:1152, :]], axis=0
+            )
+        parts[j, :, 0:128] = stack(last_keys[block, :], pl.ds(0, 128))
+        parts[j, :, 128:1152] = stack(product[:, 0:1024], pl.ds(128, 1024))
+        parts[j, :, 1152:1280] = stack(
+            product[:, 1024:1152] + last_queries[block, :], pl.ds(1152, 128)
+        )
+
+    def same_layer():
+        return pltpu.make_async_remote_copy(
+            src_ref=rows.at[c],
+            dst_ref=out_rows.at[z],
+            send_sem=home_send.at[0],
+            recv_sem=home_recv.at[0],
+            device_id=at(c, 1 - z, x),
+            device_id_type=MESH,
+        )
+
+    def same_here():
+        return pltpu.make_async_copy(rows.at[c], out_rows.at[z], home_local)
+
+    def other_layer(t):
+        return pltpu.make_async_remote_copy(
+            src_ref=rows.at[1 - c],
+            dst_ref=out_rows.at[z],
+            send_sem=home_send.at[1],
+            recv_sem=home_recv.at[1 + t],
+            device_id=at(1 - c, c, x),
+            device_id_type=MESH,
+        )
+
+    stages = []
+
+    def begin():
+        if rings:
+            stages.extend(layer_rings(pieces, out_pieces, *ring_refs))
+
+        @pl.when(z == c)
+        def _():
+            same_here().start()
+
+        @pl.when(z != c)
+        def _():
+            same_layer().start()
+
+        other_layer(z).start()
+
+    def during():
+        if rings:
+            stages[0]()
+            stages[1]()
+
+    def end():
+        if rings:
+            stages[2]()
+
+        @pl.when(z == c)
+        def _():
+            same_here().wait()
+            same_layer().wait_recv()
+
+        @pl.when(z != c)
+        def _():
+            other_layer(0).wait_recv()
+            other_layer(1).wait_recv()
+            same_layer().wait_send()
+
+        other_layer(z).wait_send()
+
+    friends = [at(c, 1 - z, x), at(1 - c, 1 - z, x)]
+    if rings:
+        y, zf, (y_up, y_down, z_up, z_down) = grid_place()
+        z_other = {
+            "section": c,
+            "shard": (1 - z) * 4 + x,
+            "replica": y * 2 + ((zf + 3 + 2 * z) % 4) // 2,
+        }
+        friends += [y_up, y_down, z_other]
+
+    def mine_part(where, part):
+        return parts[c * 4 + where, part, :].astype(F32)
+
+    scatter_core(
+        64,
+        lambda where: parts.at[(1 - c) * 4 + where],
+        mine_part,
+        lambda where: None,
+        (friends, begin, during, end),
+        out,
+        *scatter_refs,
+    )
+
+
+def shared_scatter(operands, pieces):
+    rings = pieces is not None
+    dma = pltpu.SemaphoreType.DMA
+    out_shape = (
+        jax.ShapeDtypeStruct((144, 1280), F32),
+        jax.ShapeDtypeStruct((2, 128, D), BF),
+    )
+    if rings:
+        operands = (pieces,) + operands
+        out_shape += (jax.ShapeDtypeStruct((ROWS, 128), BF),)
+    return pl.pallas_call(
+        functools.partial(shared_kernel, rings),
+        out_shape=out_shape,
+        in_specs=[VMEM] * len(operands),
+        out_specs=(VMEM,) * len(out_shape),
+        scratch_shapes=[
+            pltpu.VMEM((1152, 1152), F32),
+            pltpu.VMEM((D, 128), F32),
+            pltpu.VMEM((D, 128), F32),
+            pltpu.VMEM((8, 144, 1280), BF),
+            dma((2,)),
+            dma((3,)),
+            dma,
+        ]
+        + scatter_scratch(144, 1280, 64)
+        + (rings_scratch() if rings else []),
+        compiler_params=pltpu.CompilerParams(
+            collective_id=11 if rings else 6, has_side_effects=True, vmem_limit_bytes=LIMIT
+        ),
+    )(*operands)
+
+
+def segments(start, size, piece_rows):
+    done = 0
+    while done < size:
+        piece, row = divmod(start + done, piece_rows)
+        count = min(piece_rows - row, size - done)
+        yield piece, row, done, count
+        done += count
+
+
+def pieces_kernel(
+    normed_all, qkv_grad, second_all, up_grad, activated, low_all, shared, out, wide, tall
+):
+    wide[:, 896:1024] = jnp.zeros((D, 128), F32)
+    wide[:, 0:384] = dot_tn(normed_all[...], qkv_grad[:, 0:384])
+    wide[:, 384:928] = dot_tn(second_all[...], up_grad[...])
+    blank = jnp.zeros((8, 128), F32)
+    for chunk in range(8):
+        for j in range(8):
+            block = wide[136 * j : 136 * j + 136, 128 * chunk : 128 * chunk + 128]
+            place_at = pl.ds((j % 4) * 144, 144)
+            out[chunk // 2, (chunk % 2) * 2 + j // 4, place_at, :] = jnp.concatenate(
+                [block, blank], axis=0
+            ).astype(BF)
+    tall[:, 1024:1152] = jnp.zeros((544, 128), F32)
+    tall[:, 0:D] = dot_tn(activated[...], low_all[...])
+
+    def put(base, piece_rows, start, value):
+        for piece, row, at_row, count in segments(start, value.shape[0], piece_rows):
+            out[piece // 4, piece % 4, base + row : base + row + count, :] = value[
+                at_row : at_row + count
+            ].astype(BF)
+
+    for k in range(9):
+        put(SPLIT_ROWS, DOWN_ROWS, 544 * k, tall[:, 128 * k : 128 * k + 128])
+    put(SPLIT_ROWS, DOWN_ROWS, 9 * 544, jnp.zeros((16 * DOWN_ROWS - 9 * 544, 128), F32))
+    base = SPLIT_ROWS + DOWN_ROWS
+    for k in range(10):
+        put(base, SHARED_ROWS, 144 * k, shared[:, 128 * k : 128 * k + 128])
+    put(base, SHARED_ROWS, 1440, jnp.zeros((16 * SHARED_ROWS - 1440, 128), F32))
+
+
+def grad_pieces(*operands):
+    return pl.pallas_call(
+        pieces_kernel,
+        out_shape=jax.ShapeDtypeStruct((4, 4, ROWS, 128), BF),
+        in_specs=[VMEM] * 7,
+        out_specs=VMEM,
+        scratch_shapes=[pltpu.VMEM((D, 1024), F32), pltpu.VMEM((544, 1152), F32)],
+        compiler_params=pltpu.CompilerParams(vmem_limit_bytes=LIMIT),
+    )(*operands)
+
+
+def assemble_kernel(got, qkv, out_w, up, down, vectors, shared):
+    for q in range(8):
+        for chunk in range(8):
+            block = got[chunk, 144 * q : 144 * q + 144, :].astype(F32)[:136]
+            if chunk < 3:
+                start = chunk * D + 128 * q
+                qkv[:, start : start + 128] = block
+            elif chunk < 7:
+                start = 544 * q + 128 * (chunk - 3)
+                up[:, start : start + 128] = block
+            else:
+                up[:, 544 * q + 512 : 544 * q + 544] = block[:, :32]
+    for k in range(9):
+        width = 128 if k < 8 else 64
+        for piece, row, at_row, count in segments(544 * k, 544, DOWN_ROWS):
+            start = 8 * 144 + (piece % 2) * OWN_ROWS + row
+            block = got[piece // 2, start : start + count, :].astype(F32)
+            down[at_row : at_row + count, 128 * k : 128 * k + width] = block[:, :width]
+    for k in range(10):
+        for piece, row, at_row, count in segments(144 * k, 144, SHARED_ROWS):
+            start = 8 * 144 + (piece % 2) * OWN_ROWS + DOWN_ROWS + row
+            block = got[piece // 2, start : start + count, :].astype(F32)
+            shared[k, at_row : at_row + count, :] = block
+        vectors[:, 128 * k : 128 * k + 128] = shared[k, 136:144, :]
+        if 1 <= k < 9:
+            out_w[:, 128 * (k - 1) : 128 * k] = shared[k, 0:136, :]
+    out_w[:, 1024:D] = shared[9, 0:136, 0:64]
+    qkv[:, 1024:D] = shared[9, 0:136, 64:128]
+    qkv[:, D + 1024 : 2 * D] = shared[0, 0:136, 0:64]
+    qkv[:, 2 * D + 1024 : 3 * D] = shared[0, 0:136, 64:128]
+
+
+def assemble(got):
+    shapes = ((136, 3 * D), (136, D), (136, FF), (544, D), (8, 1280))
+    return pl.pallas_call(
+        assemble_kernel,
+        out_shape=tuple(jax.ShapeDtypeStruct(shape, F32) for shape in shapes),
+        in_specs=[VMEM],
+        out_specs=(VMEM,) * 5,
+        scratch_shapes=[pltpu.VMEM((10, 144, 128), F32)],
+        compiler_params=pltpu.CompilerParams(vmem_limit_bytes=LIMIT),
+    )(got)
 
 
 def dot_nt(left, right):
@@ -524,18 +1396,30 @@
 def layer_forward(hidden, w):
     normed, unit_one, inverse_one = norm_forward(hidden, w["gain_one"], w["bias_one"])
     normed = normed.astype(BF)
-    normed_all = team_gather(normed).reshape(1024, D)
-    projected = (dot(normed_all, w["qkv"]) + w["qkv_bias"]).astype(BF)
+    normed_all, projected = team_gather(
+        gather_qkv_kernel,
+        0,
+        normed,
+        w["qkv"],
+        w["qkv_bias"].reshape(1, 512),
+        (jax.ShapeDtypeStruct((1024, 512), BF),),
+    )
+    normed_all = normed_all.reshape(1024, D)
     last_query = (dot(normed, w["last_query"]) + w["last_bias"]).astype(BF)
     heads, last = attend(projected, last_query)
     attended = heads_to_rows(heads.reshape(8, 128, 128), last)
     middle = hidden + dot(attended, w["out"]) + w["out_bias"]
     second, unit_two, inverse_two = norm_forward(middle, w["gain_two"], w["bias_two"])
-    second_all = team_gather(second.astype(BF)).reshape(1024, D)
-    upper = dot(second_all, w["up"]) + w["up_bias"]
-    activated = gelu_pair(upper)[0].astype(BF)
-    parts = dot(activated, w["down"]).astype(BF).reshape(8, 128, D)
-    output = middle + team_scatter(parts, 5) + w["down_bias"]
+    second_all, upper, activated = team_gather(
+        gather_up_kernel,
+        7,
+        second.astype(BF),
+        w["up"],
+        w["up_bias"].reshape(1, 544),
+        (jax.ShapeDtypeStruct((1024, 544), F32), jax.ShapeDtypeStruct((1024, 544), BF)),
+    )
+    second_all = second_all.reshape(1024, D)
+    output = middle + product_scatter(dot, 5, activated, w["down"]) + w["down_bias"]
     saved = dict(
         normed=normed,
         normed_all=normed_all,
@@ -553,13 +1437,22 @@
     return output, saved
 
 
-def layer_backward(grad_out, w, kept, q):
+def layer_backward(grad_out, grad_low_all, w, kept, q):
     grad_low = grad_out.astype(BF)
-    grad_low_all = team_gather(grad_low).reshape(1024, D)
-    slope = gelu_pair(kept["upper"])[1]
-    up_grad = (dot_nt(grad_low_all, w["down"]) * slope).astype(BF)
-    parts = dot_nt(up_grad, w["up"]).astype(BF).reshape(8, 128, D)
-    grad_second = team_scatter(parts, 5)
+    if grad_low_all is None:
+        grad_low_all, up_grad = team_gather(
+            gather_back_kernel,
+            8,
+            grad_low,
+            w["down"],
+            kept["upper"],
+            (jax.ShapeDtypeStruct((1024, 544), BF),),
+        )
+        grad_low_all = grad_low_all.reshape(1024, D)
+    else:
+        slope = gelu_pair(kept["upper"])[1]
+        up_grad = (dot_nt(grad_low_all, w["down"]) * slope).astype(BF)
+    grad_second = product_scatter(dot_nt, 9, up_grad, w["up"])
     grad_in, gain_two, bias_two = norm_backward(
         grad_second, kept["unit_two"], kept["inverse_two"], w["gain_two"]
     )
@@ -570,23 +1463,12 @@
     qkv_grad, last_grad = attend_back(
         kept["projected"], kept["last_query"], heads_grad, attended_grad[:, 1024:]
     )
-    parts = dot_nt(qkv_grad, w["qkv"]).astype(BF).reshape(8, 128, D)
-    grad_normed = team_scatter(parts, 5) + dot_nt(last_grad, w["last_query"])
+    grad_normed = product_scatter(dot_nt, 10, qkv_grad, w["qkv"])
+    grad_normed = grad_normed + dot_nt(last_grad, w["last_query"])
     grad_in, gain_one, bias_one = norm_backward(
         grad_normed, kept["unit_one"], kept["inverse_one"], w["gain_one"]
     )
     grad_input = grad_middle + grad_in
-
-    grad_qkv = dot_tn(kept["normed_all"], qkv_grad)
-    grad_last_query = dot_tn(kept["normed"], last_grad)
-    grad_up = dot_tn(kept["second_all"], up_grad)
-    grad_down = dot_tn(kept["activated"], grad_low_all)
-    grad_out_w = dot_tn(kept["attended"], middle_low)
-    split = jnp.concatenate([grad_qkv[:, :384], grad_up], axis=1).astype(BF).reshape(8, 136, 928)
-    out_rows = jnp.concatenate([grad_out_w[:1024], grad_out_w[1088:]], axis=0)
-    shared = jnp.concatenate(
-        [out_rows, grad_qkv[:, 384:512], grad_last_query[:, :64]], axis=1
-    ).reshape(8, 136, 1280)
 
     qkv_sums = jnp.sum(qkv_grad, axis=0, dtype=F32)
     last_sums = jnp.sum(last_grad, axis=0, dtype=F32)
@@ -616,9 +1498,25 @@
         axis=1,
     )
     vectors = jnp.pad(vectors, ((0, 0), (0, 8 * 1280 - 1632))).reshape(8, 8, 1280)
-    shared = jnp.concatenate([shared, vectors], axis=1).astype(BF)
-    shared = team_scatter(shared, 6).astype(BF)
-    return grad_input, (split, grad_down.astype(BF), shared)
+    swapped_grad = jnp.concatenate([jnp.zeros((128, 64), BF), last_grad[:, :64]], axis=1)
+    operands = (
+        kept["attended"],
+        jnp.pad(middle_low, ((0, 0), (0, 64))),
+        kept["normed_all"],
+        qkv_grad,
+        kept["normed"],
+        swapped_grad,
+        vectors,
+    )
+    split = (
+        kept["normed_all"],
+        qkv_grad,
+        kept["second_all"],
+        up_grad,
+        kept["activated"],
+        grad_low_all,
+    )
+    return grad_input, operands, split
 
 
 BOTH = ("section", "shard")
@@ -652,12 +1550,11 @@
 ):
     c, z, x = place()
     q = c * 4 + x
-    swap = pairs(lambda a, b: (b, a))
-    cross = pairs(lambda a, b: (1 - b, a))
+    swap = [pair for pair in pairs(lambda a, b: (b, a)) if pair[0] != pair[1]]
     cross_back = pairs(lambda a, b: (b, 1 - a))
 
-    def mine(array):
-        return lax.ppermute(jnp.where(c == z, array[z], array[1 - z])[0], BOTH, swap)
+    def swapped(array):
+        return jnp.where(c == z, array, lax.ppermute(array, BOTH, swap))
 
     def by_z(own, other):
         return jnp.where(z == 0, jnp.stack([own, other]), jnp.stack([other, own]))
@@ -665,12 +1562,12 @@
     small = jnp.concatenate(
         [
             qv_bias[0],
+            up_bias[0],
             out_bias[0],
             gain_one[0],
             bias_one[0],
             gain_two[0],
             bias_two[0],
-            up_bias[0],
             down_bias[0],
         ]
     )
@@ -689,14 +1586,34 @@
         + [w_up[0].reshape(136, 8, 544)],
         axis=2,
     ).transpose(1, 0, 2)
-    all_blocks, all_common = spread_weights(blocks, common)
-    all_out = lax.all_gather(w_out[0], BOTH, axis=0, tiled=True).reshape(2, D, D)
-    down_own = lax.ppermute(w_down[0], BOTH, swap)
+    blocks = jnp.pad(blocks, ((0, 0), (0, 8), (0, 0)))
+    replica = lax.axis_index("replica")
+    late = lax.dynamic_slice(
+        jnp.pad(blocks, ((0, 0), (0, 0), (0, 96))), (0, 0, replica * 128), (8, 144, 128)
+    )
+    first_blocks, late, all_common, hidden, top_grad = spread_weights(
+        late, common, inputs[:, 0], cotangent[:, 0]
+    )
+    teams = [[a * 8 + b * 4 + d for a in range(2) for d in range(4)] for b in range(2)]
+    top_grad_all = lax.all_gather(top_grad, BOTH, axis_index_groups=teams, axis=0, tiled=True)
+    second_blocks = lax.all_gather(late, "replica", axis=0)
+    own_out = lax.all_gather(w_out[0], "shard", axis=0, tiled=True)
+    partner_out = lax.ppermute(own_out, "section", [(0, 1), (1, 0)])
+    all_out = jnp.where(
+        c == 0, jnp.stack([own_out, partner_out]), jnp.stack([partner_out, own_out])
+    )
+    cuts = (
+        first_blocks.reshape(4, 2, 2, 4, 144, 128)
+        .transpose(2, 3, 4, 0, 1, 5)[:, :, :136]
+        .reshape(D, 1024)[:, :928],
+        second_blocks.transpose(1, 2, 0, 3)[:, :136].reshape(D, 1024)[:, :928],
+    )
+    down_own = swapped(w_down[0])
     down_other = lax.ppermute(w_down[0], BOTH, cross_back)
     all_down = by_z(down_own, down_other)
 
     def layer_weights(layer):
-        cut = all_blocks[layer].reshape(D, 928)
+        cut = cuts[layer]
         shared = all_common[layer, :, :136].reshape(D, 256)
         vec = all_common[layer, :, 136:].reshape(8, 2048)[:, :1632].astype(F32)
 
@@ -704,6 +1621,8 @@
             return vec[:, start : start + size].reshape(-1)
 
         qv = piece(0, 272)
+        six = vec[:, 816:].reshape(8, 6, 136).transpose(1, 0, 2).reshape(6, D)
+        six = lax.optimization_barrier(six)
         none = jnp.zeros((128,), F32)
         qkv_bias = jnp.concatenate(
             [
@@ -721,71 +1640,44 @@
             qkv_bias=qkv_bias,
             last_bias=jnp.concatenate([qv[1024:D], none[:64]]),
             out=jnp.concatenate([out[:1024], jnp.zeros((64, D), BF), out[1024:]]),
-            out_bias=piece(272, 136),
-            gain_one=piece(408, 136),
-            bias_one=piece(544, 136),
-            gain_two=piece(680, 136),
-            bias_two=piece(816, 136),
+            out_bias=six[0:1],
+            gain_one=six[1:2],
+            bias_one=six[2:3],
+            gain_two=six[3:4],
+            bias_two=six[4:5],
             up=cut[:, 384:],
-            up_bias=lax.dynamic_slice(piece(952, 544), (q * 544,), (544,)),
+            up_bias=lax.dynamic_slice(piece(272, 544), (q * 544,), (544,)),
             down=all_down[layer],
-            down_bias=piece(1496, 136),
+            down_bias=six[5:6],
         )
 
     weights = [layer_weights(0), layer_weights(1)]
-    hidden = mine(inputs).astype(F32)
-    top_grad = mine(cotangent).astype(F32)
+    hidden = hidden.astype(F32)
+    top_grad = top_grad.astype(F32)
     out_first, kept_first = layer_forward(hidden, weights[0])
     out_second, kept_second = layer_forward(out_first.astype(BF).astype(F32), weights[1])
-    grad_second, parts_second = layer_backward(top_grad, weights[1], kept_second, q)
-    grad_first, parts_first = layer_backward(
-        grad_second.astype(BF).astype(F32), weights[0], kept_first, q
-    )
-
-    def home(first, second):
-        own = lax.ppermute(jnp.where(z == 0, first, second), BOTH, swap)
-        other = lax.ppermute(jnp.where(z == 0, second, first), BOTH, cross)
-        return own, other
-
-    def rows_home(first, second):
-        own, other = home(first.astype(BF), second.astype(BF))
-        stacked = jnp.where(c == 0, jnp.stack([own, other]), jnp.stack([other, own]))
-        return stacked.astype(F32)[None, :, None]
-
-    section_out = rows_home(out_first, out_second)
-    input_grad = rows_home(grad_first, grad_second)
-
-    def sum_home(first, second):
-        own, other = home(first, second)
-        return (own.astype(F32) + other.astype(F32)).astype(BF)
-
-    down_grad = sum_home(parts_first[1], parts_second[1])
-    shared_grad = sum_home(parts_first[2], parts_second[2])
-    split_grad = collect_grads(jnp.stack([parts_first[0], parts_second[0]]))
-    split_grad, down_grad, shared_grad = lax.psum((split_grad, down_grad, shared_grad), "replica")
-    split_grad, down_grad, shared_grad = (
-        array.astype(F32) for array in (split_grad, down_grad, shared_grad)
-    )
-    split_rows = split_grad.transpose(1, 0, 2)
-    head_rows = split_rows[:, :, :384].reshape(136, 8, 3, 128)
-    last = shared_grad[:136, D:]
-    grad_qkv = jnp.concatenate(
-        [
-            head_rows[:, :, 0].reshape(136, 1024),
-            last[:, 128:],
-            head_rows[:, :, 1].reshape(136, 1024),
-            last[:, :64],
-            head_rows[:, :, 2].reshape(136, 1024),
-            last[:, 64:128],
-        ],
-        axis=1,
-    )
-    grad_up = split_rows[:, :, 384:].reshape(136, FF)
-    vec = shared_grad[136:].reshape(-1)
+    grad_second, operands, split = layer_backward(
+        top_grad, top_grad_all, weights[1], kept_second, q
+    )
+    rows = jnp.stack([out_first.astype(BF), out_second.astype(BF)])
+    shared, section_out = shared_scatter(operands + (rows,), None)
+    pieces = grad_pieces(*split, shared)
+    grad_first, operands, split = layer_backward(
+        grad_second.astype(BF).astype(F32), None, weights[0], kept_first, q
+    )
+    rows = jnp.stack([grad_first.astype(BF), grad_second.astype(BF)])
+    shared, input_grad, second_layer = shared_scatter(operands + (rows,), pieces)
+    pieces = grad_pieces(*split, shared)
+    grad_qkv, grad_out_w, grad_up, grad_down, vectors = assemble(
+        reduce_grads(pieces, second_layer)
+    )
+    section_out = section_out.astype(F32)[None, :, None]
+    input_grad = input_grad.astype(F32)[None, :, None]
+    vec = vectors.reshape(-1)
     grads = (
         grad_qkv,
         vec[:272],
-        shared_grad[:136, :D],
+        grad_out_w,
         vec[272:408],
         vec[408:544],
         vec[544:680],
@@ -793,7 +1685,7 @@
         vec[816:952],
         grad_up,
         vec[952:1496],
-        down_grad,
+        grad_down,
         vec[1496:1632],
     )
     return (section_out, input_grad) + tuple(grad[None] for grad in grads)

time: 971 us -> 640 us (0.66)
  waiting for transfers between devices: 174 us -> 0.75 us
  matrix products: 80 us -> 18.1 us
  local copies, waits for them, and re-layouts: 108 us -> 57 us
  starting transfers between devices: 37.5 us -> 4.1 us
  other arithmetic: 57.4 us -> 27 us
  Pallas kernels: 489 us -> 509 us
    psum x1 -> x0, waiting for transfers between devices: 158 us -> none  [local(): lax.psum((split_grad, down_grad, shared_grad), 'replica')]
    ppermute x11 -> x2, starting transfers between devices: 35.5 us -> 2.07 us  [the longest x1 1.71 us: swapped(): return jnp.where(c == z, array, lax.ppermute(array, BOTH, swap))]
    dot_general x10 -> x0, matrix products: 26.5 us -> none  [dot_tn(): lax.dot_general(left, right, (((0,), (0,)), ((), ())), preferred_element_...]
    convert_element_type x6 -> x0, local copies, waits for them, and re-layouts: 22.2 us -> none  [the longest x2 8.72 us: layer_backward(): parts = dot_nt(up_grad, w['up']).astype(BF).reshape(8, 128, D)]
    pallas_call x16 -> x18, Pallas kernels: 422 us -> 443 us  [the longest x6 119 us: product_scatter(): pl.pallas_call(functools.partial(product_scatter_kernel, product), out_sh...]
    dot_general x10 -> x4, matrix products: 26 us -> 5.4 us  [dot(): return jnp.dot(left, right, preferred_element_type=F32)]
    ppermute x11 -> x2, waiting for transfers between devices: 15.3 us -> 0.01 us  [the longest x1 0.01 us: swapped(): return jnp.where(c == z, array, lax.ppermute(array, BOTH, swap))]
    dot_general x10 -> x5, matrix products: 27.5 us -> 12.7 us  [dot_nt(): lax.dot_general(left, right, (((1,), (1,)), ((), ())), preferred_element_...]
  transfers between devices with their start and end apart: 14 -> 6, of which waited for: 3 -> 0; matrix products, arithmetic and copies ran while one was open for 6% -> 10% of each run, Pallas kernels for 24% -> 29%
where the time goes in v2:
time: 640 us; the launch traced here: 631 us
  Pallas kernels  509 us (80%)
  local copies, waits for them, and re-layouts  57 us (9%)
  other arithmetic  27 us (4%)
  matrix products  18.1 us (3%)
  between operations  15.6 us (2%)
    pallas_call x6, Pallas kernels, product_scatter(): pl.pallas_call(functools.partial(product_scatter_kernel, product), out_sh...  119 us
    pallas_call x5, Pallas kernels, team_gather(): pl.pallas_call(kernel, out_shape=(jax.ShapeDtypeStruct((8, rows, columns)...  95.4 us
    pallas_call x1, Pallas kernels, reduce_grads(): pl.pallas_call(reduce_kernel, out_shape=jax.ShapeDtypeStruct((8, GOT_ROWS...  73.6 us
    pallas_call x2, Pallas kernels, shared_scatter(): pl.pallas_call(functools.partial(shared_kernel, rings), out_shape=out_sha...  65.4 us
    pallas_call x1, Pallas kernels, spread_weights(): pl.pallas_call(weights_kernel, out_shape=(jax.ShapeDtypeStruct((4, 4, 4,...  61.4 us
    pallas_call x2, Pallas kernels, grad_pieces(): pl.pallas_call(pieces_kernel, out_shape=jax.ShapeDtypeStruct((4, 4, ROWS,...  21.9 us
    pallas_call x2, Pallas kernels, attend_back(): pl.pallas_call(attend_back_kernel, out_shape=(jax.ShapeDtypeStruct((1024,...  20 us
    pallas_call x2, Pallas kernels, heads_to_rows(): pl.pallas_call(heads_to_rows_kernel, out_shape=jax.ShapeDtypeStruct((128,...  18 us
  transfers between devices with their start and end apart: 6, of which 0 were waited for; matrix products, arithmetic and copies ran while one was open for 10% of the time, Pallas kernels for 29%

profile of v2, /device:TPU:16, one launch (start us, length us, event | category | flops | bytes accessed | tf_op | source)
XLA Modules:
  0.0 631.4 jit_solution(10579378519507113403)
XLA Ops:
  8.0 2.0 slice_bitcast_fusion.6
  10.2 2.3 reshape_squeeze.15
  13.0 2.1 copy.63
  15.1 2.1 copy.64
  20.1 61.4 %shard_map.245 = (bf16[4,4,4,144,128]{4,3,2,1,0:T(8,128)(2,1)}, bf16[8,144,128]{2,1,0:T(8,128)(2,1)}, bf16[2,8,144,256]{3,2,1,0:T(8,128)(2,1)}, bf16[128,1088]{1,0:T(8,128)(2,1)}, bf16[128,1088]{1,0:T(8,128)(2,1)}) custom-call(bf16[8,144,128]{2,1,0:T(8,128)(2,1)} %pad_dynamic-slice_fusion.late, bf16[144,256]{1,0:T(8,128)(2,1)} %pad_maximum_fusion.10.common, ...), custom_call_target="tpu_custom_call" | custom-call | tf_op jit(solution)/shard_map/pallas_call | solution.py:626
  81.6 1.7 collective-permute-start.1
  83.3 1.9 collective-permute-start.2
  86.2 2.1 fusion.56
  90.1 4.2 copy.98
  94.3 1.5 slice.318
  95.8 2.8 reshape.262
  98.6 2.7 slice.330.weight.right
  107.4 17.7 %shard_map.246 = (bf16[8,128,1088]{2,1,0:T(8,128)(2,1)}, bf16[1024,512]{1,0:T(8,128)(2,1)}) custom-call(bf16[128,1088]{1,0:T(8,128)(2,1)} %copy-done.9, bf16[1088,512]{1,0:T(8,128)(2,1)} %pad_maximum_fusion.6.weight.right, f32[1,512]{1,0:T(1,128)} %bitcast.162), custom_call_target="tpu_custom_call" | custom-call | tf_op jit(solution)/shard_map/pallas_call | solution.py:145
  125.1 5.4 shard_map.247
  130.5 9.2 %shard_map.248.refs_1_ = bf16[128,1152]{1,0:T(8,128)(2,1)} custom-call(bf16[8,128,128]{2,1,0:T(8,128)(2,1)} %bitcast.155, bf16[128,128]{1,0:T(8,128)(2,1)} %get-tuple-element.54.extra), custom_call_target="tpu_custom_call" | custom-call | tf_op jit(solution)/shard_map/pallas_call | solution.py:319
  144.2 2.7 maximum_select_fusion.1
  146.9 1.7 slice_bitcast_fusion.2
  148.6 3.3 copy.97
  155.2 4.4 maximum_select_fusion
  162.6 20.0 %shard_map.249 = (bf16[8,128,1088]{2,1,0:T(8,128)(2,1)}, f32[1024,544]{1,0:T(8,128)}, bf16[1024,544]{1,0:T(8,128)(2,1)}) custom-call(bf16[128,1088]{1,0:T(8,128)(2,1)} %add_convert_fusion.3.own, bf16[1088,544]{1,0:T(8,128)(2,1)} %slice.330.weight.right, f32[1,544]{1,0:T(1,128)} %reshape.267.bias), custom_call_target="tpu_custom_call" | custom-call | tf_op jit(solution)/shard_map/pallas_call | solution.py:145
  182.7 19.2 %shard_map.250 = f32[128,1088]{1,0:T(8,128)} custom-call(bf16[1024,544]{1,0:T(8,128)(2,1)} %get-tuple-element.55.left.activated, bf16[544,1088]{1,0:T(8,128)(2,1)} %get-tuple-element.169.right.weight), custom_call_target="tpu_custom_call" | custom-call | tf_op jit(solution)/shard_map/pallas_call | solution.py:279
  204.5 17.4 %shard_map.251 = (bf16[8,128,1088]{2,1,0:T(8,128)(2,1)}, bf16[1024,512]{1,0:T(8,128)(2,1)}) custom-call(bf16[128,1088]{1,0:T(8,128)(2,1)} %fusion.28.own.refs_4_, bf16[1088,512]{1,0:T(8,128)(2,1)} %pad_maximum_fusion.7.weight.right, f32[1,512]{1,0:T(1,128)} %bitcast.161), custom_call_target="tpu_custom_call" | custom-call | tf_op jit(solution)/shard_map/pallas_call | solution.py:145
  221.9 1.8 fusion.14.last_query
  223.7 5.4 shard_map.252
  229.1 8.7 %shard_map.253.refs_0_ = bf16[128,1152]{1,0:T(8,128)(2,1)} custom-call(bf16[8,128,128]{2,1,0:T(8,128)(2,1)} %bitcast.156, bf16[128,128]{1,0:T(8,128)(2,1)} %get-tuple-element.59.extra), custom_call_target="tpu_custom_call" | custom-call | tf_op jit(solution)/shard_map/pallas_call | solution.py:319
  237.9 1.9 fusion.64
  241.4 20.1 %shard_map.254 = (bf16[8,128,1088]{2,1,0:T(8,128)(2,1)}, f32[1024,544]{1,0:T(8,128)}, bf16[1024,544]{1,0:T(8,128)(2,1)}) custom-call(bf16[128,1088]{1,0:T(8,128)(2,1)} %add_convert_fusion.1.own, bf16[1088,544]{1,0:T(8,128)(2,1)} %slice.351.weight.right, f32[1,544]{1,0:T(1,128)} %reshape.275.bias), custom_call_target="tpu_custom_call" | custom-call | tf_op jit(solution)/shard_map/pallas_call | solution.py:145
  261.6 7.2 %convert_reduce_fusion.1 = (f32[544]{0:T(1024)}, bf16[1024,544]{1,0:T(8,128)(2,1)}) fusion(f32[1024,544]{1,0:T(8,128)} %get-tuple-element.61, bf16[1024,1088]{1,0:T(8,128)(2,1)} %all-gather.6.cloned.1.call-done.low_all, bf16[2,544,1088]{2,1,0:T(8,128)(2,1)S(1)} %maximum_select_fusion.1), kind=kOutput, calls=%fused_computation.13 | convolution fusion | flops 1223851520 | bytes 6826112 | tf_op jit(solution)/shard_map/dot_general | solution.py:1262
  268.9 20.7 %shard_map.255 = f32[128,1088]{1,0:T(8,128)} custom-call(bf16[1024,544]{1,0:T(8,128)(2,1)} %get-tuple-element.202.left.up_grad, bf16[1088,544]{1,0:T(8,128)(2,1)} %slice.351.weight.right), custom_call_target="tpu_custom_call" | custom-call | tf_op jit(solution)/shard_map/pallas_call | solution.py:279
  291.1 18.8 %shard_map.259 = f32[128,1088]{1,0:T(8,128)} custom-call(bf16[1024,544]{1,0:T(8,128)(2,1)} %get-tuple-element.65.left.activated, bf16[544,1088]{1,0:T(8,128)(2,1)} %get-tuple-element.168.right), custom_call_target="tpu_custom_call" | custom-call | tf_op jit(solution)/shard_map/pallas_call | solution.py:279
  311.4 1.7 convolution_convert_fusion.1.rows
  313.1 8.8 %shard_map.256 = bf16[8,128,128]{2,1,0:T(8,128)(2,1)} custom-call(bf16[128,1152]{1,0:T(8,128)(2,1)} %convolution_convert_fusion.1.rows), custom_call_target="tpu_custom_call" | custom-call | tf_op jit(solution)/shard_map/pallas_call | solution.py:359
  323.3 9.9 %shard_map.257 = (bf16[1024,512]{1,0:T(8,128)(2,1)}, bf16[128,128]{1,0:T(8,128)(2,1)}) custom-call(bf16[1024,512]{1,0:T(8,128)(2,1)} %get-tuple-element.57.projected, bf16[128,128]{1,0:T(8,128)(2,1)} %fusion.14.last_query, bf16[1024,128]{1,0:T(8,128)(2,1)} %bitcast.149, bf16[128,128]{1,0:T(8,128)(2,1)} %slice.353.last_grad), custom_call_target="tpu_custom_call" | custom-call | tf_op jit(solution)/shard_map/pallas_call | solution.py:1357
  333.2 20.1 %shard_map.258 = f32[128,1088]{1,0:T(8,128)} custom-call(bf16[1024,512]{1,0:T(8,128)(2,1)} %get-tuple-element.63.left.refs_3_.qkv_grad, bf16[1088,512]{1,0:T(8,128)(2,1)} %pad_maximum_fusion.7.weight.right), custom_call_target="tpu_custom_call" | custom-call | tf_op jit(solution)/shard_map/pallas_call | solution.py:279
  353.3 1.5 fusion.30
  355.8 20.2 %shard_map.262 = (bf16[8,128,1088]{2,1,0:T(8,128)(2,1)}, bf16[1024,544]{1,0:T(8,128)(2,1)}) custom-call(bf16[128,1088]{1,0:T(8,128)(2,1)} %get-tuple-element.155.own, bf16[544,1088]{1,0:T(8,128)(2,1)} %get-tuple-element.169.right.weight, f32[1024,544]{1,0:T(8,128)} %get-tuple-element.69.upper), custom_call_target="tpu_custom_call" | custom-call | tf_op jit(solution)/shard_map/pallas_call | solution.py:145
  376.1 20.2 %shard_map.263 = f32[128,1088]{1,0:T(8,128)} custom-call(bf16[1024,544]{1,0:T(8,128)(2,1)} %get-tuple-element.70.left.up_grad, bf16[1088,544]{1,0:T(8,128)(2,1)} %slice.330.weight.right), custom_call_target="tpu_custom_call" | custom-call | tf_op jit(solution)/shard_map/pallas_call | solution.py:279
  396.3 1.5 multiply_reduce_fusion
  399.2 1.8 convolution_convert_fusion.rows
  401.0 8.7 %shard_map.264 = bf16[8,128,128]{2,1,0:T(8,128)(2,1)} custom-call(bf16[128,1152]{1,0:T(8,128)(2,1)} %convolution_convert_fusion.rows), custom_call_target="tpu_custom_call" | custom-call | tf_op jit(solution)/shard_map/pallas_call | solution.py:359
  411.0 10.2 %shard_map.265 = (bf16[1024,512]{1,0:T(8,128)(2,1)}, bf16[128,128]{1,0:T(8,128)(2,1)}) custom-call(bf16[1024,512]{1,0:T(8,128)(2,1)} %get-tuple-element.52.projected, bf16[128,128]{1,0:T(8,128)(2,1)} %fusion.13.last_query, bf16[1024,128]{1,0:T(8,128)(2,1)} %bitcast.150, bf16[128,128]{1,0:T(8,128)(2,1)} %slice.355.last_grad), custom_call_target="tpu_custom_call" | custom-call | tf_op jit(solution)/shard_map/pallas_call | solution.py:1357
  421.2 20.2 %shard_map.266 = f32[128,1088]{1,0:T(8,128)} custom-call(bf16[1024,512]{1,0:T(8,128)(2,1)} %get-tuple-element.72.left.refs_4_.qkv_grad, bf16[1088,512]{1,0:T(8,128)(2,1)} %pad_maximum_fusion.6.weight.right), custom_call_target="tpu_custom_call" | custom-call | tf_op jit(solution)/shard_map/pallas_call | solution.py:279
  452.3 21.6 %shard_map.260 = (f32[144,1280]{1,0:T(8,128)}, bf16[2,128,1088]{2,1,0:T(8,128)(2,1)}) custom-call(bf16[128,1152]{1,0:T(8,128)(2,1)} %shard_map.253.refs_0_, bf16[128,1152]{1,0:T(8,128)(2,1)} %pad.33.refs_1_, bf16[1024,1088]{1,0:T(8,128)(2,1)} %bitcast.121, bf16[1024,512]{1,0:T(8,128)(2,1)} %get-tuple-element.63.left.refs_3_.qkv_grad, ...), custom_call_target="tpu_custom_call" | custom-call | tf_op jit(solution)/shard_map/pallas_call | solution.py:1143
  473.9 11.0 %shard_map.261.refs_0_ = bf16[4,4,992,128]{3,2,1,0:T(8,128)(2,1)} custom-call(bf16[1024,1088]{1,0:T(8,128)(2,1)} %bitcast.122, bf16[1024,512]{1,0:T(8,128)(2,1)} %get-tuple-element.63.left.refs_3_.qkv_grad, bf16[1024,1088]{1,0:T(8,128)(2,1)} %bitcast.136, bf16[1024,544]{1,0:T(8,128)(2,1)} %get-tuple-element.202.left.up_grad, ...), custom_call_target="tpu_custom_call" | custom-call | tf_op jit(solution)/shard_map/pallas_call | solution.py:1207
  484.9 43.7 %shard_map.267 = (f32[144,1280]{1,0:T(8,128)}, bf16[2,128,1088]{2,1,0:T(8,128)(2,1)}, bf16[992,128]{1,0:T(8,128)(2,1)}) custom-call(bf16[4,4,992,128]{3,2,1,0:T(8,128)(2,1)} %shard_map.261.refs_0_, bf16[128,1152]{1,0:T(8,128)(2,1)} %shard_map.248.refs_1_, bf16[128,1152]{1,0:T(8,128)(2,1)} %pad.35.refs_2_, bf16[1024,1088]{1,0:T(8,128)(2,1)} %bitcast.119, ...), custom_call_target="tpu_custom_call" | custom-call | tf_op jit(solution)/shard_map/pallas_call | solution.py:1143
  528.7 11.0 %shard_map.268.pieces = bf16[4,4,992,128]{3,2,1,0:T(8,128)(2,1)} custom-call(bf16[1024,1088]{1,0:T(8,128)(2,1)} %bitcast.120, bf16[1024,512]{1,0:T(8,128)(2,1)} %get-tuple-element.72.left.refs_4_.qkv_grad, bf16[1024,1088]{1,0:T(8,128)(2,1)} %bitcast.135, bf16[1024,544]{1,0:T(8,128)(2,1)} %get-tuple-element.70.left.up_grad, ...), custom_call_target="tpu_custom_call" | custom-call | tf_op jit(solution)/shard_map/pallas_call | solution.py:1207
  539.6 73.6 %shard_map.269.got = bf16[8,1984,128]{2,1,0:T(8,128)(2,1)} custom-call(bf16[4,4,992,128]{3,2,1,0:T(8,128)(2,1)} %shard_map.268.pieces, bf16[992,128]{1,0:T(8,128)(2,1)} %get-tuple-element.78.second_layer), custom_call_target="tpu_custom_call" | custom-call | tf_op jit(solution)/shard_map/pallas_call | solution.py:993
  613.3 5.7 shard_map.270
  (323 shorter events, 52.1 us)
Async XLA Ops:
  7.2 133.1 %all-gather.8.cloned.1.call-start = ((), (), s32[]{:S(2)}) async-start(), calls=%async_computation.1 | async-start | bytes 2820096 | tf_op jit(solution)/shard_map/all_gather | solution.py:1600
  7.9 140.7 %all-gather.10.cloned.1.call-start = ((), (), s32[]{:S(2)}) async-start(), calls=%async_computation.2 | async-start | bytes 2654208 | tf_op jit(solution)/shard_map/all_gather | solution.py:1599
  12.6 6.3 copy-start.24
  81.5 6.8 %copy-start.7 = (bf16[128,1088]{1,0:T(8,128)(2,1)S(1)}, bf16[128,1088]{1,0:T(8,128)(2,1)}, u32[]{:S(2)}) copy-start(bf16[128,1088]{1,0:T(8,128)(2,1)} %get-tuple-element.49) | copy-start | bytes 835588
  81.6 180.0 %all-gather.6.cloned.1.call-start = ((), (), s32[]{:S(2)}) async-start(), calls=%async_computation | async-start | bytes 2654208 | tf_op jit(solution)/shard_map/all_gather | solution.py:1598
  81.6 61.1 %collective-permute-start.1 = (bf16[544,1088]{1,0:T(8,128)(2,1)}, bf16[544,1088]{1,0:T(8,128)(2,1)}, u32[]{:S(2)}, u32[]{:S(2)}) collective-permute-start(bf16[544,1088]{1,0:T(8,128)(2,1)} %bitcast.14), channel_id=1, source_target_pairs={{32,64},{40,72},{48,80},{56,88},{64,32},{72,40},{80,48},{88,56},{3... | collective-permute-start | bytes 3551240 | tf_op jit(solution)/shard_map/ppermute | solution.py:1557
  83.3 60.8 %collective-permute-start.2 = (bf16[544,1088]{1,0:T(8,128)(2,1)}, bf16[544,1088]{1,0:T(8,128)(2,1)}, u32[]{:S(2)}, u32[]{:S(2)}) collective-permute-start(bf16[544,1088]{1,0:T(8,128)(2,1)} %bitcast.14), channel_id=1, source_target_pairs={{0,32},{8,40},{16,48},{24,56},{32,96},{40,104},{48,112},{56,120},{... | collective-permute-start | bytes 3551240 | tf_op jit(solution)/shard_map/ppermute | solution.py:1612
  88.3 15.7 %copy-start.15 = (bf16[1,8,136,256]{3,2,1,0:T(8,128)(2,1)}, bf16[1,8,136,256]{3,2,1,0:T(8,128)(2,1)S(1)}, u32[]{:S(2)}) copy-start(bf16[1,8,136,256]{3,2,1,0:T(8,128)(2,1)S(1)} %get-tuple-element.171) | copy-start | bytes 1671172
  88.8 5.5 copy-start.60
  89.6 4.7 copy-start.32
  89.9 14.1 %copy-start.9 = (bf16[128,1088]{1,0:T(8,128)(2,1)}, bf16[128,1088]{1,0:T(8,128)(2,1)S(1)}, u32[]{:S(2)}) copy-start(bf16[128,1088]{1,0:T(8,128)(2,1)S(1)} %fusion.37.own.refs_5_) | copy-start | bytes 835588
  98.6 6.2 slice-start
  140.3 14.8 %collective-permute-start = (bf16[1088,1088]{1,0:T(8,128)(2,1)}, bf16[1088,1088]{1,0:T(8,128)(2,1)}, u32[]{:S(2)}, u32[]{:S(2)}) collective-permute-start(bf16[1088,1088]{1,0:T(8,128)(2,1)} %bitcast.130), channel_id=1, source_target_pairs={{0,64},{64,0},{1,65},{65,1},{2,66},{66,2},{3,67},{67,3},{4,68},{68... | collective-permute-start | bytes 7102472 | tf_op jit(solution)/shard_map/ppermute | solution.py:1601
  160.0 77.8 %copy-start.13 = (bf16[1024,1088]{1,0:T(8,128)(2,1)}, bf16[1024,1088]{1,0:T(8,128)(2,1)S(1)}, u32[]{:S(2)}) copy-start(bf16[1024,1088]{1,0:T(8,128)(2,1)S(1)} %get-tuple-element.164) | copy-start | bytes 6684676
  160.0 77.8 %copy-start.28 = (bf16[64,1088]{1,0:T(8,128)(2,1)}, bf16[64,1088]{1,0:T(8,128)(2,1)S(1)}, u32[]{:S(2)}) copy-start(bf16[64,1088]{1,0:T(8,128)(2,1)S(1)} %get-tuple-element.166) | copy-start | bytes 417796
  161.5 21.2 %copy-start.44 = (f32[128]{0:T(128)}, f32[128]{0:T(128)S(1)}, u32[]{:S(2)}) copy-start(f32[128]{0:T(128)S(1)} %broadcast_multiply_fusion.10) | copy-start | bytes 1540
  161.7 20.9 %copy-start.50 = (f32[128]{0:T(128)}, f32[128]{0:T(128)S(1)}, u32[]{:S(2)}) copy-start(f32[128]{0:T(128)S(1)} %add_rsqrt_fusion.2) | copy-start | bytes 1540
  162.6 39.3 %copy-start.36 = (f32[1088]{0:T(1024)S(1)}, f32[1088]{0:T(1024)}, u32[]{:S(2)}) copy-start(f32[1088]{0:T(1024)} %get-tuple-element.148) | copy-start | bytes 13060
  182.6 20.9 %copy-start.34 = (f32[1088]{0:T(1024)S(1)}, f32[1088]{0:T(1024)}, u32[]{:S(2)}) copy-start(f32[1088]{0:T(1024)} %get-tuple-element.147) | copy-start | bytes 13060
  182.6 20.9 %copy-start.40 = (f32[1088]{0:T(1024)S(1)}, f32[1088]{0:T(1024)}, u32[]{:S(2)}) copy-start(f32[1088]{0:T(1024)} %get-tuple-element.146) | copy-start | bytes 13060
  201.9 20.0 %copy-start.18 = (bf16[1,8,136,256]{3,2,1,0:T(8,128)(2,1)S(1)}, bf16[1,8,136,256]{3,2,1,0:T(8,128)(2,1)}, u32[]{:S(2)}) copy-start(bf16[1,8,136,256]{3,2,1,0:T(8,128)(2,1)} %get-tuple-element.170) | copy-start | bytes 1671172
  201.9 20.0 %copy-start.71 = (f32[128]{0:T(128)S(1)}, f32[128]{0:T(128)}, u32[]{:S(2)}) copy-start(f32[128]{0:T(128)} %concatenate.64) | copy-start | bytes 1540
  203.2 34.6 %copy-start.43 = (f32[1088]{0:T(1024)S(1)}, f32[1088]{0:T(1024)}, u32[]{:S(2)}) copy-start(f32[1088]{0:T(1024)} %get-tuple-element.145) | copy-start | bytes 13060
  203.2 36.5 %copy-start.52 = (f32[128]{0:T(128)}, f32[128]{0:T(128)S(1)}, u32[]{:S(2)}) copy-start(f32[128]{0:T(128)S(1)} %broadcast_multiply_fusion.9) | copy-start | bytes 1540
  203.5 36.2 %copy-start.62 = (f32[128]{0:T(128)}, f32[128]{0:T(128)S(1)}, u32[]{:S(2)}) copy-start(f32[128]{0:T(128)S(1)} %add_rsqrt_fusion.1) | copy-start | bytes 1540
  268.9 20.7 %copy-start.4 = (f32[128,1088]{1,0:T(8,128)S(1)}, f32[128,1088]{1,0:T(8,128)}, u32[]{:S(2)}) copy-start(f32[128,1088]{1,0:T(8,128)} %copy-done.3) | copy-start | bytes 1671172
  268.9 20.7 %copy-start.47 = (f32[128]{0:T(128)S(1)}, f32[128]{0:T(128)}, u32[]{:S(2)}) copy-start(f32[128]{0:T(128)} %copy-done.46) | copy-start | bytes 1540
  268.9 20.7 %copy-start.55 = (f32[128]{0:T(128)S(1)}, f32[128]{0:T(128)}, u32[]{:S(2)}) copy-start(f32[128]{0:T(128)} %copy-done.54) | copy-start | bytes 1540
  289.6 20.3 %copy-start.5 = (f32[128,1088]{1,0:T(8,128)S(1)}, f32[128,1088]{1,0:T(8,128)}, u32[]{:S(2)}) copy-start(f32[128,1088]{1,0:T(8,128)} %shard_map.255) | copy-start | bytes 1671172
  289.6 20.3 %copy-start.22 = (bf16[128,1088]{1,0:T(8,128)(2,1)S(1)}, bf16[128,1088]{1,0:T(8,128)(2,1)}, u32[]{:S(2)}) copy-start(bf16[128,1088]{1,0:T(8,128)(2,1)} %get-tuple-element.60) | copy-start | bytes 835588
  289.6 20.3 %copy-start.38 = (f32[1088]{0:T(1024)S(1)}, f32[1088]{0:T(1024)}, u32[]{:S(2)}) copy-start(f32[1088]{0:T(1024)} %get-tuple-element.142) | copy-start | bytes 13060
  291.1 20.3 %copy-start.14 = (bf16[1024,1088]{1,0:T(8,128)(2,1)S(1)}, bf16[1024,1088]{1,0:T(8,128)(2,1)}, u32[]{:S(2)}) copy-start(bf16[1024,1088]{1,0:T(8,128)(2,1)} %copy-done.13) | copy-start | bytes 6684676
  291.1 20.3 %copy-start.29 = (bf16[64,1088]{1,0:T(8,128)(2,1)S(1)}, bf16[64,1088]{1,0:T(8,128)(2,1)}, u32[]{:S(2)}) copy-start(bf16[64,1088]{1,0:T(8,128)(2,1)} %copy-done.28) | copy-start | bytes 417796
  291.1 20.3 %copy-start.57 = (bf16[1152]{0:T(1024)(128)(2,1)S(1)}, bf16[1152]{0:T(1024)(128)(2,1)}, u32[]{:S(2)}) copy-start(bf16[1152]{0:T(1024)(128)(2,1)} %pad.51.clone) | copy-start | bytes 6916
  313.1 40.1 %copy-start.19 = (bf16[1,8,136,256]{3,2,1,0:T(8,128)(2,1)S(1)}, bf16[1,8,136,256]{3,2,1,0:T(8,128)(2,1)}, u32[]{:S(2)}) copy-start(bf16[1,8,136,256]{3,2,1,0:T(8,128)(2,1)} %get-tuple-element.170) | copy-start | bytes 1671172
  313.1 40.1 %copy-start.35 = (f32[1088]{0:T(1024)S(1)}, f32[1088]{0:T(1024)}, u32[]{:S(2)}) copy-start(f32[1088]{0:T(1024)} %get-tuple-element.147) | copy-start | bytes 13060
  313.1 40.1 %copy-start.53 = (f32[128]{0:T(128)S(1)}, f32[128]{0:T(128)}, u32[]{:S(2)}) copy-start(f32[128]{0:T(128)} %copy-done.52) | copy-start | bytes 1540
  313.1 40.1 %copy-start.63 = (f32[128]{0:T(128)S(1)}, f32[128]{0:T(128)}, u32[]{:S(2)}) copy-start(f32[128]{0:T(128)} %copy-done.62) | copy-start | bytes 1540
  333.2 20.1 %copy-start.30 = (bf16[128,128]{1,0:T(8,128)(2,1)S(1)}, bf16[128,128]{1,0:T(8,128)(2,1)}, u32[]{:S(2)}) copy-start(bf16[128,128]{1,0:T(8,128)(2,1)} %get-tuple-element.64) | copy-start | bytes 98308
  376.1 20.2 %copy-start.45 = (f32[128]{0:T(128)S(1)}, f32[128]{0:T(128)}, u32[]{:S(2)}) copy-start(f32[128]{0:T(128)} %copy-done.44) | copy-start | bytes 1540
  376.1 20.2 %copy-start.51 = (f32[128]{0:T(128)S(1)}, f32[128]{0:T(128)}, u32[]{:S(2)}) copy-start(f32[128]{0:T(128)} %copy-done.50) | copy-start | bytes 1540
  376.1 21.7 %copy-start.6 = (bf16[128,1088]{1,0:T(8,128)(2,1)S(1)}, bf16[128,1088]{1,0:T(8,128)(2,1)}, u32[]{:S(2)}) copy-start(bf16[128,1088]{1,0:T(8,128)(2,1)} %get-tuple-element.155.own) | copy-start | bytes 835588
  411.0 30.7 %copy-start.2 = (bf16[1024,544]{1,0:T(8,128)(2,1)S(1)}, bf16[1024,544]{1,0:T(8,128)(2,1)}, u32[]{:S(2)}) copy-start(bf16[1024,544]{1,0:T(8,128)(2,1)} %get-tuple-element.70.left.up_grad) | copy-start | bytes 3342340
  421.2 20.2 %copy-start.1 = (bf16[1024,512]{1,0:T(8,128)(2,1)S(1)}, bf16[1024,512]{1,0:T(8,128)(2,1)}, u32[]{:S(2)}) copy-start(bf16[1024,512]{1,0:T(8,128)(2,1)} %get-tuple-element.72.left.refs_4_.qkv_grad) | copy-start | bytes 3145732
  421.2 21.5 %copy-start = (bf16[1024,512]{1,0:T(8,128)(2,1)S(1)}, bf16[1024,512]{1,0:T(8,128)(2,1)}, u32[]{:S(2)}) copy-start(bf16[1024,512]{1,0:T(8,128)(2,1)} %get-tuple-element.63.left.refs_3_.qkv_grad) | copy-start | bytes 3145732
  442.7 5.5 copy-start.58
  613.3 8.4 %copy-start.26 = (bf16[2,128,1088]{2,1,0:T(8,128)(2,1)S(1)}, bf16[2,128,1088]{2,1,0:T(8,128)(2,1)}, u32[]{:S(2)}) copy-start(bf16[2,128,1088]{2,1,0:T(8,128)(2,1)} %get-tuple-element.74) | copy-start | bytes 1671172
  618.9 4.2 copy-start.25
  (31 other events, 65.9 us)
Sparse Core Ops, SparseCore 0:
  9.7 51.3 all-gather.7
  81.7 57.2 all-gather.9
  140.7 25.0 all-gather.5

commit v3 on v2

--- a/solution.py
+++ b/solution.py
@@ -30,11 +30,26 @@
     return {"section": c, "shard": z * 4 + x}
 
 
-def greet(devices):
+def arrive(devices):
     barrier = pltpu.get_barrier_semaphore()
     for device in devices:
         pl.semaphore_signal(barrier, inc=1, device_id=device, device_id_type=MESH)
-    pl.semaphore_wait(barrier, len(devices))
+
+
+def meet(devices):
+    pl.semaphore_wait(pltpu.get_barrier_semaphore(), len(devices))
+
+
+def greet(devices):
+    arrive(devices)
+    meet(devices)
+
+
+def nothing():
+    pass
+
+
+ALONE = ([], nothing, nothing, nothing, nothing)
 
 
 def sender(send_sems, recv_sems):
@@ -53,7 +68,7 @@
     return make
 
 
-def gather_core(own, out, send_sems, recv_sems, local_sem, use):
+def gather_core(own, out, send_sems, recv_sems, local_sem, use, beside=ALONE):
     c, z, x = place()
     ahead, behind, far = (x + 1) % 4, (x + 3) % 4, (x + 2) % 4
     partner, up, down = at(1 - c, z, x), at(c, z, ahead), at(c, z, behind)
@@ -62,7 +77,10 @@
     me, other = c * 4 + x, (1 - c) * 4
     local = pltpu.make_async_copy(own, out.at[me], local_sem)
     local.start()
-    greet((partner, up, down))
+    friends = [partner, up, down] + beside[0]
+    arrive(friends)
+    local.wait()
+    meet(friends)
     send = sender(send_sems, recv_sems)
     to_up = send(own.at[first], out.at[me, first], 0, up)
     to_down = send(own.at[second], out.at[me, second], 1, down)
@@ -70,7 +88,7 @@
     up_rest = send(own.at[second], out.at[me, second], 3, up)
     down_rest = send(own.at[first], out.at[me, first], 4, down)
     from_down, from_up, from_far = c * 4 + behind, c * 4 + ahead, c * 4 + far
-    local.wait()
+    beside[1]()
     use(me)
     to_up.wait_recv()
     pass_up = send(out.at[from_down, first], out.at[from_down, first], 5, up)
@@ -84,11 +102,13 @@
     share_up = send(out.at[from_up], out.at[from_up], 8, partner)
     use(from_down)
     use(from_up)
+    beside[2]()
     pass_up.wait_recv()
     share_first = send(out.at[from_far, first], out.at[from_far, first], 9, partner)
     pass_down.wait_recv()
     share_second = send(out.at[from_far, second], out.at[from_far, second], 10, partner)
     use(from_far)
+    beside[3]()
     share_down.wait_recv()
     use(other + behind)
     share_up.wait_recv()
@@ -110,6 +130,7 @@
         share_second,
     ):
         copy.wait_send()
+    beside[4]()
 
 
 def row_block(q):
@@ -132,30 +153,52 @@
     gather_core(own, out, send_sems, recv_sems, local_sem, use)
 
 
-def gather_back_kernel(own, weight, upper, out, up_grad, send_sems, recv_sems, local_sem):
+def gather_back_kernel(
+    own, weight, upper, pieces, out, up_grad, out_pieces, send_sems, recv_sems, local_sem, *rings
+):
     def use(q):
         slope = gelu_pair(upper[row_block(q), :])[1]
         up_grad[row_block(q), :] = (dot_nt(out[q], weight[...]) * slope).astype(BF)
 
-    gather_core(own, out, send_sems, recv_sems, local_sem, use)
-
-
-def team_gather(kernel, collective_id, own, weight, third, results):
+    stages = []
+
+    def begin():
+        stages.extend(layer_rings(pieces, out_pieces, *rings))
+
+    gather_core(
+        own,
+        out,
+        send_sems,
+        recv_sems,
+        local_sem,
+        use,
+        (
+            list(grid_place()[2]),
+            begin,
+            lambda: stages[0](),
+            lambda: stages[1](),
+            lambda: stages[2](),
+        ),
+    )
+
+
+def team_gather(kernel, collective_id, own, weight, rest, results, scratch=()):
     rows, columns = own.shape
     return pl.pallas_call(
         kernel,
         out_shape=(jax.ShapeDtypeStruct((8, rows, columns), BF),) + results,
-        in_specs=[VMEM] * 3,
+        in_specs=[VMEM] * (2 + len(rest)),
         out_specs=(VMEM,) * (1 + len(results)),
         scratch_shapes=[
             pltpu.SemaphoreType.DMA((11,)),
             pltpu.SemaphoreType.DMA((11,)),
             pltpu.SemaphoreType.DMA,
-        ],
+        ]
+        + list(scratch),
         compiler_params=pltpu.CompilerParams(
             collective_id=collective_id, has_side_effects=True, vmem_limit_bytes=LIMIT
         ),
-    )(own, weight, third)
+    )(own, weight, *rest)
 
 
 def scatter_core(
@@ -182,10 +225,15 @@
     rows = out.shape[0]
     first, second = pl.ds(0, half), pl.ds(half, rows - half)
     send = sender(send_sems, recv_sems)
-    greet([partner, up, down] + beside[0])
-    swaps = []
-    for index, where in enumerate((far, ahead, behind, x)):
-        swaps.append(send(other_part(where), from_partner.at[where], index, partner))
+    friends = [partner, up, down] + beside[0]
+    arrive(friends)
+    order = (far, ahead, behind, x)
+    parts = [other_part(where) for where in order]
+    meet(friends)
+    swaps = [
+        send(part, from_partner.at[where], index, partner)
+        for index, (where, part) in enumerate(zip(order, parts))
+    ]
     beside[1]()
     for where in (far, ahead, behind, x):
         prepare(where)
@@ -205,6 +253,7 @@
     swap_down.wait_recv()
     down_sum[first, :] = both(behind, first).astype(BF)
     down_first = send(down_sum.at[first], got_up.at[first], 7, down)
+    beside[2]()
     far_up.wait_recv()
     up_sum[first, :] = (both(ahead, first) + far_first[...].astype(F32)).astype(BF)
     up_first = send(up_sum.at[first], got_down.at[first], 8, up)
@@ -214,7 +263,7 @@
     swap_own.wait_recv()
     out[first, :] = both(x, first)
     out[second, :] = both(x, second)
-    beside[2]()
+    beside[3]()
     up_second.wait_recv()
     up_first.wait_recv()
     down_first.wait_recv()
@@ -233,18 +282,18 @@
         down_second,
     ):
         copy.wait_send()
-    beside[3]()
-
-
-def nothing():
-    pass
-
-
-ALONE = ([], nothing, nothing, nothing)
-
-
-def product_scatter_kernel(product, left, right, out, other, mine, *rest):
+    beside[4]()
+
+
+def product_scatter_kernel(product, spreads, left, right, *refs):
     c, z, x = place()
+    beside = ALONE
+    if spreads:
+        summed, out, got, other, mine, *refs = refs
+        refs, spread_refs = refs[:10], refs[10:]
+        beside = spread_beside(1, summed, got, spread_refs)
+    else:
+        out, other, mine, *refs = refs
 
     def other_part(where):
         rows = left[row_block((1 - c) * 4 + where), :]
@@ -255,7 +304,7 @@
         mine[where] = product(left[row_block(c * 4 + where), :], right[...])
 
     scatter_core(
-        64, other_part, lambda where, part: mine[where, part, :], prepare, ALONE, out, *rest
+        64, other_part, lambda where, part: mine[where, part, :], prepare, beside, out, *refs
     )
 
 
@@ -275,101 +324,29 @@
     ]
 
 
-def product_scatter(product, collective_id, left, right):
-    return pl.pallas_call(
-        functools.partial(product_scatter_kernel, product),
-        out_shape=jax.ShapeDtypeStruct((128, D), F32),
-        in_specs=[VMEM, VMEM],
-        out_specs=VMEM,
+def product_scatter(product, collective_id, left, right, summed=None):
+    spreads = summed is not None
+    out_shape = (jax.ShapeDtypeStruct((128, D), F32),)
+    operands = (left, right)
+    if spreads:
+        out_shape += (jax.ShapeDtypeStruct((8, GOT_ROWS, 128), BF),)
+        operands += (summed,)
+    out = pl.pallas_call(
+        functools.partial(product_scatter_kernel, product, spreads),
+        out_shape=out_shape,
+        in_specs=[VMEM] * len(operands),
+        out_specs=(VMEM,) * len(out_shape),
         scratch_shapes=[pltpu.VMEM((4, 128, D), BF), pltpu.VMEM((4, 128, D), F32)]
-        + scatter_scratch(128, D, 64),
+        + scatter_scratch(128, D, 64)
+        + (spread_scratch() if spreads else []),
         compiler_params=pltpu.CompilerParams(
             collective_id=collective_id, has_side_effects=True, vmem_limit_bytes=LIMIT
         ),
-    )(left, right)
+    )(*operands)
+    return out if spreads else out[0]
 
 
 TEAM_STEPS = tuple((dc, dx) for dc in range(2) for dx in range(4) if dc or dx)
-
-
-def heads_to_rows_kernel(heads, extra, out, send_sems, recv_sems, local_sems):
-    c, z, x = place()
-    me = c * 4 + x
-    spots = [((c + dc) % 2, (x + dx) % 4) for dc, dx in TEAM_STEPS]
-    own_columns = pl.ds(pl.multiple_of(me * 128, 128), 128)
-    local = pltpu.make_async_copy(heads.at[me], out.at[:, own_columns], local_sems.at[0])
-    local.start()
-    last = pltpu.make_async_copy(extra, out.at[:, pl.ds(1024, 128)], local_sems.at[1])
-    last.start()
-    greet([at(tc, z, tx) for tc, tx in spots])
-    send = sender(send_sems, recv_sems)
-    copies = [
-        send(heads.at[tc * 4 + tx], out.at[:, own_columns], index, at(tc, z, tx))
-        for index, (tc, tx) in enumerate(spots)
-    ]
-    for copy in copies:
-        copy.wait_recv()
-    for copy in copies:
-        copy.wait_send()
-    local.wait()
-    last.wait()
-
-
-def heads_to_rows(heads, extra):
-    return pl.pallas_call(
-        heads_to_rows_kernel,
-        out_shape=jax.ShapeDtypeStruct((128, 1152), BF),
-        in_specs=[VMEM, VMEM],
-        out_specs=VMEM,
-        scratch_shapes=[
-            pltpu.SemaphoreType.DMA((7,)),
-            pltpu.SemaphoreType.DMA((7,)),
-            pltpu.SemaphoreType.DMA((2,)),
-        ],
-        compiler_params=pltpu.CompilerParams(
-            collective_id=1, has_side_effects=True, vmem_limit_bytes=LIMIT
-        ),
-    )(heads, extra)
-
-
-def rows_to_heads_kernel(rows, out, send_sems, recv_sems, local_sem):
-    c, z, x = place()
-    me = c * 4 + x
-    spots = [((c + dc) % 2, (x + dx) % 4) for dc, dx in TEAM_STEPS]
-
-    def columns(q):
-        return rows.at[:, pl.ds(pl.multiple_of(q * 128, 128), 128)]
-
-    local = pltpu.make_async_copy(columns(me), out.at[me], local_sem)
-    local.start()
-    greet([at(tc, z, tx) for tc, tx in spots])
-    send = sender(send_sems, recv_sems)
-    copies = [
-        send(columns(tc * 4 + tx), out.at[me], index, at(tc, z, tx))
-        for index, (tc, tx) in enumerate(spots)
-    ]
-    for copy in copies:
-        copy.wait_recv()
-    for copy in copies:
-        copy.wait_send()
-    local.wait()
-
-
-def rows_to_heads(rows):
-    return pl.pallas_call(
-        rows_to_heads_kernel,
-        out_shape=jax.ShapeDtypeStruct((8, 128, 128), BF),
-        in_specs=[VMEM],
-        out_specs=VMEM,
-        scratch_shapes=[
-            pltpu.SemaphoreType.DMA((7,)),
-            pltpu.SemaphoreType.DMA((7,)),
-            pltpu.SemaphoreType.DMA,
-        ],
-        compiler_params=pltpu.CompilerParams(
-            collective_id=2, has_side_effects=True, vmem_limit_bytes=LIMIT
-        ),
-    )(rows)
 
 
 def ring_spread(send, base, source, block, me, up, down, first, second):
@@ -841,187 +818,258 @@
     return middle, turn, finish
 
 
-def reduce_kernel(
-    pieces,
-    second_layer,
-    out,
-    summed,
-    own,
-    home_send,
-    home_recv,
-    local_sems,
-    spread_send,
-    spread_recv,
-    *scratch,
-):
+def spread_scratch():
+    dma = pltpu.SemaphoreType.DMA
+    return [pltpu.VMEM((GOT_ROWS, 128), BF), dma((9,)), dma((10,)), dma((3,)), dma((13,)), dma((13,))]
+
+
+def spread_stages(layer, summed, out, own, home_send, home_recv, local_sems, sends, recvs):
     c, z, x = place()
     r = lax.axis_index("replica")
     y, zh = r // 2, r % 2
-    zf, (y_up, y_down, z_up, z_down) = grid_place()[1:]
+    zf, (y_up, y_down, _, _) = grid_place()[1:]
     across = {"section": c, "shard": z * 4 + x, "replica": y * 2 + 1 - zh}
-    team = [at((c + dc) % 2, z, (x + dx) % 4) for dc, dx in TEAM_STEPS]
-    greet([y_up, y_down, z_up, z_down, across, at(1 - c, 1 - z, x)] + team)
-
-    def remote(src, dst, sends, recvs, index, target):
-        copy = pltpu.make_async_remote_copy(
+    me = c * 4 + x
+    mine = pl.ds(pl.multiple_of(me * 144, 16), 144)
+    holds = c == layer
+    other = c != layer
+    stays = jnp.logical_and(holds, z == layer)
+    leaves = jnp.logical_or(other, z != layer)
+
+    def copy(src, dst, send_sem, recv_sem, target):
+        return pltpu.make_async_remote_copy(
             src_ref=src,
             dst_ref=dst,
-            send_sem=sends.at[index],
-            recv_sem=recvs.at[index],
+            send_sem=send_sem,
+            recv_sem=recv_sem,
             device_id=target,
             device_id_type=MESH,
         )
-        copy.start()
-        return copy
-
-    middle, turn, finish = layer_rings(pieces, summed.at[0], *scratch)
-    summed[1] = second_layer[...]
+
+    def split_part(tx):
+        return summed.at[pl.ds(pl.multiple_of(tx * 144, 16), 144)]
+
+    def to_row(dx, base):
+        tx = (x + dx) % 4
+        return copy(
+            split_part(tx),
+            own.at[mine],
+            home_send.at[base + dx],
+            home_recv.at[base + dx],
+            at(layer, z, tx),
+        )
+
+    def split_here():
+        return pltpu.make_async_copy(split_part(x), own.at[mine], local_sems.at[0])
+
+    own_part = pl.ds(SPLIT_ROWS, OWN_ROWS)
+    slot = pl.ds(pl.multiple_of(8 * 144 + z * OWN_ROWS, 16), OWN_ROWS)
+
+    def to_owner(t):
+        return copy(
+            summed.at[own_part],
+            own.at[slot],
+            home_send.at[8],
+            home_recv.at[8 + t],
+            at(layer, c, x),
+        )
+
+    def from_row(dx):
+        return copy(
+            split_part(x),
+            own.at[mine],
+            home_send.at[4 + dx],
+            home_recv.at[4 + dx],
+            at(1 - c, z, x),
+        )
+
+    def from_owner(t):
+        return copy(
+            summed.at[own_part],
+            own.at[slot],
+            home_send.at[8],
+            home_recv.at[8 + t],
+            at(1 - c, z, x),
+        )
+
+    def own_here():
+        return pltpu.make_async_copy(summed.at[own_part], own.at[slot], local_sems.at[1])
+
+    def home():
+        @pl.when(holds)
+        def _():
+            split_here().start()
+            for dx in (1, 2, 3):
+                to_row(dx, 0).start()
+
+        @pl.when(other)
+        def _():
+            for dx in range(4):
+                to_row(dx, 4).start()
+
+        @pl.when(stays)
+        def _():
+            own_here().start()
+
+        @pl.when(leaves)
+        def _():
+            to_owner(z).start()
+
+    here, there = y * 2 + zh, y * 2 + 1 - zh
+    front, back = pl.ds(0, GOT_ROWS // 2), pl.ds(GOT_ROWS // 2, GOT_ROWS // 2)
+
+    def step(index, source, place_at, target):
+        return copy(source, place_at, sends.at[index], recvs.at[index], target)
+
+    def over():
+        return step(0, own, out.at[here], across)
+
+    def kept():
+        return pltpu.make_async_copy(own, out.at[here], local_sems.at[2])
+
+    def ring(base, source, block):
+        def item(i):
+            part = (front, back, back, front)[i]
+            target = (y_up, y_down, y_up, y_down)[i]
+            return step(base + i, source.at[part], out.at[block, part], target)
+
+        return item
+
+    def relays(base, which):
+        below, above = ((y + 3) % 4) * 2 + which, ((y + 1) % 4) * 2 + which
+
+        def item(i):
+            place_at = (out.at[below, front], out.at[above, back])[i]
+            return step(base + 4 + i, place_at, place_at, (y_up, y_down)[i])
+
+        return item
+
+    def first_ring():
+        return ring(1, own, here)
+
+    def second_ring():
+        return ring(7, out.at[there], there)
+
+    def arrived():
+        @pl.when(holds)
+        def _():
+            split_here().wait()
+            for dx in (1, 2, 3):
+                to_row(dx, 0).wait_recv()
+            for dx in range(4):
+                from_row(dx).wait_recv()
+
+            @pl.when(z == layer)
+            def _():
+                own_here().wait()
+                from_owner(1 - layer).wait_recv()
+
+            @pl.when(z != layer)
+            def _():
+                from_owner(0).wait_recv()
+                from_owner(1).wait_recv()
+
+            kept().start()
+            over().start()
+            for i in range(4):
+                first_ring()(i).start()
+
+    def pass_first():
+        @pl.when(holds)
+        def _():
+            for i in range(2):
+                first_ring()(i).wait_recv()
+                relays(1, zh)(i).start()
+            over().wait_recv()
+            for i in range(4):
+                second_ring()(i).start()
+
+    def pass_second():
+        @pl.when(holds)
+        def _():
+            for i in range(2):
+                second_ring()(i).wait_recv()
+                relays(7, 1 - zh)(i).start()
+
+    def end():
+        @pl.when(holds)
+        def _():
+            rounds = ((first_ring(), relays(1, zh)), (second_ring(), relays(7, 1 - zh)))
+            for direct, relayed in rounds:
+                for i in (2, 3):
+                    direct(i).wait_recv()
+                for i in range(2):
+                    relayed(i).wait_recv()
+            over().wait_send()
+            for direct, relayed in rounds:
+                for i in range(4):
+                    direct(i).wait_send()
+                for i in range(2):
+                    relayed(i).wait_send()
+            kept().wait()
+            for dx in (1, 2, 3):
+                to_row(dx, 0).wait_send()
+
+        @pl.when(other)
+        def _():
+            for dx in range(4):
+                to_row(dx, 4).wait_send()
+
+        @pl.when(leaves)
+        def _():
+            to_owner(z).wait_send()
+
+    return home, arrived, pass_first, pass_second, end
+
+
+def spread_beside(layer, summed, out, refs):
+    c, z, x = place()
+    r = lax.axis_index("replica")
+    y_up, y_down, _, _ = grid_place()[2]
+    across = {"section": c, "shard": z * 4 + x, "replica": (r // 2) * 2 + 1 - r % 2}
+    friends = [at(c, z, (x + 2) % 4)] + [at(1 - c, z, (x + dx) % 4) for dx in (1, 2, 3)]
+    friends += [at(c, 1 - z, x), at(1 - c, 1 - z, x), y_up, y_down, across]
+    home, arrived, pass_first, pass_second, end = spread_stages(layer, summed, out, *refs)
+
+    def finish():
+        pass_second()
+        end()
+
+    return friends, home, arrived, pass_first, finish
+
+
+def reduce_kernel(pieces, out, summed, *refs):
+    c, z, x = place()
+    r = lax.axis_index("replica")
+    across = {"section": c, "shard": z * 4 + x, "replica": (r // 2) * 2 + 1 - r % 2}
+    greet(list(grid_place()[2]) + [across, at(1 - c, 1 - z, x)] + team_mates())
+    spread_refs, ring_refs = refs[:6], refs[6:]
+    middle, turn, finish = layer_rings(pieces, summed, *ring_refs)
     middle()
     turn()
     finish()
-
-    me = c * 4 + x
-    mine = pl.ds(pl.multiple_of(me * 144, 16), 144)
-    own_part = pl.ds(SPLIT_ROWS, OWN_ROWS)
-
-    def home_part(t):
-        return own.at[pl.ds(pl.multiple_of(8 * 144 + t * OWN_ROWS, 16), OWN_ROWS)]
-
-    def split_part(tc, tx):
-        return summed.at[tc, pl.ds(pl.multiple_of(tx * 144, 16), 144)]
-
-    keep = pltpu.make_async_copy(split_part(c, x), own.at[mine], local_sems.at[0])
-    keep.start()
-    copies = []
-    for index, (dc, dx) in enumerate(TEAM_STEPS):
-        tc, tx = (c + dc) % 2, (x + dx) % 4
-        copies.append(
-            remote(split_part(tc, tx), own.at[mine], home_send, home_recv, index, at(tc, z, tx))
-        )
-
-    def same_layer():
-        return pltpu.make_async_remote_copy(
-            src_ref=summed.at[c, own_part],
-            dst_ref=home_part(z),
-            send_sem=home_send.at[7],
-            recv_sem=home_recv.at[7],
-            device_id=at(c, 1 - z, x),
-            device_id_type=MESH,
-        )
-
-    def same_here():
-        return pltpu.make_async_copy(summed.at[c, own_part], home_part(z), local_sems.at[1])
-
-    def other_layer(t):
-        return pltpu.make_async_remote_copy(
-            src_ref=summed.at[1 - c, own_part],
-            dst_ref=home_part(z),
-            send_sem=home_send.at[8],
-            recv_sem=home_recv.at[8 + t],
-            device_id=at(1 - c, c, x),
-            device_id_type=MESH,
-        )
-
-    @pl.when(z == c)
-    def _():
-        same_here().start()
-
-    @pl.when(z != c)
-    def _():
-        same_layer().start()
-
-    other_layer(z).start()
-    for copy in copies:
-        copy.wait_recv()
-
-    @pl.when(z == c)
-    def _():
-        same_here().wait()
-        same_layer().wait_recv()
-
-    @pl.when(z != c)
-    def _():
-        other_layer(0).wait_recv()
-        other_layer(1).wait_recv()
-        same_layer().wait_send()
-
-    other_layer(z).wait_send()
-    for copy in copies:
-        copy.wait_send()
-    keep.wait()
-
-    here = y * 2 + zh
-    front, back = pl.ds(0, GOT_ROWS // 2), pl.ds(GOT_ROWS // 2, GOT_ROWS // 2)
-    local = pltpu.make_async_copy(own, out.at[here], local_sems.at[2])
-    local.start()
-
-    def send(src, dst, index, target):
-        return remote(src, dst, spread_send, spread_recv, index, target)
-
-    over = send(own, out.at[here], 0, across)
-
-    def spread(base, source, block):
-        return [
-            send(source.at[front], out.at[block, front], base, y_up),
-            send(source.at[back], out.at[block, back], base + 1, y_down),
-            send(source.at[back], out.at[block, back], base + 2, y_up),
-            send(source.at[front], out.at[block, front], base + 3, y_down),
-        ]
-
-    def forward(base, which, sent):
-        below, above = ((y + 3) % 4) * 2 + which, ((y + 1) % 4) * 2 + which
-        sent[0].wait_recv()
-        sent.append(send(out.at[below, front], out.at[below, front], base + 4, y_up))
-        sent[1].wait_recv()
-        sent.append(send(out.at[above, back], out.at[above, back], base + 5, y_down))
-
-    sent = spread(1, own, here)
-    forward(1, zh, sent)
-    over.wait_recv()
-    there = y * 2 + 1 - zh
-    more = spread(7, out.at[there], there)
-    forward(7, 1 - zh, more)
-    for copy in sent[2:] + more[2:]:
-        copy.wait_recv()
-    for copy in [over] + sent + more:
-        copy.wait_send()
-    local.wait()
-
-
-def reduce_grads(pieces, second_layer):
-    dma = pltpu.SemaphoreType.DMA
+    for stage in spread_stages(0, summed, out, *spread_refs):
+        stage()
+
+
+def reduce_grads(pieces):
     return pl.pallas_call(
         reduce_kernel,
         out_shape=jax.ShapeDtypeStruct((8, GOT_ROWS, 128), BF),
-        in_specs=[VMEM, VMEM],
+        in_specs=[VMEM],
         out_specs=VMEM,
-        scratch_shapes=[
-            pltpu.VMEM((2, ROWS, 128), BF),
-            pltpu.VMEM((GOT_ROWS, 128), BF),
-            dma((9,)),
-            dma((10,)),
-            dma((3,)),
-            dma((13,)),
-            dma((13,)),
-        ]
-        + rings_scratch(),
+        scratch_shapes=[pltpu.VMEM((ROWS, 128), BF)] + spread_scratch() + rings_scratch(),
         compiler_params=pltpu.CompilerParams(
             collective_id=4, has_side_effects=True, vmem_limit_bytes=LIMIT
         ),
-    )(pieces, second_layer)
-
-
-def shared_kernel(rings, *refs):
-    if rings:
-        pieces, *refs = refs
+    )(pieces)
+
+
+def shared_kernel(*refs):
     attended, middle_low, normed_all, qkv_grad, normed, last_grad, vectors, rows = refs[:8]
     refs = refs[8:]
-    if rings:
-        out, out_rows, out_pieces, *refs = refs
-    else:
-        out, out_rows, *refs = refs
-    products, last_keys, last_queries, parts, home_send, home_recv, home_local, *refs = refs
-    scatter_refs, ring_refs = refs[:10], refs[10:]
+    out, out_rows, products, last_keys, last_queries, parts, *refs = refs
+    home_send, home_recv, home_local, *scatter_refs = refs
     c, z, x = place()
     products[...] = dot_tn(attended[...], middle_low[...])
     last_keys[...] = dot_tn(normed_all[...], qkv_grad[:, 384:512])
@@ -1068,12 +1116,7 @@
             device_id_type=MESH,
         )
 
-    stages = []
-
     def begin():
-        if rings:
-            stages.extend(layer_rings(pieces, out_pieces, *ring_refs))
-
         @pl.when(z == c)
         def _():
             same_here().start()
@@ -1084,15 +1127,7 @@
 
         other_layer(z).start()
 
-    def during():
-        if rings:
-            stages[0]()
-            stages[1]()
-
     def end():
-        if rings:
-            stages[2]()
-
         @pl.when(z == c)
         def _():
             same_here().wait()
@@ -1107,15 +1142,6 @@
         other_layer(z).wait_send()
 
     friends = [at(c, 1 - z, x), at(1 - c, 1 - z, x)]
-    if rings:
-        y, zf, (y_up, y_down, z_up, z_down) = grid_place()
-        z_other = {
-            "section": c,
-            "shard": (1 - z) * 4 + x,
-            "replica": y * 2 + ((zf + 3 + 2 * z) % 4) // 2,
-        }
-        friends += [y_up, y_down, z_other]
-
     def mine_part(where, part):
         return parts[c * 4 + where, part, :].astype(F32)
 
@@ -1124,27 +1150,22 @@
         lambda where: parts.at[(1 - c) * 4 + where],
         mine_part,
         lambda where: None,
-        (friends, begin, during, end),
+        (friends, begin, nothing, nothing, end),
         out,
         *scatter_refs,
     )
 
 
-def shared_scatter(operands, pieces):
-    rings = pieces is not None
+def shared_scatter(*operands):
     dma = pltpu.SemaphoreType.DMA
-    out_shape = (
-        jax.ShapeDtypeStruct((144, 1280), F32),
-        jax.ShapeDtypeStruct((2, 128, D), BF),
-    )
-    if rings:
-        operands = (pieces,) + operands
-        out_shape += (jax.ShapeDtypeStruct((ROWS, 128), BF),)
     return pl.pallas_call(
-        functools.partial(shared_kernel, rings),
-        out_shape=out_shape,
-        in_specs=[VMEM] * len(operands),
-        out_specs=(VMEM,) * len(out_shape),
+        shared_kernel,
+        out_shape=(
+            jax.ShapeDtypeStruct((144, 1280), F32),
+            jax.ShapeDtypeStruct((2, 128, D), BF),
+        ),
+        in_specs=[VMEM] * 8,
+        out_specs=(VMEM, VMEM),
         scratch_shapes=[
             pltpu.VMEM((1152, 1152), F32),
             pltpu.VMEM((D, 128), F32),
@@ -1154,10 +1175,9 @@
             dma((3,)),
             dma,
         ]
-        + scatter_scratch(144, 1280, 64)
-        + (rings_scratch() if rings else []),
+        + scatter_scratch(144, 1280, 64),
         compiler_params=pltpu.CompilerParams(
-            collective_id=11 if rings else 6, has_side_effects=True, vmem_limit_bytes=LIMIT
+            collective_id=6, has_side_effects=True, vmem_limit_bytes=LIMIT
         ),
     )(*operands)
 
@@ -1214,7 +1234,27 @@
     )(*operands)
 
 
-def assemble_kernel(got, qkv, out_w, up, down, vectors, shared):
+def assemble_kernel(
+    first_got, second_got, qkv, out_w, up, down, vectors, shared, got, got_sem
+):
+    c = lax.axis_index("section")
+
+    @pl.when(c == 0)
+    def _():
+        pltpu.make_async_copy(first_got, got, got_sem).start()
+
+    @pl.when(c == 1)
+    def _():
+        pltpu.make_async_copy(second_got, got, got_sem).start()
+
+    @pl.when(c == 0)
+    def _():
+        pltpu.make_async_copy(first_got, got, got_sem).wait()
+
+    @pl.when(c == 1)
+    def _():
+        pltpu.make_async_copy(second_got, got, got_sem).wait()
+
     for q in range(8):
         for chunk in range(8):
             block = got[chunk, 144 * q : 144 * q + 144, :].astype(F32)[:136]
@@ -1246,16 +1286,20 @@
     qkv[:, 2 * D + 1024 : 3 * D] = shared[0, 0:136, 64:128]
 
 
-def assemble(got):
+def assemble(first_got, second_got):
     shapes = ((136, 3 * D), (136, D), (136, FF), (544, D), (8, 1280))
     return pl.pallas_call(
         assemble_kernel,
         out_shape=tuple(jax.ShapeDtypeStruct(shape, F32) for shape in shapes),
-        in_specs=[VMEM],
+        in_specs=[pl.BlockSpec(memory_space=pl.ANY)] * 2,
         out_specs=(VMEM,) * 5,
-        scratch_shapes=[pltpu.VMEM((10, 144, 128), F32)],
+        scratch_shapes=[
+            pltpu.VMEM((10, 144, 128), F32),
+            pltpu.VMEM((8, GOT_ROWS, 128), BF),
+            pltpu.SemaphoreType.DMA,
+        ],
         compiler_params=pltpu.CompilerParams(vmem_limit_bytes=LIMIT),
-    )(got)
+    )(first_got, second_got)
 
 
 def dot_nt(left, right):
@@ -1287,8 +1331,47 @@
 STEP = 256
 
 
-def attend_kernel(projected, last_query, attended, attended_last):
+def team_mates():
     c, z, x = place()
+    return [at((c + dc) % 2, z, (x + dx) % 4) for dc, dx in TEAM_STEPS]
+
+
+def lanes_of(q):
+    return pl.ds(pl.multiple_of(q * 128, 128), 128)
+
+
+def attend_kernel(projected, last_query, out, attended, send_sems, recv_sems, local_sem):
+    c, z, x = place()
+    me = c * 4 + x
+    mates = team_mates()
+    arrive(mates)
+
+    def copy_to(q):
+        return pltpu.make_async_remote_copy(
+            src_ref=attended.at[q],
+            dst_ref=out.at[:, lanes_of(me)],
+            send_sem=send_sems.at[q],
+            recv_sem=recv_sems.at[me],
+            device_id=at(q // 4, z, q % 4),
+            device_id_type=MESH,
+        )
+
+    def copy_from(q):
+        return pltpu.make_async_remote_copy(
+            src_ref=attended.at[q],
+            dst_ref=out.at[:, lanes_of(q)],
+            send_sem=send_sems.at[q],
+            recv_sem=recv_sems.at[q],
+            device_id=at(q // 4, z, q % 4),
+            device_id_type=MESH,
+        )
+
+    def keep(q):
+        return pltpu.make_async_copy(attended.at[q], out.at[:, lanes_of(q)], local_sem)
+
+    both = projected[:, 384:512]
+    soft = softmax_rows(dot_nt(last_query[...] * 0.125, both), me * 128).astype(BF)
+    out[:, 1024:1152] = dot(soft, lane_half(both, 1)).astype(BF)
     for start in range(0, 1024, STEP):
         size = start + STEP
         query = projected[start:size, 0:128] * 0.125
@@ -1298,31 +1381,91 @@
             values = lane_half(projected[0:size, 256:384], head)
             soft = softmax_rows(dot_nt(query, keys), start).astype(BF)
             total = total + dot(soft, values)
-        attended[start:size, :] = total.astype(BF)
-    both = projected[:, 384:512]
-    soft = softmax_rows(dot_nt(last_query[...] * 0.125, both), (c * 4 + x) * 128).astype(BF)
-    attended_last[...] = dot(soft, lane_half(both, 1)).astype(BF)
+        if start == 0:
+            meet(mates)
+        for q in range(start // 128, size // 128):
+            begin = q * 128 - start
+            attended[q] = total[begin : begin + 128].astype(BF)
+
+            @pl.when(me == q)
+            def _():
+                keep(q).start()
+
+            @pl.when(me != q)
+            def _():
+                copy_to(q).start()
+
+    for q in range(8):
+
+        @pl.when(me == q)
+        def _():
+            keep(q).wait()
+
+        @pl.when(me != q)
+        def _():
+            copy_from(q).wait_recv()
+            copy_to(q).wait_send()
 
 
 def attend(projected, last_query):
     return pl.pallas_call(
         attend_kernel,
-        out_shape=(
-            jax.ShapeDtypeStruct((1024, 128), BF),
-            jax.ShapeDtypeStruct((128, 128), BF),
+        out_shape=jax.ShapeDtypeStruct((128, 1152), BF),
+        in_specs=[VMEM, VMEM],
+        out_specs=VMEM,
+        scratch_shapes=[
+            pltpu.VMEM((8, 128, 128), BF),
+            pltpu.SemaphoreType.DMA((8,)),
+            pltpu.SemaphoreType.DMA((8,)),
+            pltpu.SemaphoreType.DMA,
+        ],
+        compiler_params=pltpu.CompilerParams(
+            collective_id=1, has_side_effects=True, vmem_limit_bytes=LIMIT
         ),
-        in_specs=[VMEM, VMEM],
-        out_specs=(VMEM, VMEM),
-        compiler_params=pltpu.CompilerParams(vmem_limit_bytes=LIMIT),
     )(projected, last_query)
 
 
 def attend_back_kernel(
-    projected, last_query, grad, last_grad, out, out_last, key_total, value_total
+    projected,
+    last_query,
+    rows,
+    out,
+    out_last,
+    grad,
+    key_total,
+    value_total,
+    send_sems,
+    recv_sems,
+    local_sem,
 ):
     c, z, x = place()
+    me = c * 4 + x
+    mates = team_mates()
+    arrive(mates)
+    local = pltpu.make_async_copy(rows.at[:, lanes_of(me)], grad.at[row_block(me)], local_sem)
+    local.start()
+    meet(mates)
+    send = sender(send_sems, recv_sems)
+    copies = []
+    for index, (dc, dx) in enumerate(TEAM_STEPS):
+        tc, tx = (c + dc) % 2, (x + dx) % 4
+        copies.append(
+            send(rows.at[:, lanes_of(tc * 4 + tx)], grad.at[row_block(me)], index, at(tc, z, tx))
+        )
     key_total[...] = jnp.zeros_like(key_total)
     value_total[...] = jnp.zeros_like(value_total)
+    both = projected[:, 384:512]
+    query = last_query[...] * 0.125
+    last_grad = rows[:, 1024:1152]
+    soft = softmax_rows(dot_nt(query, both), me * 128)
+    grad_soft = dot_nt(last_grad, both)
+    inner = jnp.sum(soft * grad_soft, axis=1, keepdims=True)
+    grad_scores = (soft * (grad_soft - inner)).astype(BF)
+    out_last[...] = (dot(grad_scores, lane_half(both, 0)) * 0.125).astype(BF)
+    out[:, 384:512] = (dot_tn(grad_scores, query) + dot_tn(soft.astype(BF), last_grad)).astype(BF)
+    local.wait()
+    for copy in copies:
+        copy.wait_recv()
     for start in range(0, 1024, STEP):
         size = start + STEP
         query = projected[start:size, 0:128] * 0.125
@@ -1341,30 +1484,31 @@
         out[start:size, 0:128] = (total * 0.125).astype(BF)
     out[:, 128:256] = key_total[...].astype(BF)
     out[:, 256:384] = value_total[...].astype(BF)
-    both = projected[:, 384:512]
-    query = last_query[...] * 0.125
-    soft = softmax_rows(dot_nt(query, both), (c * 4 + x) * 128)
-    grad_soft = dot_nt(last_grad[...], both)
-    inner = jnp.sum(soft * grad_soft, axis=1, keepdims=True)
-    grad_scores = (soft * (grad_soft - inner)).astype(BF)
-    out_last[...] = (dot(grad_scores, lane_half(both, 0)) * 0.125).astype(BF)
-    out[:, 384:512] = (dot_tn(grad_scores, query) + dot_tn(soft.astype(BF), last_grad[...])).astype(
-        BF
-    )
-
-
-def attend_back(projected, last_query, grad, last_grad):
+    for copy in copies:
+        copy.wait_send()
+
+
+def attend_back(projected, last_query, rows):
     return pl.pallas_call(
         attend_back_kernel,
         out_shape=(
             jax.ShapeDtypeStruct((1024, 512), BF),
             jax.ShapeDtypeStruct((128, 128), BF),
         ),
-        in_specs=[VMEM] * 4,
+        in_specs=[VMEM] * 3,
         out_specs=(VMEM, VMEM),
-        scratch_shapes=[pltpu.VMEM((1024, 128), F32), pltpu.VMEM((1024, 128), F32)],
-        compiler_params=pltpu.CompilerParams(vmem_limit_bytes=LIMIT),
-    )(projected, last_query, grad, last_grad)
+        scratch_shapes=[
+            pltpu.VMEM((1024, 128), BF),
+            pltpu.VMEM((1024, 128), F32),
+            pltpu.VMEM((1024, 128), F32),
+            pltpu.SemaphoreType.DMA((7,)),
+            pltpu.SemaphoreType.DMA((7,)),
+            pltpu.SemaphoreType.DMA,
+        ],
+        compiler_params=pltpu.CompilerParams(
+            collective_id=2, has_side_effects=True, vmem_limit_bytes=LIMIT
+        ),
+    )(projected, last_query, rows)
 
 
 def norm_forward(hidden, gain, offset):
@@ -1401,21 +1545,21 @@
         0,
         normed,
         w["qkv"],
-        w["qkv_bias"].reshape(1, 512),
+        (w["qkv_bias"].reshape(1, 512),),
         (jax.ShapeDtypeStruct((1024, 512), BF),),
     )
     normed_all = normed_all.reshape(1024, D)
     last_query = (dot(normed, w["last_query"]) + w["last_bias"]).astype(BF)
-    heads, last = attend(projected, last_query)
-    attended = heads_to_rows(heads.reshape(8, 128, 128), last)
-    middle = hidden + dot(attended, w["out"]) + w["out_bias"]
+    attended = attend(projected, last_query)
+    packed = jnp.concatenate([attended[:, :1024], attended[:, 1088:]], axis=1)
+    middle = hidden + dot(packed, w["out"]) + w["out_bias"]
     second, unit_two, inverse_two = norm_forward(middle, w["gain_two"], w["bias_two"])
     second_all, upper, activated = team_gather(
         gather_up_kernel,
         7,
         second.astype(BF),
         w["up"],
-        w["up_bias"].reshape(1, 544),
+        (w["up_bias"].reshape(1, 544),),
         (jax.ShapeDtypeStruct((1024, 544), F32), jax.ShapeDtypeStruct((1024, 544), BF)),
     )
     second_all = second_all.reshape(1024, D)
@@ -1437,32 +1581,34 @@
     return output, saved
 
 
-def layer_backward(grad_out, grad_low_all, w, kept, q):
+def layer_backward(grad_out, grad_low_all, w, kept, q, pieces):
     grad_low = grad_out.astype(BF)
     if grad_low_all is None:
-        grad_low_all, up_grad = team_gather(
+        grad_low_all, up_grad, summed = team_gather(
             gather_back_kernel,
             8,
             grad_low,
             w["down"],
-            kept["upper"],
-            (jax.ShapeDtypeStruct((1024, 544), BF),),
+            (kept["upper"], pieces),
+            (jax.ShapeDtypeStruct((1024, 544), BF), jax.ShapeDtypeStruct((ROWS, 128), BF)),
+            rings_scratch(),
         )
         grad_low_all = grad_low_all.reshape(1024, D)
+        grad_second, got = product_scatter(dot_nt, 11, up_grad, w["up"], summed)
     else:
         slope = gelu_pair(kept["upper"])[1]
         up_grad = (dot_nt(grad_low_all, w["down"]) * slope).astype(BF)
-    grad_second = product_scatter(dot_nt, 9, up_grad, w["up"])
+        grad_second, got = product_scatter(dot_nt, 9, up_grad, w["up"]), None
     grad_in, gain_two, bias_two = norm_backward(
         grad_second, kept["unit_two"], kept["inverse_two"], w["gain_two"]
     )
     grad_middle = grad_out + grad_in
     middle_low = grad_middle.astype(BF)
     attended_grad = dot_nt(middle_low, w["out"]).astype(BF)
-    heads_grad = rows_to_heads(attended_grad).reshape(1024, 128)
-    qkv_grad, last_grad = attend_back(
-        kept["projected"], kept["last_query"], heads_grad, attended_grad[:, 1024:]
-    )
+    attended_grad = jnp.concatenate(
+        [attended_grad[:, :1024], jnp.zeros((128, 64), BF), attended_grad[:, 1024:]], axis=1
+    )
+    qkv_grad, last_grad = attend_back(kept["projected"], kept["last_query"], attended_grad)
     grad_normed = product_scatter(dot_nt, 10, qkv_grad, w["qkv"])
     grad_normed = grad_normed + dot_nt(last_grad, w["last_query"])
     grad_in, gain_one, bias_one = norm_backward(
@@ -1516,7 +1662,7 @@
         kept["activated"],
         grad_low_all,
     )
-    return grad_input, operands, split
+    return grad_input, operands, split, got
 
 
 BOTH = ("section", "shard")
@@ -1557,7 +1703,7 @@
         return jnp.where(c == z, array, lax.ppermute(array, BOTH, swap))
 
     def by_z(own, other):
-        return jnp.where(z == 0, jnp.stack([own, other]), jnp.stack([other, own]))
+        return jnp.where(z == 0, own, other), jnp.where(z == 0, other, own)
 
     small = jnp.concatenate(
         [
@@ -1599,8 +1745,9 @@
     second_blocks = lax.all_gather(late, "replica", axis=0)
     own_out = lax.all_gather(w_out[0], "shard", axis=0, tiled=True)
     partner_out = lax.ppermute(own_out, "section", [(0, 1), (1, 0)])
-    all_out = jnp.where(
-        c == 0, jnp.stack([own_out, partner_out]), jnp.stack([partner_out, own_out])
+    all_out = (
+        jnp.where(c == 0, own_out, partner_out),
+        jnp.where(c == 0, partner_out, own_out),
     )
     cuts = (
         first_blocks.reshape(4, 2, 2, 4, 144, 128)
@@ -1633,13 +1780,12 @@
                 qv[2 * D - 64 :],
             ]
         )
-        out = all_out[layer]
         return dict(
             qkv=jnp.concatenate([cut[:, :384], shared[:, :128]], axis=1),
             last_query=shared[:, 128:],
             qkv_bias=qkv_bias,
             last_bias=jnp.concatenate([qv[1024:D], none[:64]]),
-            out=jnp.concatenate([out[:1024], jnp.zeros((64, D), BF), out[1024:]]),
+            out=all_out[layer],
             out_bias=six[0:1],
             gain_one=six[1:2],
             bias_one=six[2:3],
@@ -1656,21 +1802,19 @@
     top_grad = top_grad.astype(F32)
     out_first, kept_first = layer_forward(hidden, weights[0])
     out_second, kept_second = layer_forward(out_first.astype(BF).astype(F32), weights[1])
-    grad_second, operands, split = layer_backward(
-        top_grad, top_grad_all, weights[1], kept_second, q
+    grad_second, operands, split, _ = layer_backward(
+        top_grad, top_grad_all, weights[1], kept_second, q, None
     )
     rows = jnp.stack([out_first.astype(BF), out_second.astype(BF)])
-    shared, section_out = shared_scatter(operands + (rows,), None)
+    shared, section_out = shared_scatter(*operands, rows)
     pieces = grad_pieces(*split, shared)
-    grad_first, operands, split = layer_backward(
-        grad_second.astype(BF).astype(F32), None, weights[0], kept_first, q
+    grad_first, operands, split, second_got = layer_backward(
+        grad_second.astype(BF).astype(F32), None, weights[0], kept_first, q, pieces
     )
     rows = jnp.stack([grad_first.astype(BF), grad_second.astype(BF)])
-    shared, input_grad, second_layer = shared_scatter(operands + (rows,), pieces)
-    pieces = grad_pieces(*split, shared)
-    grad_qkv, grad_out_w, grad_up, grad_down, vectors = assemble(
-        reduce_grads(pieces, second_layer)
-    )
+    shared, input_grad = shared_scatter(*operands, rows)
+    first_got = reduce_grads(grad_pieces(*split, shared))
+    grad_qkv, grad_out_w, grad_up, grad_down, vectors = assemble(first_got, second_got)
     section_out = section_out.astype(F32)[None, :, None]
     input_grad = input_grad.astype(F32)[None, :, None]
     vec = vectors.reshape(-1)

time: 640 us -> 613 us (0.958)
  Pallas kernels: 509 us -> 487 us
  local copies, waits for them, and re-layouts: 57 us -> 49.8 us
    pallas_call x14 -> x10, Pallas kernels: 231 us -> 174 us  [the longest x6 112 us: product_scatter(): pl.pallas_call(functools.partial(product_scatter_kernel, product, spreads...]
    pallas_call x5, Pallas kernels: 95.4 us -> 119 us  [team_gather(): pl.pallas_call(kernel, out_shape=(jax.ShapeDtypeStruct((8, rows, columns)...]
    pallas_call x2, Pallas kernels: 20 us -> 42.6 us  [attend_back(): pl.pallas_call(attend_back_kernel, out_shape=(jax.ShapeDtypeStruct((1024,...]
    pallas_call x1, Pallas kernels: 73.6 us -> 60.3 us  [reduce_grads(): pl.pallas_call(reduce_kernel, out_shape=jax.ShapeDtypeStruct((8, GOT_ROWS...]
    unnamed x155 -> x93, local copies, waits for them, and re-layouts: 13.5 us -> 9.79 us
  transfers between devices with their start and end apart: 6 -> 6, of which waited for: 0 -> 1; matrix products, arithmetic and copies ran while one was open for 10% -> 9% of each run, Pallas kernels for 29% -> 30%
where the time goes in v3:
time: 613 us; the launch traced here: 602 us
  Pallas kernels  487 us (79%)
  local copies, waits for them, and re-layouts  49.8 us (8%)
  other arithmetic  25.6 us (4%)
  matrix products  20.3 us (3%)
  between operations  15.2 us (2%)
    pallas_call x5, Pallas kernels, team_gather(): pl.pallas_call(kernel, out_shape=(jax.ShapeDtypeStruct((8, rows, columns)...  119 us
    pallas_call x6, Pallas kernels, product_scatter(): pl.pallas_call(functools.partial(product_scatter_kernel, product, spreads...  112 us
    pallas_call x1, Pallas kernels, spread_weights(): pl.pallas_call(weights_kernel, out_shape=(jax.ShapeDtypeStruct((4, 4, 4,...  63.2 us
    pallas_call x1, Pallas kernels, reduce_grads(): pl.pallas_call(reduce_kernel, out_shape=jax.ShapeDtypeStruct((8, GOT_ROWS...  60.3 us
    pallas_call x2, Pallas kernels, shared_scatter(): pl.pallas_call(shared_kernel, out_shape=(jax.ShapeDtypeStruct((144, 1280)...  44.7 us
    pallas_call x2, Pallas kernels, attend_back(): pl.pallas_call(attend_back_kernel, out_shape=(jax.ShapeDtypeStruct((1024,...  42.6 us
    pallas_call x2, Pallas kernels, grad_pieces(): pl.pallas_call(pieces_kernel, out_shape=jax.ShapeDtypeStruct((4, 4, ROWS,...  21.9 us
    pallas_call x2, Pallas kernels, attend(): pl.pallas_call(attend_kernel, out_shape=jax.ShapeDtypeStruct((128, 1152),...  17.2 us
  transfers between devices with their start and end apart: 6, of which 1 were waited for; matrix products, arithmetic and copies ran while one was open for 9% of the time, Pallas kernels for 30%

profile of v3, /device:TPU:16, one launch (start us, length us, event | category | flops | bytes accessed | tf_op | source)
XLA Modules:
  0.0 602.1 jit_solution(3311397538510384625)
XLA Ops:
  8.0 3.5 reshape_squeeze.15
  18.3 63.2 %shard_map.245 = (bf16[4,4,4,144,128]{4,3,2,1,0:T(8,128)(2,1)}, bf16[8,144,128]{2,1,0:T(8,128)(2,1)}, bf16[2,8,144,256]{3,2,1,0:T(8,128)(2,1)}, bf16[128,1088]{1,0:T(8,128)(2,1)}, bf16[128,1088]{1,0:T(8,128)(2,1)}) custom-call(bf16[8,144,128]{2,1,0:T(8,128)(2,1)} %pad_dynamic-slice_fusion.late, bf16[144,256]{1,0:T(8,128)(2,1)} %pad_maximum_fusion.4.common, ...), custom_call_target="tpu_custom_call" | custom-call | tf_op jit(solution)/shard_map/pallas_call | solution.py:603
  81.7 1.9 collective-permute-start.1
  83.6 1.4 slice_bitcast_fusion.3
  85.0 2.1 fusion.60
  89.0 2.4 copy.106
  91.4 1.5 slice.296
  93.0 2.8 reshape.246
  95.8 1.3 slice.297
  100.8 18.2 %shard_map.246 = (bf16[8,128,1088]{2,1,0:T(8,128)(2,1)}, bf16[1024,512]{1,0:T(8,128)(2,1)}) custom-call(bf16[128,1088]{1,0:T(8,128)(2,1)} %fusion.33.own.refs_4_, bf16[1088,512]{1,0:T(8,128)(2,1)} %pad_maximum_fusion.weight.right, f32[1,512]{1,0:T(1,128)} %bitcast.156), custom_call_target="tpu_custom_call" | custom-call | tf_op jit(solution)/shard_map/pallas_call | solution.py:187
  119.0 1.8 fusion.9.last_query
  120.8 8.6 %shard_map.247.refs_0_ = bf16[128,1152]{1,0:T(8,128)(2,1)} custom-call(bf16[1024,512]{1,0:T(8,128)(2,1)} %get-tuple-element.50.projected, bf16[128,128]{1,0:T(8,128)(2,1)} %fusion.9.last_query), custom_call_target="tpu_custom_call" | custom-call | tf_op jit(solution)/shard_map/pallas_call | solution.py:1411
  134.5 3.0 broadcast_select_fusion.3
  137.7 3.5 copy.105
  146.5 29.4 %shard_map.248 = (bf16[8,128,1088]{2,1,0:T(8,128)(2,1)}, f32[1024,544]{1,0:T(8,128)}, bf16[1024,544]{1,0:T(8,128)(2,1)}) custom-call(bf16[128,1088]{1,0:T(8,128)(2,1)} %add_convert_fusion.3.own, bf16[1088,544]{1,0:T(8,128)(2,1)} %slice.306.weight.right, f32[1,544]{1,0:T(1,128)} %reshape.250.bias), custom_call_target="tpu_custom_call" | custom-call | tf_op jit(solution)/shard_map/pallas_call | solution.py:187
  175.9 18.1 %shard_map.249 = f32[128,1088]{1,0:T(8,128)} custom-call(bf16[1024,544]{1,0:T(8,128)(2,1)} %get-tuple-element.51.left.activated, bf16[544,1088]{1,0:T(8,128)(2,1)} %get-tuple-element.161.right.weight), custom_call_target="tpu_custom_call" | custom-call | tf_op jit(solution)/shard_map/pallas_call | solution.py:334
  194.0 1.3 convert_reduce_fusion.4
  196.5 17.8 %shard_map.250 = (bf16[8,128,1088]{2,1,0:T(8,128)(2,1)}, bf16[1024,512]{1,0:T(8,128)(2,1)}) custom-call(bf16[128,1088]{1,0:T(8,128)(2,1)} %fusion.24.own.refs_4_, bf16[1088,512]{1,0:T(8,128)(2,1)} %pad_maximum_fusion.1.weight.right, f32[1,512]{1,0:T(1,128)} %bitcast.155), custom_call_target="tpu_custom_call" | custom-call | tf_op jit(solution)/shard_map/pallas_call | solution.py:187
  214.3 1.8 fusion.10.last_query
  216.1 8.6 %shard_map.251.refs_0_ = bf16[128,1152]{1,0:T(8,128)(2,1)} custom-call(bf16[1024,512]{1,0:T(8,128)(2,1)} %get-tuple-element.53.projected, bf16[128,128]{1,0:T(8,128)(2,1)} %fusion.10.last_query), custom_call_target="tpu_custom_call" | custom-call | tf_op jit(solution)/shard_map/pallas_call | solution.py:1411
  226.5 2.6 fusion.68
  230.3 19.1 %shard_map.252 = (bf16[8,128,1088]{2,1,0:T(8,128)(2,1)}, f32[1024,544]{1,0:T(8,128)}, bf16[1024,544]{1,0:T(8,128)(2,1)}) custom-call(bf16[128,1088]{1,0:T(8,128)(2,1)} %add_convert_fusion.1.own, bf16[1088,544]{1,0:T(8,128)(2,1)} %slice.323.weight.right, f32[1,544]{1,0:T(1,128)} %reshape.257.bias), custom_call_target="tpu_custom_call" | custom-call | tf_op jit(solution)/shard_map/pallas_call | solution.py:187
  249.4 6.6 %convert_reduce_fusion.1 = (f32[544]{0:T(1024)S(1)}, bf16[1024,544]{1,0:T(8,128)(2,1)}) fusion(f32[1024,544]{1,0:T(8,128)} %get-tuple-element.55, bf16[1024,1088]{1,0:T(8,128)(2,1)} %all-gather.6.cloned.1.call-done.low_all, bf16[544,1088]{1,0:T(8,128)(2,1)S(1)} %get-tuple-element.160.right), kind=kOutput, calls=%fused_computation.10 | convolution fusion | flops 1223851520 | bytes 6756480 | tf_op jit(solution)/shard_map/dot_general | solution.py:1306
  256.1 19.5 %shard_map.253 = f32[128,1088]{1,0:T(8,128)} custom-call(bf16[1024,544]{1,0:T(8,128)(2,1)} %get-tuple-element.194.left.up_grad, bf16[1088,544]{1,0:T(8,128)(2,1)} %slice.323.weight.right), custom_call_target="tpu_custom_call" | custom-call | tf_op jit(solution)/shard_map/pallas_call | solution.py:334
  275.6 1.4 multiply_reduce_fusion.2
  277.1 18.0 %shard_map.256 = f32[128,1088]{1,0:T(8,128)} custom-call(bf16[1024,544]{1,0:T(8,128)(2,1)} %get-tuple-element.59.left.activated, bf16[544,1088]{1,0:T(8,128)(2,1)} %copy-done.3), custom_call_target="tpu_custom_call" | custom-call | tf_op jit(solution)/shard_map/pallas_call | solution.py:334
  295.1 1.8 convert_reduce_fusion.9
  297.7 2.6 convolution_convert_fusion.1
  301.2 16.0 %shard_map.254 = (bf16[1024,512]{1,0:T(8,128)(2,1)}, bf16[128,128]{1,0:T(8,128)(2,1)}) custom-call(bf16[1024,512]{1,0:T(8,128)(2,1)} %get-tuple-element.53.projected, bf16[128,128]{1,0:T(8,128)(2,1)} %fusion.10.last_query, bf16[128,1152]{1,0:T(8,128)(2,1)} %concatenate.72.rows), custom_call_target="tpu_custom_call" | custom-call | tf_op jit(solution)/shard_map/pallas_call | solution.py:1492
  317.2 1.4 convert_reduce_fusion.3
  318.6 17.9 %shard_map.255 = f32[128,1088]{1,0:T(8,128)} custom-call(bf16[1024,512]{1,0:T(8,128)(2,1)} %get-tuple-element.57.left.refs_3_.qkv_grad, bf16[1088,512]{1,0:T(8,128)(2,1)} %pad_maximum_fusion.1.weight.right), custom_call_target="tpu_custom_call" | custom-call | tf_op jit(solution)/shard_map/pallas_call | solution.py:334
  337.8 1.5 fusion.26
  343.4 22.9 %shard_map.257 = (f32[144,1280]{1,0:T(8,128)}, bf16[2,128,1088]{2,1,0:T(8,128)(2,1)}) custom-call(bf16[128,1152]{1,0:T(8,128)(2,1)} %shard_map.251.refs_0_, bf16[128,1152]{1,0:T(8,128)(2,1)} %pad.33.refs_1_, bf16[1024,1088]{1,0:T(8,128)(2,1)} %bitcast.118, bf16[1024,512]{1,0:T(8,128)(2,1)} %get-tuple-element.57.left.refs_3_.qkv_grad, ...), custom_call_target="tpu_custom_call" | custom-call | tf_op jit(solution)/shard_map/pallas_call | solution.py:1161
  366.3 11.0 %shard_map.258.pieces = bf16[4,4,992,128]{3,2,1,0:T(8,128)(2,1)} custom-call(bf16[1024,1088]{1,0:T(8,128)(2,1)} %bitcast.119, bf16[1024,512]{1,0:T(8,128)(2,1)} %get-tuple-element.57.left.refs_3_.qkv_grad, bf16[1024,1088]{1,0:T(8,128)(2,1)} %bitcast.132, bf16[1024,544]{1,0:T(8,128)(2,1)} %get-tuple-element.194.left.up_grad, ...), custom_call_target="tpu_custom_call" | custom-call | tf_op jit(solution)/shard_map/pallas_call | solution.py:1227
  377.3 35.0 %shard_map.259 = (bf16[8,128,1088]{2,1,0:T(8,128)(2,1)}, bf16[1024,544]{1,0:T(8,128)(2,1)}, bf16[992,128]{1,0:T(8,128)(2,1)}) custom-call(bf16[128,1088]{1,0:T(8,128)(2,1)} %get-tuple-element.151.own, bf16[544,1088]{1,0:T(8,128)(2,1)} %get-tuple-element.161.right.weight, f32[1024,544]{1,0:T(8,128)} %get-tuple-element.61.upper, ...), custom_call_target="tpu_custom_call" | custom-call | tf_op jit(solution)/shard_map/pallas_call | solution.py:187
  412.3 20.8 %shard_map.260 = (f32[128,1088]{1,0:T(8,128)}, bf16[8,1984,128]{2,1,0:T(8,128)(2,1)}) custom-call(bf16[1024,544]{1,0:T(8,128)(2,1)} %get-tuple-element.64.left.up_grad, bf16[1088,544]{1,0:T(8,128)(2,1)} %slice.306.weight.right, bf16[992,128]{1,0:T(8,128)(2,1)} %get-tuple-element.65.refs_0_), custom_call_target="tpu_custom_call" | custom-call | tf_op jit(solution)/shard_map/pallas_call | solution.py:334
  433.1 1.5 multiply_reduce_fusion
  434.6 1.4 convert_reduce_fusion.8
  438.6 26.6 %shard_map.261 = (bf16[1024,512]{1,0:T(8,128)(2,1)}, bf16[128,128]{1,0:T(8,128)(2,1)}) custom-call(bf16[1024,512]{1,0:T(8,128)(2,1)} %get-tuple-element.50.projected, bf16[128,128]{1,0:T(8,128)(2,1)} %fusion.9.last_query, bf16[128,1152]{1,0:T(8,128)(2,1)} %concatenate.76.rows), custom_call_target="tpu_custom_call" | custom-call | tf_op jit(solution)/shard_map/pallas_call | solution.py:1492
  465.2 1.4 convert_reduce_fusion.2
  466.6 18.1 %shard_map.262 = f32[128,1088]{1,0:T(8,128)} custom-call(bf16[1024,512]{1,0:T(8,128)(2,1)} %get-tuple-element.68.left.refs_3_.qkv_grad, bf16[1088,512]{1,0:T(8,128)(2,1)} %pad_maximum_fusion.weight.right), custom_call_target="tpu_custom_call" | custom-call | tf_op jit(solution)/shard_map/pallas_call | solution.py:334
  486.4 1.5 fusion.35
  490.9 21.8 %shard_map.263 = (f32[144,1280]{1,0:T(8,128)}, bf16[2,128,1088]{2,1,0:T(8,128)(2,1)}) custom-call(bf16[128,1152]{1,0:T(8,128)(2,1)} %shard_map.247.refs_0_, bf16[128,1152]{1,0:T(8,128)(2,1)} %pad.35.refs_1_, bf16[1024,1088]{1,0:T(8,128)(2,1)} %bitcast.116, bf16[1024,512]{1,0:T(8,128)(2,1)} %get-tuple-element.68.left.refs_3_.qkv_grad, ...), custom_call_target="tpu_custom_call" | custom-call | tf_op jit(solution)/shard_map/pallas_call | solution.py:1161
  512.7 11.0 %shard_map.264.pieces = bf16[4,4,992,128]{3,2,1,0:T(8,128)(2,1)} custom-call(bf16[1024,1088]{1,0:T(8,128)(2,1)} %bitcast.117, bf16[1024,512]{1,0:T(8,128)(2,1)} %get-tuple-element.68.left.refs_3_.qkv_grad, bf16[1024,1088]{1,0:T(8,128)(2,1)} %bitcast.131, bf16[1024,544]{1,0:T(8,128)(2,1)} %get-tuple-element.64.left.up_grad, ...), custom_call_target="tpu_custom_call" | custom-call | tf_op jit(solution)/shard_map/pallas_call | solution.py:1227
  523.7 60.3 %shard_map.265.first_got = bf16[8,1984,128]{2,1,0:T(8,128)(2,1)} custom-call(bf16[4,4,992,128]{3,2,1,0:T(8,128)(2,1)} %shard_map.264.pieces), custom_call_target="tpu_custom_call" | custom-call | tf_op jit(solution)/shard_map/pallas_call | solution.py:1056
  584.0 5.7 shard_map.266
  591.3 1.4 copy.80
  592.8 1.4 copy.81
  (260 shorter events, 44.6 us)
Async XLA Ops:
  7.2 92.1 %all-gather.8.cloned.1.call-start = ((), (), s32[]{:S(2)}) async-start(), calls=%async_computation.1 | async-start | bytes 2820096 | tf_op jit(solution)/shard_map/all_gather | solution.py:1746
  7.9 129.8 %all-gather.10.cloned.1.call-start = ((), (), s32[]{:S(2)}) async-start(), calls=%async_computation.2 | async-start | bytes 2654208 | tf_op jit(solution)/shard_map/all_gather | solution.py:1745
  11.4 1.2 copy-start.13
  11.5 1.4 copy-start.31
  11.5 1.4 copy-start.28
  11.5 1.4 copy-start.32
  11.5 1.5 copy-start.33
  11.5 1.5 copy-start.34
  11.5 1.5 copy-start.35
  11.5 1.5 copy-start.36
  11.5 1.5 copy-start.37
  11.7 1.5 copy-start.16
  11.7 2.6 copy-start.17
  81.5 6.6 %copy-start.5 = (bf16[128,1088]{1,0:T(8,128)(2,1)S(1)}, bf16[128,1088]{1,0:T(8,128)(2,1)}, u32[]{:S(2)}) copy-start(bf16[128,1088]{1,0:T(8,128)(2,1)} %get-tuple-element.47) | copy-start | bytes 835588
  81.5 7.5 %copy-start.6 = (bf16[4,4,4,144,128]{4,3,2,1,0:T(8,128)(2,1)S(1)}, bf16[4,4,4,144,128]{4,3,2,1,0:T(8,128)(2,1)}, u32[]{:S(2)}) copy-start(bf16[4,4,4,144,128]{4,3,2,1,0:T(8,128)(2,1)} %get-tuple-element.49) | copy-start | bytes 7077892
  81.5 167.9 %all-gather.6.cloned.1.call-start = ((), (), s32[]{:S(2)}) async-start(), calls=%async_computation | async-start | bytes 2654208 | tf_op jit(solution)/shard_map/all_gather | solution.py:1744
  81.6 52.9 %collective-permute-start.2 = (bf16[544,1088]{1,0:T(8,128)(2,1)}, bf16[544,1088]{1,0:T(8,128)(2,1)}, u32[]{:S(2)}, u32[]{:S(2)}) collective-permute-start(bf16[544,1088]{1,0:T(8,128)(2,1)} %bitcast.138), channel_id=1, source_target_pairs={{0,32},{8,40},{16,48},{24,56},{32,96},{40,104},{48,112},{56,120},{... | collective-permute-start | bytes 3551240 | tf_op jit(solution)/shard_map/ppermute | solution.py:1759
  81.7 52.9 %collective-permute-start.1 = (bf16[544,1088]{1,0:T(8,128)(2,1)}, bf16[544,1088]{1,0:T(8,128)(2,1)}, u32[]{:S(2)}, u32[]{:S(2)}) collective-permute-start(bf16[544,1088]{1,0:T(8,128)(2,1)} %bitcast.139), channel_id=1, source_target_pairs={{32,64},{40,72},{48,80},{56,88},{64,32},{72,40},{80,48},{88,56},{3... | collective-permute-start | bytes 3551240 | tf_op jit(solution)/shard_map/ppermute | solution.py:1703
  87.1 31.9 %copy-start.7 = (bf16[1,8,136,256]{3,2,1,0:T(8,128)(2,1)}, bf16[1,8,136,256]{3,2,1,0:T(8,128)(2,1)S(1)}, u32[]{:S(2)}) copy-start(bf16[1,8,136,256]{3,2,1,0:T(8,128)(2,1)S(1)} %get-tuple-element.163) | copy-start | bytes 1671172
  87.1 4.3 copy-start.18
  93.0 4.1 slice-start.1
  95.8 2.5 copy-start.23
  95.8 2.5 copy-start.26
  95.8 2.5 copy-start.29
  98.3 32.0 %copy-start.1 = (bf16[1088,1024]{1,0:T(8,128)(2,1)S(1)}, bf16[1088,1024]{1,0:T(8,128)(2,1)}, u32[]{:S(2)}) copy-start(bf16[1088,1024]{1,0:T(8,128)(2,1)} %reshape.246) | copy-start | bytes 6684676
  99.3 45.2 %collective-permute-start = (bf16[1088,1088]{1,0:T(8,128)(2,1)}, bf16[1088,1088]{1,0:T(8,128)(2,1)}, u32[]{:S(2)}, u32[]{:S(2)}) collective-permute-start(bf16[1088,1088]{1,0:T(8,128)(2,1)} %bitcast.165), channel_id=1, source_target_pairs={{0,64},{64,0},{1,65},{65,1},{2,66},{66,2},{3,67},{67,3},{4,68},{68... | collective-permute-start | bytes 7102472 | tf_op jit(solution)/shard_map/ppermute | solution.py:1747
  120.8 10.8 %copy-start.19 = (f32[8,1632]{1,0:T(8,128)S(1)}, f32[8,1632]{1,0:T(8,128)}, u32[]{:S(2)}) copy-start(f32[8,1632]{1,0:T(8,128)} %copy-done.18) | copy-start | bytes 156676
  120.8 10.9 %copy-start.22 = (bf16[1,8,8,256]{3,2,1,0:T(8,128)(2,1)S(1)}, bf16[1,8,8,256]{3,2,1,0:T(8,128)(2,1)}, u32[]{:S(2)}) copy-start(bf16[1,8,8,256]{3,2,1,0:T(8,128)(2,1)} %get-tuple-element.164) | copy-start | bytes 98308
  129.4 3.4 copy-start.9
  137.5 111.9 %copy-start.3 = (bf16[544,1088]{1,0:T(8,128)(2,1)}, bf16[544,1088]{1,0:T(8,128)(2,1)S(1)}, u32[]{:S(2)}) copy-start(bf16[544,1088]{1,0:T(8,128)(2,1)S(1)} %get-tuple-element.160.right) | copy-start | bytes 3551236
  142.1 2.4 slice-start
  142.1 2.4 copy-start.27
  142.1 2.4 copy-start.38
  146.5 47.5 %copy-start.24 = (f32[1088]{0:T(1024)S(1)}, f32[1088]{0:T(1024)}, u32[]{:S(2)}) copy-start(f32[1088]{0:T(1024)} %get-tuple-element.144) | copy-start | bytes 13060
  194.0 20.4 %copy-start.10 = (bf16[1,8,136,256]{3,2,1,0:T(8,128)(2,1)S(1)}, bf16[1,8,136,256]{3,2,1,0:T(8,128)(2,1)}, u32[]{:S(2)}) copy-start(bf16[1,8,136,256]{3,2,1,0:T(8,128)(2,1)} %get-tuple-element.162) | copy-start | bytes 1671172
  275.6 19.5 %copy-start.2 = (f32[128,1088]{1,0:T(8,128)S(1)}, f32[128,1088]{1,0:T(8,128)}, u32[]{:S(2)}) copy-start(f32[128,1088]{1,0:T(8,128)} %shard_map.253) | copy-start | bytes 1671172
  275.6 19.5 %copy-start.12 = (bf16[128,1088]{1,0:T(8,128)(2,1)S(1)}, bf16[128,1088]{1,0:T(8,128)(2,1)}, u32[]{:S(2)}) copy-start(bf16[128,1088]{1,0:T(8,128)(2,1)} %get-tuple-element.54) | copy-start | bytes 835588
  295.1 2.6 copy-start.39
  301.2 36.6 %copy-start.11 = (bf16[1,8,136,256]{3,2,1,0:T(8,128)(2,1)S(1)}, bf16[1,8,136,256]{3,2,1,0:T(8,128)(2,1)}, u32[]{:S(2)}) copy-start(bf16[1,8,136,256]{3,2,1,0:T(8,128)(2,1)} %get-tuple-element.162) | copy-start | bytes 1671172
  317.2 19.4 %copy-start.21 = (bf16[128,128]{1,0:T(8,128)(2,1)S(1)}, bf16[128,128]{1,0:T(8,128)(2,1)}, u32[]{:S(2)}) copy-start(bf16[128,128]{1,0:T(8,128)(2,1)} %get-tuple-element.58) | copy-start | bytes 98308
  412.3 22.3 %copy-start.4 = (bf16[128,1088]{1,0:T(8,128)(2,1)S(1)}, bf16[128,1088]{1,0:T(8,128)(2,1)}, u32[]{:S(2)}) copy-start(bf16[128,1088]{1,0:T(8,128)(2,1)} %get-tuple-element.151.own) | copy-start | bytes 835588
  433.1 3.6 copy-start.40
  438.6 46.1 %copy-start = (bf16[1024,544]{1,0:T(8,128)(2,1)S(1)}, bf16[1024,544]{1,0:T(8,128)(2,1)}, u32[]{:S(2)}) copy-start(bf16[1024,544]{1,0:T(8,128)(2,1)} %get-tuple-element.64.left.up_grad) | copy-start | bytes 3342340
  465.2 19.8 %copy-start.20 = (bf16[128,128]{1,0:T(8,128)(2,1)S(1)}, bf16[128,128]{1,0:T(8,128)(2,1)}, u32[]{:S(2)}) copy-start(bf16[128,128]{1,0:T(8,128)(2,1)} %get-tuple-element.69) | copy-start | bytes 98308
  466.6 19.8 %copy-start.8 = (bf16[1,8,136,256]{3,2,1,0:T(8,128)(2,1)S(1)}, bf16[1,8,136,256]{3,2,1,0:T(8,128)(2,1)}, u32[]{:S(2)}) copy-start(bf16[1,8,136,256]{3,2,1,0:T(8,128)(2,1)} %copy-done.7) | copy-start | bytes 1671172
  466.6 19.8 %copy-start.30 = (f32[128]{0:T(128)S(1)}, f32[128]{0:T(128)}, u32[]{:S(2)}) copy-start(f32[128]{0:T(128)} %add_rsqrt_fusion.3) | copy-start | bytes 1540
  584.0 7.3 %copy-start.14 = (bf16[2,128,1088]{2,1,0:T(8,128)(2,1)S(1)}, bf16[2,128,1088]{2,1,0:T(8,128)(2,1)}, u32[]{:S(2)}) copy-start(bf16[2,128,1088]{2,1,0:T(8,128)(2,1)} %get-tuple-element.60) | copy-start | bytes 1671172
  589.7 3.0 copy-start.15
  (1 other events, 1.1 us)
Sparse Core Ops, SparseCore 0:
  9.7 52.1 all-gather.7
  81.6 55.9 all-gather.9
  139.4 30.6 all-gather.5

commit v4 on v3

--- a/solution.py
+++ b/solution.py
@@ -154,7 +154,7 @@
 
 
 def gather_back_kernel(
-    own, weight, upper, pieces, out, up_grad, out_pieces, send_sems, recv_sems, local_sem, *rings
+    own, weight, upper, pieces, out, up_grad, wide_sum, send_sems, recv_sems, local_sem, *rings
 ):
     def use(q):
         slope = gelu_pair(upper[row_block(q), :])[1]
@@ -163,7 +163,11 @@
     stages = []
 
     def begin():
-        stages.extend(layer_rings(pieces, out_pieces, *rings))
+        stages.extend(rings_first(pieces, wide_sum, *rings))
+
+    def end():
+        stages[1]()
+        stages[2]()
 
     gather_core(
         own,
@@ -175,9 +179,9 @@
         (
             list(grid_place()[2]),
             begin,
+            nothing,
             lambda: stages[0](),
-            lambda: stages[1](),
-            lambda: stages[2](),
+            end,
         ),
     )
 
@@ -285,13 +289,17 @@
     beside[4]()
 
 
-def product_scatter_kernel(product, spreads, left, right, *refs):
+def product_scatter_kernel(product, task, left, right, *refs):
     c, z, x = place()
     beside = ALONE
-    if spreads:
-        summed, out, got, other, mine, *refs = refs
-        refs, spread_refs = refs[:10], refs[10:]
-        beside = spread_beside(1, summed, got, spread_refs)
+    if task == "home":
+        wide_sum, out, own, other, mine, *refs = refs
+        refs, summed, more = refs[:10], refs[10], refs[11:]
+        beside = home_beside(1, wide_sum, summed, own, more[:5], more[5:])
+    elif task == "spread":
+        own, out, got, other, mine, *refs = refs
+        refs, more = refs[:10], refs[10:]
+        beside = spread_beside(1, own, got, more)
     else:
         out, other, mine, *refs = refs
 
@@ -324,26 +332,33 @@
     ]
 
 
-def product_scatter(product, collective_id, left, right, summed=None):
-    spreads = summed is not None
+def product_scatter(product, collective_id, left, right, extra=None):
     out_shape = (jax.ShapeDtypeStruct((128, D), F32),)
     operands = (left, right)
-    if spreads:
-        out_shape += (jax.ShapeDtypeStruct((8, GOT_ROWS, 128), BF),)
-        operands += (summed,)
+    task, scratch = "", []
+    if extra is not None:
+        operands += (extra,)
+        if extra.shape == WIDE:
+            task = "home"
+            out_shape += (jax.ShapeDtypeStruct((GOT_ROWS, 128), BF),)
+            scratch = [pltpu.VMEM((ROWS, 128), BF)] + second_scratch() + home_scratch()
+        else:
+            task = "spread"
+            out_shape += (jax.ShapeDtypeStruct((8, GOT_ROWS, 128), BF),)
+            scratch = spread_scratch()
     out = pl.pallas_call(
-        functools.partial(product_scatter_kernel, product, spreads),
+        functools.partial(product_scatter_kernel, product, task),
         out_shape=out_shape,
         in_specs=[VMEM] * len(operands),
         out_specs=(VMEM,) * len(out_shape),
         scratch_shapes=[pltpu.VMEM((4, 128, D), BF), pltpu.VMEM((4, 128, D), F32)]
         + scatter_scratch(128, D, 64)
-        + (spread_scratch() if spreads else []),
+        + scratch,
         compiler_params=pltpu.CompilerParams(
             collective_id=collective_id, has_side_effects=True, vmem_limit_bytes=LIMIT
         ),
     )(*operands)
-    return out if spreads else out[0]
+    return out[0] if extra is None else out
 
 
 TEAM_STEPS = tuple((dc, dx) for dc in range(2) for dx in range(4) if dc or dx)
@@ -679,18 +694,28 @@
 CUT = TOP // 32 * 16
 
 
-def rings_scratch():
+WIDE = (2, 4, TOP, 128)
+
+
+def first_scratch():
     dma = pltpu.SemaphoreType.DMA
     return [
-        pltpu.VMEM((2, 4, TOP, 128), BF),
         pltpu.VMEM((2, 2, 2, TOP, 128), BF),
         pltpu.VMEM((2, 2, 2, TOP, 128), BF),
         pltpu.VMEM((2, 2, 4, TOP, 128), BF),
+        dma((12,)),
+        dma((12,)),
+    ]
+
+
+def second_scratch():
+    dma = pltpu.SemaphoreType.DMA
+    return [
         pltpu.VMEM((2, 2, TOP - CUT, 128), BF),
         pltpu.VMEM((2, 2, TOP - CUT, 128), BF),
         pltpu.VMEM((2, 2, TOP, 128), BF),
-        dma((24,)),
-        dma((24,)),
+        dma((12,)),
+        dma((12,)),
     ]
 
 
@@ -715,9 +740,7 @@
     )
 
 
-def layer_rings(pieces, out, wide_sum, far, relay, got, far_s, relay_s, got_s, sends, recvs):
-    y, zf, (y_up, y_down, z_up, z_down) = grid_place()
-
+def starter(sends, recvs):
     def send(src, dst, index, target):
         copy = pltpu.make_async_remote_copy(
             src_ref=src,
@@ -730,25 +753,21 @@
         copy.start()
         return copy
 
+    return send
+
+
+def rings_first(pieces, wide_sum, far, relay, got, sends, recvs):
+    y, zf, (y_up, y_down, z_up, z_down) = grid_place()
+    send = starter(sends, recvs)
     low, high = pl.ds(0, 2), pl.ds(2, 2)
     top, bottom = pl.ds(0, TOP), pl.ds(TOP, TOP)
-    first, second = pl.ds(0, CUT), pl.ds(CUT, TOP - CUT)
-
-    def wide(k):
+
+    def buffers(k):
         return (
             [far.at[k, 0], far.at[k, 1]],
             [relay.at[k, 0], relay.at[k, 1]],
             [got.at[k, 0], got.at[k, 1]],
             wide_sum.at[k],
-        )
-
-    def small(k, result):
-        parts = pl.ds(0, CUT), pl.ds(0, TOP - CUT)
-        return (
-            [far_s.at[k, 0, parts[0]], far_s.at[k, 1, parts[1]]],
-            [relay_s.at[k, 0, parts[0]], relay_s.at[k, 1, parts[1]]],
-            [got_s.at[k, 0], got_s.at[k, 1]],
-            result,
         )
 
     y_mid, y_last = ring_reduce(
@@ -760,7 +779,7 @@
         y_down,
         low,
         high,
-        *wide(0),
+        *buffers(0),
     )
     z_mid, z_last = ring_reduce(
         send,
@@ -771,80 +790,66 @@
         z_down,
         low,
         high,
-        *wide(1),
-    )
-    later = []
-
-    def turn():
-        y_last()
-        later.append(
-            ring_reduce(
-                send,
-                12,
-                lambda i, part: wide_sum.at[0, i, part],
-                zf,
-                z_up,
-                z_down,
-                first,
-                second,
-                *small(0, out.at[top]),
-            )
-        )
-        z_last()
-        later.append(
-            ring_reduce(
-                send,
-                18,
-                lambda i, part: wide_sum.at[1, i, part],
-                y,
-                y_up,
-                y_down,
-                first,
-                second,
-                *small(1, out.at[bottom]),
-            )
-        )
+        *buffers(1),
+    )
 
     def middle():
         y_mid()
         z_mid()
 
-    def finish():
-        for mid, _ in later:
-            mid()
-        for _, last in later:
-            last()
-
-    return middle, turn, finish
+    return middle, y_last, z_last
+
+
+def rings_second(k, wide_sum, out, far, relay, got, sends, recvs):
+    y, zf, (y_up, y_down, z_up, z_down) = grid_place()
+    parts = pl.ds(0, CUT), pl.ds(0, TOP - CUT)
+    me, up, down = ((zf, z_up, z_down), (y, y_up, y_down))[k]
+    return ring_reduce(
+        starter(sends, recvs),
+        6 * k,
+        lambda i, part: wide_sum.at[k, i, part],
+        me,
+        up,
+        down,
+        pl.ds(0, CUT),
+        pl.ds(CUT, TOP - CUT),
+        [far.at[k, 0, parts[0]], far.at[k, 1, parts[1]]],
+        [relay.at[k, 0, parts[0]], relay.at[k, 1, parts[1]]],
+        [got.at[k, 0], got.at[k, 1]],
+        out.at[pl.ds(TOP * k, TOP)],
+    )
+
+
+def home_scratch():
+    dma = pltpu.SemaphoreType.DMA
+    return [dma((9,)), dma((10,)), dma((2,))]
 
 
 def spread_scratch():
     dma = pltpu.SemaphoreType.DMA
-    return [pltpu.VMEM((GOT_ROWS, 128), BF), dma((9,)), dma((10,)), dma((3,)), dma((13,)), dma((13,))]
-
-
-def spread_stages(layer, summed, out, own, home_send, home_recv, local_sems, sends, recvs):
+    return [dma, dma((13,)), dma((13,))]
+
+
+def remote_copy(src, dst, send_sem, recv_sem, target):
+    return pltpu.make_async_remote_copy(
+        src_ref=src,
+        dst_ref=dst,
+        send_sem=send_sem,
+        recv_sem=recv_sem,
+        device_id=target,
+        device_id_type=MESH,
+    )
+
+
+def home_stages(layer, summed, own, home_send, home_recv, local_sems):
     c, z, x = place()
-    r = lax.axis_index("replica")
-    y, zh = r // 2, r % 2
-    zf, (y_up, y_down, _, _) = grid_place()[1:]
-    across = {"section": c, "shard": z * 4 + x, "replica": y * 2 + 1 - zh}
     me = c * 4 + x
     mine = pl.ds(pl.multiple_of(me * 144, 16), 144)
     holds = c == layer
     other = c != layer
     stays = jnp.logical_and(holds, z == layer)
     leaves = jnp.logical_or(other, z != layer)
-
-    def copy(src, dst, send_sem, recv_sem, target):
-        return pltpu.make_async_remote_copy(
-            src_ref=src,
-            dst_ref=dst,
-            send_sem=send_sem,
-            recv_sem=recv_sem,
-            device_id=target,
-            device_id_type=MESH,
-        )
+    copy = remote_copy
 
     def split_part(tx):
         return summed.at[pl.ds(pl.multiple_of(tx * 144, 16), 144)]
@@ -915,41 +920,6 @@
         def _():
             to_owner(z).start()
 
-    here, there = y * 2 + zh, y * 2 + 1 - zh
-    front, back = pl.ds(0, GOT_ROWS // 2), pl.ds(GOT_ROWS // 2, GOT_ROWS // 2)
-
-    def step(index, source, place_at, target):
-        return copy(source, place_at, sends.at[index], recvs.at[index], target)
-
-    def over():
-        return step(0, own, out.at[here], across)
-
-    def kept():
-        return pltpu.make_async_copy(own, out.at[here], local_sems.at[2])
-
-    def ring(base, source, block):
-        def item(i):
-            part = (front, back, back, front)[i]
-            target = (y_up, y_down, y_up, y_down)[i]
-            return step(base + i, source.at[part], out.at[block, part], target)
-
-        return item
-
-    def relays(base, which):
-        below, above = ((y + 3) % 4) * 2 + which, ((y + 1) % 4) * 2 + which
-
-        def item(i):
-            place_at = (out.at[below, front], out.at[above, back])[i]
-            return step(base + 4 + i, place_at, place_at, (y_up, y_down)[i])
-
-        return item
-
-    def first_ring():
-        return ring(1, own, here)
-
-    def second_ring():
-        return ring(7, out.at[there], there)
-
     def arrived():
         @pl.when(holds)
         def _():
@@ -969,6 +939,70 @@
                 from_owner(0).wait_recv()
                 from_owner(1).wait_recv()
 
+    def end():
+        @pl.when(holds)
+        def _():
+            for dx in (1, 2, 3):
+                to_row(dx, 0).wait_send()
+
+        @pl.when(other)
+        def _():
+            for dx in range(4):
+                to_row(dx, 4).wait_send()
+
+        @pl.when(leaves)
+        def _():
+            to_owner(z).wait_send()
+
+    return home, arrived, end
+
+
+def spread_stages(layer, own, out, local_sem, sends, recvs):
+    c, z, x = place()
+    r = lax.axis_index("replica")
+    y, zh = r // 2, r % 2
+    y_up, y_down, _, _ = grid_place()[2]
+    across = {"section": c, "shard": z * 4 + x, "replica": y * 2 + 1 - zh}
+    holds = c == layer
+    copy = remote_copy
+    here, there = y * 2 + zh, y * 2 + 1 - zh
+    front, back = pl.ds(0, GOT_ROWS // 2), pl.ds(GOT_ROWS // 2, GOT_ROWS // 2)
+
+    def step(index, source, place_at, target):
+        return copy(source, place_at, sends.at[index], recvs.at[index], target)
+
+    def over():
+        return step(0, own, out.at[here], across)
+
+    def kept():
+        return pltpu.make_async_copy(own, out.at[here], local_sem)
+
+    def ring(base, source, block):
+        def item(i):
+            part = (front, back, back, front)[i]
+            target = (y_up, y_down, y_up, y_down)[i]
+            return step(base + i, source.at[part], out.at[block, part], target)
+
+        return item
+
+    def relays(base, which):
+        below, above = ((y + 3) % 4) * 2 + which, ((y + 1) % 4) * 2 + which
+
+        def item(i):
+            place_at = (out.at[below, front], out.at[above, back])[i]
+            return step(base + 4 + i, place_at, place_at, (y_up, y_down)[i])
+
+        return item
+
+    def first_ring():
+        return ring(1, own, here)
+
+    def second_ring():
+        return ring(7, out.at[there], there)
+
+    def start():
+        @pl.when(holds)
+        def _():
             kept().start()
             over().start()
             for i in range(4):
@@ -1007,48 +1041,66 @@
                 for i in range(2):
                     relayed(i).wait_send()
             kept().wait()
-            for dx in (1, 2, 3):
-                to_row(dx, 0).wait_send()
-
-        @pl.when(other)
-        def _():
-            for dx in range(4):
-                to_row(dx, 4).wait_send()
-
-        @pl.when(leaves)
-        def _():
-            to_owner(z).wait_send()
-
-    return home, arrived, pass_first, pass_second, end
-
-
-def spread_beside(layer, summed, out, refs):
+
+    return start, pass_first, pass_second, end
+
+
+def across_device():
     c, z, x = place()
     r = lax.axis_index("replica")
-    y_up, y_down, _, _ = grid_place()[2]
-    across = {"section": c, "shard": z * 4 + x, "replica": (r // 2) * 2 + 1 - r % 2}
+    return {"section": c, "shard": z * 4 + x, "replica": (r // 2) * 2 + 1 - r % 2}
+
+
+def home_beside(layer, wide_sum, summed, own, second_refs, home_refs):
+    c, z, x = place()
     friends = [at(c, z, (x + 2) % 4)] + [at(1 - c, z, (x + dx) % 4) for dx in (1, 2, 3)]
-    friends += [at(c, 1 - z, x), at(1 - c, 1 - z, x), y_up, y_down, across]
-    home, arrived, pass_first, pass_second, end = spread_stages(layer, summed, out, *refs)
+    friends += [at(1 - c, 1 - z, x)] + list(grid_place()[2])
+    home, arrived, end = home_stages(layer, summed, own, *home_refs)
+    rings = []
+
+    def begin():
+        for k in range(2):
+            rings.append(rings_second(k, wide_sum, summed, *second_refs))
+
+    def first():
+        for ring in rings:
+            ring[0]()
+
+    def second():
+        for ring in rings:
+            ring[1]()
+        home()
 
     def finish():
-        pass_second()
+        arrived()
         end()
 
-    return friends, home, arrived, pass_first, finish
-
-
-def reduce_kernel(pieces, out, summed, *refs):
+    return friends, begin, first, second, finish
+
+
+def spread_beside(layer, own, out, refs):
+    start, pass_first, pass_second, end = spread_stages(layer, own, out, *refs)
+    friends = list(grid_place()[2][:2]) + [across_device()]
+    return friends, start, pass_first, pass_second, end
+
+
+def reduce_kernel(pieces, out, wide_sum, summed, own, *refs):
     c, z, x = place()
-    r = lax.axis_index("replica")
-    across = {"section": c, "shard": z * 4 + x, "replica": (r // 2) * 2 + 1 - r % 2}
-    greet(list(grid_place()[2]) + [across, at(1 - c, 1 - z, x)] + team_mates())
-    spread_refs, ring_refs = refs[:6], refs[6:]
-    middle, turn, finish = layer_rings(pieces, summed, *ring_refs)
+    greet(list(grid_place()[2]) + [across_device(), at(1 - c, 1 - z, x)] + team_mates())
+    first_refs, second_refs, home_refs, spread_refs = refs[:5], refs[5:10], refs[10:13], refs[13:]
+    middle, y_last, z_last = rings_first(pieces, wide_sum, *first_refs)
     middle()
-    turn()
-    finish()
-    for stage in spread_stages(0, summed, out, *spread_refs):
+    y_last()
+    rings = [rings_second(0, wide_sum, summed, *second_refs)]
+    z_last()
+    rings.append(rings_second(1, wide_sum, summed, *second_refs))
+    for ring in rings:
+        ring[0]()
+    for ring in rings:
+        ring[1]()
+    for stage in home_stages(0, summed, own, *home_refs):
+        stage()
+    for stage in spread_stages(0, own, out, *spread_refs):
         stage()
 
 
@@ -1058,7 +1110,15 @@
         out_shape=jax.ShapeDtypeStruct((8, GOT_ROWS, 128), BF),
         in_specs=[VMEM],
         out_specs=VMEM,
-        scratch_shapes=[pltpu.VMEM((ROWS, 128), BF)] + spread_scratch() + rings_scratch(),
+        scratch_shapes=[
+            pltpu.VMEM(WIDE, BF),
+            pltpu.VMEM((ROWS, 128), BF),
+            pltpu.VMEM((GOT_ROWS, 128), BF),
+        ]
+        + first_scratch()
+        + second_scratch()
+        + home_scratch()
+        + spread_scratch(),
         compiler_params=pltpu.CompilerParams(
             collective_id=4, has_side_effects=True, vmem_limit_bytes=LIMIT
         ),
@@ -1584,21 +1644,21 @@
 def layer_backward(grad_out, grad_low_all, w, kept, q, pieces):
     grad_low = grad_out.astype(BF)
     if grad_low_all is None:
-        grad_low_all, up_grad, summed = team_gather(
+        grad_low_all, up_grad, wide_sum = team_gather(
             gather_back_kernel,
             8,
             grad_low,
             w["down"],
             (kept["upper"], pieces),
-            (jax.ShapeDtypeStruct((1024, 544), BF), jax.ShapeDtypeStruct((ROWS, 128), BF)),
-            rings_scratch(),
+            (jax.ShapeDtypeStruct((1024, 544), BF), jax.ShapeDtypeStruct(WIDE, BF)),
+            first_scratch(),
         )
         grad_low_all = grad_low_all.reshape(1024, D)
-        grad_second, got = product_scatter(dot_nt, 11, up_grad, w["up"], summed)
+        grad_second, own = product_scatter(dot_nt, 11, up_grad, w["up"], wide_sum)
     else:
         slope = gelu_pair(kept["upper"])[1]
         up_grad = (dot_nt(grad_low_all, w["down"]) * slope).astype(BF)
-        grad_second, got = product_scatter(dot_nt, 9, up_grad, w["up"]), None
+        grad_second, own = product_scatter(dot_nt, 9, up_grad, w["up"]), None
     grad_in, gain_two, bias_two = norm_backward(
         grad_second, kept["unit_two"], kept["inverse_two"], w["gain_two"]
     )
@@ -1609,7 +1669,10 @@
         [attended_grad[:, :1024], jnp.zeros((128, 64), BF), attended_grad[:, 1024:]], axis=1
     )
     qkv_grad, last_grad = attend_back(kept["projected"], kept["last_query"], attended_grad)
-    grad_normed = product_scatter(dot_nt, 10, qkv_grad, w["qkv"])
+    if own is None:
+        grad_normed, got = product_scatter(dot_nt, 10, qkv_grad, w["qkv"]), None
+    else:
+        grad_normed, got = product_scatter(dot_nt, 12, qkv_grad, w["qkv"], own)
     grad_normed = grad_normed + dot_nt(last_grad, w["last_query"])
     grad_in, gain_one, bias_one = norm_backward(
         grad_normed, kept["unit_one"], kept["inverse_one"], w["gain_one"]
@@ -1740,10 +1803,10 @@
     first_blocks, late, all_common, hidden, top_grad = spread_weights(
         late, common, inputs[:, 0], cotangent[:, 0]
     )
+    own_out = lax.all_gather(w_out[0], "shard", axis=0, tiled=True)
     teams = [[a * 8 + b * 4 + d for a in range(2) for d in range(4)] for b in range(2)]
     top_grad_all = lax.all_gather(top_grad, BOTH, axis_index_groups=teams, axis=0, tiled=True)
     second_blocks = lax.all_gather(late, "replica", axis=0)
-    own_out = lax.all_gather(w_out[0], "shard", axis=0, tiled=True)
     partner_out = lax.ppermute(own_out, "section", [(0, 1), (1, 0)])
     all_out = (
         jnp.where(c == 0, own_out, partner_out),

time: 613 us -> 606 us (0.989)
  Pallas kernels: 487 us -> 479 us
    pallas_call x2, Pallas kernels: 42.6 us -> 34 us  [attend_back(): pl.pallas_call(attend_back_kernel, out_shape=(jax.ShapeDtypeStruct((1024,...]
  transfers between devices with their start and end apart: 6 -> 6, of which waited for: 1 -> 1; matrix products, arithmetic and copies ran while one was open for 9% -> 9% of each run, Pallas kernels for 30% -> 31%
where the time goes in v4:
time: 606 us; the launch traced here: 595 us
  Pallas kernels  479 us (79%)
  local copies, waits for them, and re-layouts  50.7 us (8%)
  other arithmetic  26.4 us (4%)
  matrix products  20.3 us (3%)
  between operations  15.2 us (3%)
    pallas_call x6, Pallas kernels, product_scatter(): pl.pallas_call(functools.partial(product_scatter_kernel, product, task),...  114 us
    pallas_call x5, Pallas kernels, team_gather(): pl.pallas_call(kernel, out_shape=(jax.ShapeDtypeStruct((8, rows, columns)...  114 us
    pallas_call x1, Pallas kernels, spread_weights(): pl.pallas_call(weights_kernel, out_shape=(jax.ShapeDtypeStruct((4, 4, 4,...  63.2 us
    pallas_call x1, Pallas kernels, reduce_grads(): pl.pallas_call(reduce_kernel, out_shape=jax.ShapeDtypeStruct((8, GOT_ROWS...  60.1 us
    pallas_call x2, Pallas kernels, shared_scatter(): pl.pallas_call(shared_kernel, out_shape=(jax.ShapeDtypeStruct((144, 1280)...  48.8 us
    pallas_call x2, Pallas kernels, attend_back(): pl.pallas_call(attend_back_kernel, out_shape=(jax.ShapeDtypeStruct((1024,...  34 us
    pallas_call x2, Pallas kernels, grad_pieces(): pl.pallas_call(pieces_kernel, out_shape=jax.ShapeDtypeStruct((4, 4, ROWS,...  22.1 us
    pallas_call x2, Pallas kernels, attend(): pl.pallas_call(attend_kernel, out_shape=jax.ShapeDtypeStruct((128, 1152),...  17.2 us
  transfers between devices with their start and end apart: 6, of which 1 were waited for; matrix products, arithmetic and copies ran while one was open for 9% of the time, Pallas kernels for 31%

profile of v4, /device:TPU:16, one launch (start us, length us, event | category | flops | bytes accessed | tf_op | source)
XLA Modules:
  0.0 595.1 jit_solution(12906004732001534275)
XLA Ops:
  8.0 3.5 reshape_squeeze.15
  18.3 63.2 %shard_map.245 = (bf16[4,4,4,144,128]{4,3,2,1,0:T(8,128)(2,1)}, bf16[8,144,128]{2,1,0:T(8,128)(2,1)}, bf16[2,8,144,256]{3,2,1,0:T(8,128)(2,1)}, bf16[128,1088]{1,0:T(8,128)(2,1)}, bf16[128,1088]{1,0:T(8,128)(2,1)}) custom-call(bf16[8,144,128]{2,1,0:T(8,128)(2,1)} %pad_dynamic-slice_fusion.late, bf16[144,256]{1,0:T(8,128)(2,1)} %pad_maximum_fusion.4.common, ...), custom_call_target="tpu_custom_call" | custom-call | tf_op jit(solution)/shard_map/pallas_call | solution.py:618
  81.6 1.9 collective-permute-start.1
  83.5 1.4 slice_bitcast_fusion.3
  84.9 2.1 fusion.60
  88.9 2.4 copy.106
  91.4 1.5 slice.296
  92.9 2.8 reshape.246
  100.7 18.1 %shard_map.246 = (bf16[8,128,1088]{2,1,0:T(8,128)(2,1)}, bf16[1024,512]{1,0:T(8,128)(2,1)}) custom-call(bf16[128,1088]{1,0:T(8,128)(2,1)} %fusion.33.own.refs_4_, bf16[1088,512]{1,0:T(8,128)(2,1)} %pad_maximum_fusion.weight.right, f32[1,512]{1,0:T(1,128)} %bitcast.156), custom_call_target="tpu_custom_call" | custom-call | tf_op jit(solution)/shard_map/pallas_call | solution.py:191
  118.9 1.8 fusion.9.last_query
  120.7 8.6 %shard_map.247.refs_0_ = bf16[128,1152]{1,0:T(8,128)(2,1)} custom-call(bf16[1024,512]{1,0:T(8,128)(2,1)} %get-tuple-element.52.projected, bf16[128,128]{1,0:T(8,128)(2,1)} %fusion.9.last_query), custom_call_target="tpu_custom_call" | custom-call | tf_op jit(solution)/shard_map/pallas_call | solution.py:1471
  134.5 3.0 broadcast_select_fusion.3
  137.7 3.5 copy.105
  146.5 29.5 %shard_map.248 = (bf16[8,128,1088]{2,1,0:T(8,128)(2,1)}, f32[1024,544]{1,0:T(8,128)}, bf16[1024,544]{1,0:T(8,128)(2,1)}) custom-call(bf16[128,1088]{1,0:T(8,128)(2,1)} %add_convert_fusion.3.own, bf16[1088,544]{1,0:T(8,128)(2,1)} %slice.306.weight.right, f32[1,544]{1,0:T(1,128)} %reshape.250.bias), custom_call_target="tpu_custom_call" | custom-call | tf_op jit(solution)/shard_map/pallas_call | solution.py:191
  175.9 18.0 %shard_map.249 = f32[128,1088]{1,0:T(8,128)} custom-call(bf16[1024,544]{1,0:T(8,128)(2,1)} %get-tuple-element.53.left.activated, bf16[544,1088]{1,0:T(8,128)(2,1)} %get-tuple-element.165.right.weight), custom_call_target="tpu_custom_call" | custom-call | tf_op jit(solution)/shard_map/pallas_call | solution.py:349
  194.0 1.3 convert_reduce_fusion.4
  196.5 17.8 %shard_map.250 = (bf16[8,128,1088]{2,1,0:T(8,128)(2,1)}, bf16[1024,512]{1,0:T(8,128)(2,1)}) custom-call(bf16[128,1088]{1,0:T(8,128)(2,1)} %fusion.24.own.refs_4_, bf16[1088,512]{1,0:T(8,128)(2,1)} %pad_maximum_fusion.1.weight.right, f32[1,512]{1,0:T(1,128)} %bitcast.155), custom_call_target="tpu_custom_call" | custom-call | tf_op jit(solution)/shard_map/pallas_call | solution.py:191
  214.3 1.8 fusion.10.last_query
  216.1 8.6 %shard_map.251.refs_0_ = bf16[128,1152]{1,0:T(8,128)(2,1)} custom-call(bf16[1024,512]{1,0:T(8,128)(2,1)} %get-tuple-element.55.projected, bf16[128,128]{1,0:T(8,128)(2,1)} %fusion.10.last_query), custom_call_target="tpu_custom_call" | custom-call | tf_op jit(solution)/shard_map/pallas_call | solution.py:1471
  226.5 2.6 fusion.68
  230.3 19.1 %shard_map.252 = (bf16[8,128,1088]{2,1,0:T(8,128)(2,1)}, f32[1024,544]{1,0:T(8,128)}, bf16[1024,544]{1,0:T(8,128)(2,1)}) custom-call(bf16[128,1088]{1,0:T(8,128)(2,1)} %add_convert_fusion.1.own, bf16[1088,544]{1,0:T(8,128)(2,1)} %slice.323.weight.right, f32[1,544]{1,0:T(1,128)} %reshape.257.bias), custom_call_target="tpu_custom_call" | custom-call | tf_op jit(solution)/shard_map/pallas_call | solution.py:191
  249.4 6.6 %convert_reduce_fusion.1 = (f32[544]{0:T(1024)S(1)}, bf16[1024,544]{1,0:T(8,128)(2,1)}) fusion(f32[1024,544]{1,0:T(8,128)} %get-tuple-element.57, bf16[1024,1088]{1,0:T(8,128)(2,1)} %all-gather.6.cloned.1.call-done.low_all, bf16[544,1088]{1,0:T(8,128)(2,1)S(1)} %get-tuple-element.164.right), kind=kOutput, calls=%fused_computation.10 | convolution fusion | flops 1223851520 | bytes 6756480 | tf_op jit(solution)/shard_map/dot_general | solution.py:1366
  256.0 19.6 %shard_map.253 = f32[128,1088]{1,0:T(8,128)} custom-call(bf16[1024,544]{1,0:T(8,128)(2,1)} %get-tuple-element.198.left.up_grad, bf16[1088,544]{1,0:T(8,128)(2,1)} %slice.323.weight.right), custom_call_target="tpu_custom_call" | custom-call | tf_op jit(solution)/shard_map/pallas_call | solution.py:349
  275.6 1.4 multiply_reduce_fusion.2
  277.1 18.1 %shard_map.256 = f32[128,1088]{1,0:T(8,128)} custom-call(bf16[1024,544]{1,0:T(8,128)(2,1)} %get-tuple-element.61.left.activated, bf16[544,1088]{1,0:T(8,128)(2,1)} %copy-done.3), custom_call_target="tpu_custom_call" | custom-call | tf_op jit(solution)/shard_map/pallas_call | solution.py:349
  295.2 1.8 convert_reduce_fusion.9
  297.7 2.6 convolution_convert_fusion.1
  301.2 16.0 %shard_map.254 = (bf16[1024,512]{1,0:T(8,128)(2,1)}, bf16[128,128]{1,0:T(8,128)(2,1)}) custom-call(bf16[1024,512]{1,0:T(8,128)(2,1)} %get-tuple-element.55.projected, bf16[128,128]{1,0:T(8,128)(2,1)} %fusion.10.last_query, bf16[128,1152]{1,0:T(8,128)(2,1)} %concatenate.72.rows), custom_call_target="tpu_custom_call" | custom-call | tf_op jit(solution)/shard_map/pallas_call | solution.py:1552
  317.2 1.4 convert_reduce_fusion.3
  318.6 17.9 %shard_map.255 = f32[128,1088]{1,0:T(8,128)} custom-call(bf16[1024,512]{1,0:T(8,128)(2,1)} %get-tuple-element.59.left.refs_3_.qkv_grad, bf16[1088,512]{1,0:T(8,128)(2,1)} %pad_maximum_fusion.1.weight.right), custom_call_target="tpu_custom_call" | custom-call | tf_op jit(solution)/shard_map/pallas_call | solution.py:349
  337.8 1.5 fusion.26
  343.4 22.9 %shard_map.257 = (f32[144,1280]{1,0:T(8,128)}, bf16[2,128,1088]{2,1,0:T(8,128)(2,1)}) custom-call(bf16[128,1152]{1,0:T(8,128)(2,1)} %shard_map.251.refs_0_, bf16[128,1152]{1,0:T(8,128)(2,1)} %pad.33.refs_1_, bf16[1024,1088]{1,0:T(8,128)(2,1)} %bitcast.118, bf16[1024,512]{1,0:T(8,128)(2,1)} %get-tuple-element.59.left.refs_3_.qkv_grad, ...), custom_call_target="tpu_custom_call" | custom-call | tf_op jit(solution)/shard_map/pallas_call | solution.py:1221
  366.4 11.1 %shard_map.258.pieces = bf16[4,4,992,128]{3,2,1,0:T(8,128)(2,1)} custom-call(bf16[1024,1088]{1,0:T(8,128)(2,1)} %bitcast.119, bf16[1024,512]{1,0:T(8,128)(2,1)} %get-tuple-element.59.left.refs_3_.qkv_grad, bf16[1024,1088]{1,0:T(8,128)(2,1)} %bitcast.133, bf16[1024,544]{1,0:T(8,128)(2,1)} %get-tuple-element.198.left.up_grad, ...), custom_call_target="tpu_custom_call" | custom-call | tf_op jit(solution)/shard_map/pallas_call | solution.py:1287
  377.5 29.1 %shard_map.259 = (bf16[8,128,1088]{2,1,0:T(8,128)(2,1)}, bf16[1024,544]{1,0:T(8,128)(2,1)}, bf16[2,4,496,128]{3,2,1,0:T(8,128)(2,1)}) custom-call(bf16[128,1088]{1,0:T(8,128)(2,1)} %get-tuple-element.155.own, bf16[544,1088]{1,0:T(8,128)(2,1)} %get-tuple-element.165.right.weight, f32[1024,544]{1,0:T(8,128)} %get-tuple-element.63.upper, ...), custom_call_target="tpu_custom_call" | custom-call | tf_op jit(solution)/shard_map/pallas_call | solution.py:191
  406.6 20.0 %shard_map.260 = (f32[128,1088]{1,0:T(8,128)}, bf16[1984,128]{1,0:T(8,128)(2,1)}) custom-call(bf16[1024,544]{1,0:T(8,128)(2,1)} %get-tuple-element.66.left.up_grad, bf16[1088,544]{1,0:T(8,128)(2,1)} %slice.306.weight.right, bf16[2,4,496,128]{3,2,1,0:T(8,128)(2,1)} %get-tuple-element.67.refs_0_), custom_call_target="tpu_custom_call" | custom-call | tf_op jit(solution)/shard_map/pallas_call | solution.py:349
  426.6 1.5 multiply_reduce_fusion
  428.1 1.4 convert_reduce_fusion.8
  432.6 18.1 %shard_map.261 = (bf16[1024,512]{1,0:T(8,128)(2,1)}, bf16[128,128]{1,0:T(8,128)(2,1)}) custom-call(bf16[1024,512]{1,0:T(8,128)(2,1)} %get-tuple-element.52.projected, bf16[128,128]{1,0:T(8,128)(2,1)} %fusion.9.last_query, bf16[128,1152]{1,0:T(8,128)(2,1)} %concatenate.76.rows), custom_call_target="tpu_custom_call" | custom-call | tf_op jit(solution)/shard_map/pallas_call | solution.py:1552
  451.5 1.5 concatenate.77.refs_5_
  453.0 1.4 convert_reduce_fusion.2
  454.9 20.6 %shard_map.262 = (f32[128,1088]{1,0:T(8,128)}, bf16[8,1984,128]{2,1,0:T(8,128)(2,1)}) custom-call(bf16[1024,512]{1,0:T(8,128)(2,1)} %get-tuple-element.70.left.refs_3_.qkv_grad, bf16[1088,512]{1,0:T(8,128)(2,1)} %pad_maximum_fusion.weight.right, bf16[1984,128]{1,0:T(8,128)(2,1)} %get-tuple-element.72.refs_0_), custom_call_target="tpu_custom_call" | custom-call | tf_op jit(solution)/shard_map/pallas_call | solution.py:349
  475.5 1.5 fusion.35
  480.0 25.8 %shard_map.263 = (f32[144,1280]{1,0:T(8,128)}, bf16[2,128,1088]{2,1,0:T(8,128)(2,1)}) custom-call(bf16[128,1152]{1,0:T(8,128)(2,1)} %shard_map.247.refs_0_, bf16[128,1152]{1,0:T(8,128)(2,1)} %pad.35.refs_1_, bf16[1024,1088]{1,0:T(8,128)(2,1)} %bitcast.116, bf16[1024,512]{1,0:T(8,128)(2,1)} %get-tuple-element.70.left.refs_3_.qkv_grad, ...), custom_call_target="tpu_custom_call" | custom-call | tf_op jit(solution)/shard_map/pallas_call | solution.py:1221
  505.8 11.0 %shard_map.264.pieces = bf16[4,4,992,128]{3,2,1,0:T(8,128)(2,1)} custom-call(bf16[1024,1088]{1,0:T(8,128)(2,1)} %bitcast.117, bf16[1024,512]{1,0:T(8,128)(2,1)} %get-tuple-element.70.left.refs_3_.qkv_grad, bf16[1024,1088]{1,0:T(8,128)(2,1)} %bitcast.131, bf16[1024,544]{1,0:T(8,128)(2,1)} %get-tuple-element.66.left.up_grad, ...), custom_call_target="tpu_custom_call" | custom-call | tf_op jit(solution)/shard_map/pallas_call | solution.py:1287
  516.9 60.1 %shard_map.265.first_got = bf16[8,1984,128]{2,1,0:T(8,128)(2,1)} custom-call(bf16[4,4,992,128]{3,2,1,0:T(8,128)(2,1)} %shard_map.264.pieces), custom_call_target="tpu_custom_call" | custom-call | tf_op jit(solution)/shard_map/pallas_call | solution.py:1108
  577.0 5.7 shard_map.266
  584.3 1.4 copy.80
  585.8 1.4 copy.81
  (260 shorter events, 46.2 us)
Async XLA Ops:
  7.2 92.0 %all-gather.8.cloned.1.call-start = ((), (), s32[]{:S(2)}) async-start(), calls=%async_computation.1 | async-start | bytes 2820096 | tf_op jit(solution)/shard_map/all_gather | solution.py:1806
  7.9 129.7 %all-gather.10.cloned.1.call-start = ((), (), s32[]{:S(2)}) async-start(), calls=%async_computation.2 | async-start | bytes 2654208 | tf_op jit(solution)/shard_map/all_gather | solution.py:1809
  11.4 1.2 copy-start.13
  11.5 1.4 copy-start.31
  11.5 1.4 copy-start.28
  11.5 1.4 copy-start.32
  11.5 1.5 copy-start.33
  11.5 1.5 copy-start.34
  11.5 1.5 copy-start.35
  11.5 1.5 copy-start.36
  11.5 1.5 copy-start.37
  11.7 1.5 copy-start.16
  11.7 2.6 copy-start.17
  81.4 6.6 %copy-start.5 = (bf16[128,1088]{1,0:T(8,128)(2,1)S(1)}, bf16[128,1088]{1,0:T(8,128)(2,1)}, u32[]{:S(2)}) copy-start(bf16[128,1088]{1,0:T(8,128)(2,1)} %get-tuple-element.49) | copy-start | bytes 835588
  81.5 7.5 %copy-start.6 = (bf16[4,4,4,144,128]{4,3,2,1,0:T(8,128)(2,1)S(1)}, bf16[4,4,4,144,128]{4,3,2,1,0:T(8,128)(2,1)}, u32[]{:S(2)}) copy-start(bf16[4,4,4,144,128]{4,3,2,1,0:T(8,128)(2,1)} %get-tuple-element.51) | copy-start | bytes 7077892
  81.5 167.9 %all-gather.6.cloned.1.call-start = ((), (), s32[]{:S(2)}) async-start(), calls=%async_computation | async-start | bytes 2654208 | tf_op jit(solution)/shard_map/all_gather | solution.py:1808
  81.5 52.9 %collective-permute-start.2 = (bf16[544,1088]{1,0:T(8,128)(2,1)}, bf16[544,1088]{1,0:T(8,128)(2,1)}, u32[]{:S(2)}, u32[]{:S(2)}) collective-permute-start(bf16[544,1088]{1,0:T(8,128)(2,1)} %bitcast.138), channel_id=1, source_target_pairs={{0,32},{8,40},{16,48},{24,56},{32,96},{40,104},{48,112},{56,120},{... | collective-permute-start | bytes 3551240 | tf_op jit(solution)/shard_map/ppermute | solution.py:1822
  81.6 52.8 %collective-permute-start.1 = (bf16[544,1088]{1,0:T(8,128)(2,1)}, bf16[544,1088]{1,0:T(8,128)(2,1)}, u32[]{:S(2)}, u32[]{:S(2)}) collective-permute-start(bf16[544,1088]{1,0:T(8,128)(2,1)} %bitcast.139), channel_id=1, source_target_pairs={{32,64},{40,72},{48,80},{56,88},{64,32},{72,40},{80,48},{88,56},{3... | collective-permute-start | bytes 3551240 | tf_op jit(solution)/shard_map/ppermute | solution.py:1766
  87.0 31.8 %copy-start.7 = (bf16[1,8,136,256]{3,2,1,0:T(8,128)(2,1)}, bf16[1,8,136,256]{3,2,1,0:T(8,128)(2,1)S(1)}, u32[]{:S(2)}) copy-start(bf16[1,8,136,256]{3,2,1,0:T(8,128)(2,1)S(1)} %get-tuple-element.167) | copy-start | bytes 1671172
  87.0 4.3 copy-start.18
  92.9 4.1 slice-start.1
  95.7 2.5 copy-start.23
  95.7 2.5 copy-start.26
  95.7 2.5 copy-start.29
  98.2 32.0 %copy-start.1 = (bf16[1088,1024]{1,0:T(8,128)(2,1)S(1)}, bf16[1088,1024]{1,0:T(8,128)(2,1)}, u32[]{:S(2)}) copy-start(bf16[1088,1024]{1,0:T(8,128)(2,1)} %reshape.246) | copy-start | bytes 6684676
  99.2 45.2 %collective-permute-start = (bf16[1088,1088]{1,0:T(8,128)(2,1)}, bf16[1088,1088]{1,0:T(8,128)(2,1)}, u32[]{:S(2)}, u32[]{:S(2)}) collective-permute-start(bf16[1088,1088]{1,0:T(8,128)(2,1)} %bitcast.165), channel_id=1, source_target_pairs={{0,64},{64,0},{1,65},{65,1},{2,66},{66,2},{3,67},{67,3},{4,68},{68... | collective-permute-start | bytes 7102472 | tf_op jit(solution)/shard_map/ppermute | solution.py:1810
  120.7 10.8 %copy-start.19 = (f32[8,1632]{1,0:T(8,128)S(1)}, f32[8,1632]{1,0:T(8,128)}, u32[]{:S(2)}) copy-start(f32[8,1632]{1,0:T(8,128)} %copy-done.18) | copy-start | bytes 156676
  120.7 10.9 %copy-start.22 = (bf16[1,8,8,256]{3,2,1,0:T(8,128)(2,1)S(1)}, bf16[1,8,8,256]{3,2,1,0:T(8,128)(2,1)}, u32[]{:S(2)}) copy-start(bf16[1,8,8,256]{3,2,1,0:T(8,128)(2,1)} %get-tuple-element.168) | copy-start | bytes 98308
  129.3 3.4 copy-start.9
  137.5 111.9 %copy-start.3 = (bf16[544,1088]{1,0:T(8,128)(2,1)}, bf16[544,1088]{1,0:T(8,128)(2,1)S(1)}, u32[]{:S(2)}) copy-start(bf16[544,1088]{1,0:T(8,128)(2,1)S(1)} %get-tuple-element.164.right) | copy-start | bytes 3551236
  142.1 2.4 slice-start
  142.1 2.4 copy-start.27
  142.1 2.4 copy-start.38
  146.5 47.5 %copy-start.24 = (f32[1088]{0:T(1024)S(1)}, f32[1088]{0:T(1024)}, u32[]{:S(2)}) copy-start(f32[1088]{0:T(1024)} %get-tuple-element.148) | copy-start | bytes 13060
  194.0 20.3 %copy-start.10 = (bf16[1,8,136,256]{3,2,1,0:T(8,128)(2,1)S(1)}, bf16[1,8,136,256]{3,2,1,0:T(8,128)(2,1)}, u32[]{:S(2)}) copy-start(bf16[1,8,136,256]{3,2,1,0:T(8,128)(2,1)} %get-tuple-element.166) | copy-start | bytes 1671172
  275.6 19.5 %copy-start.2 = (f32[128,1088]{1,0:T(8,128)S(1)}, f32[128,1088]{1,0:T(8,128)}, u32[]{:S(2)}) copy-start(f32[128,1088]{1,0:T(8,128)} %shard_map.253) | copy-start | bytes 1671172
  275.6 19.5 %copy-start.12 = (bf16[128,1088]{1,0:T(8,128)(2,1)S(1)}, bf16[128,1088]{1,0:T(8,128)(2,1)}, u32[]{:S(2)}) copy-start(bf16[128,1088]{1,0:T(8,128)(2,1)} %get-tuple-element.56) | copy-start | bytes 835588
  295.1 2.6 copy-start.39
  301.2 36.6 %copy-start.11 = (bf16[1,8,136,256]{3,2,1,0:T(8,128)(2,1)S(1)}, bf16[1,8,136,256]{3,2,1,0:T(8,128)(2,1)}, u32[]{:S(2)}) copy-start(bf16[1,8,136,256]{3,2,1,0:T(8,128)(2,1)} %get-tuple-element.166) | copy-start | bytes 1671172
  317.2 19.4 %copy-start.21 = (bf16[128,128]{1,0:T(8,128)(2,1)S(1)}, bf16[128,128]{1,0:T(8,128)(2,1)}, u32[]{:S(2)}) copy-start(bf16[128,128]{1,0:T(8,128)(2,1)} %get-tuple-element.60) | copy-start | bytes 98308
  406.6 21.5 %copy-start.4 = (bf16[128,1088]{1,0:T(8,128)(2,1)S(1)}, bf16[128,1088]{1,0:T(8,128)(2,1)}, u32[]{:S(2)}) copy-start(bf16[128,1088]{1,0:T(8,128)(2,1)} %get-tuple-element.155.own) | copy-start | bytes 835588
  426.5 3.6 copy-start.40
  430.2 1.3 copy-start
  432.6 42.9 %copy-start.8 = (bf16[1,8,136,256]{3,2,1,0:T(8,128)(2,1)S(1)}, bf16[1,8,136,256]{3,2,1,0:T(8,128)(2,1)}, u32[]{:S(2)}) copy-start(bf16[1,8,136,256]{3,2,1,0:T(8,128)(2,1)} %copy-done.7) | copy-start | bytes 1671172
  432.6 42.9 %copy-start.30 = (f32[128]{0:T(128)S(1)}, f32[128]{0:T(128)}, u32[]{:S(2)}) copy-start(f32[128]{0:T(128)} %add_rsqrt_fusion.3) | copy-start | bytes 1540
  450.6 24.9 %copy-start.20 = (bf16[128,128]{1,0:T(8,128)(2,1)S(1)}, bf16[128,128]{1,0:T(8,128)(2,1)}, u32[]{:S(2)}) copy-start(bf16[128,128]{1,0:T(8,128)(2,1)} %get-tuple-element.71) | copy-start | bytes 98308
  577.0 7.3 %copy-start.14 = (bf16[2,128,1088]{2,1,0:T(8,128)(2,1)S(1)}, bf16[2,128,1088]{2,1,0:T(8,128)(2,1)}, u32[]{:S(2)}) copy-start(bf16[2,128,1088]{2,1,0:T(8,128)(2,1)} %get-tuple-element.62) | copy-start | bytes 1671172
  582.7 3.0 copy-start.15
  (1 other events, 1.1 us)
Sparse Core Ops, SparseCore 0:
  9.7 52.1 all-gather.7
  81.6 56.0 all-gather.9
  139.4 30.6 all-gather.5
